TPU v7x, 512 devices: a whole 4x4x16 slice. The times are simulated.
512 devices in a mesh: grp: 16 (over y, z_hi, core), sp: 32 (over z_lo, x).
Axes of the slice: x: 4, y: 4, z: 16 (z_hi: 2, z_lo: 8; z = z_hi * 8 + z_lo), core: 2. Of those that a mesh axis runs over, the one named last changes fastest.
Arguments:
- tokens: bfloat16 [12288, 3072], P(('grp', 'sp')), may hold values from -110 to 110
- mod_shift: float32 [3072], replicated, may hold values from -3 to 3
- mod_scale: float32 [3072], replicated, may hold values from 0.5 to 1.5
- qkv_weight: bfloat16 [3, 3072, 2048], P(None, None, 'grp'), may hold values from -0.109375 to 0.109375
- q_gain: float32 [128], replicated, may hold values from 1 to 2
- k_gain: float32 [128], replicated, may hold values from 1 to 2
- out_weight: bfloat16 [2048, 3072], P('grp'), may hold values from -0.5 to 0.5
- out_gate: float32 [3072], replicated, may hold values from 0.5 to 1.5
Outputs:
- mixed: bfloat16 [12288, 3072], P(('grp', 'sp'))
All inputs are finite; a program needn't handle non-finite values.
Results may differ from a plain program's by a relative error of at most 0.019.
Values may be sent and summed in bfloat16 or wider, within the bound.
No kernel may reach another device: no remote copies, remote signals or barrier semaphores. Data moves between devices by JAX's collectives and lax.ppermute only.
A program may use at most 64 MiB of HBM per device.

v0:
```python
import math

import jax
import jax.numpy as jnp
from jax import lax
from jax.sharding import PartitionSpec as P

HD = 128


epsilon = 1e-06


def from_behind(block, axis, distance):
    devices = range(lax.axis_size(axis))
    route = [((i - distance) % len(devices), i) for i in devices]
    return lax.ppermute(block, axis, route)


def layer_modulate(tokens, mod_shift, mod_scale):
    widened = tokens.astype(jnp.float32)
    center = widened - jnp.mean(widened, axis=-1, keepdims=True)
    spread = jnp.mean(center * center, axis=-1, keepdims=True)
    normed = center * lax.rsqrt(spread + epsilon)
    return (normed * mod_scale + mod_shift).astype(jnp.bfloat16)


def head_norm(projected, head_gain, heads_count):
    shaped = projected.reshape(projected.shape[0], heads_count, HD)
    meansq = jnp.mean(shaped * shaped, axis=-1, keepdims=True)
    normalized = (shaped * lax.rsqrt(meansq + epsilon) * head_gain).astype(jnp.bfloat16)
    return normalized.reshape(projected.shape)


def local(tokens, mod_shift, mod_scale, qkv_weight, q_gain, k_gain, out_weight, out_gate):
    heads_here = qkv_weight.shape[2] // HD
    head_cols = heads_here * HD
    scale_factor = 1.0 / math.sqrt(HD)
    modulated = layer_modulate(tokens, mod_shift, mod_scale)
    incoming = lax.all_gather(modulated, "grp", axis=0, tiled=True)
    project_queries = head_norm(
        jnp.dot(incoming, qkv_weight[0], preferred_element_type=jnp.float32), q_gain, heads_here
    )
    keys_part = head_norm(
        jnp.dot(incoming, qkv_weight[1], preferred_element_type=jnp.float32), k_gain, heads_here
    )
    values = jnp.dot(incoming, qkv_weight[2], preferred_element_type=jnp.float32).astype(
        jnp.bfloat16
    )
    projected = jnp.concatenate([project_queries, keys_part, values], axis=1)
    query_rows = projected.shape[0]
    queries = projected[:, :head_cols].reshape(query_rows, heads_here, HD)
    keyval = projected[:, head_cols:]

    def attend(running, incoming):
        piece_rows = incoming.shape[0]
        block_rows = math.gcd(piece_rows, 512)
        blocked = incoming.reshape(piece_rows // block_rows, block_rows, 2 * head_cols)

        def one_block(partial_value, key_block):
            numerator, totals = partial_value
            block_keys = key_block[:, :head_cols].reshape(block_rows, heads_here, HD)
            block_values = key_block[:, head_cols:].reshape(block_rows, heads_here, HD)
            scores = (
                jnp.einsum("qhd,khd->hqk", queries, block_keys, preferred_element_type=jnp.float32)
                * scale_factor
            )
            weights = jnp.exp(scores)
            totals = totals + jnp.sum(weights, axis=2).T
            numerator = numerator + jnp.einsum(
                "hqk,khd->qhd",
                weights.astype(jnp.bfloat16),
                block_values,
                preferred_element_type=jnp.float32,
            )
            return ((numerator, totals), None)

        result, unused = lax.scan(one_block, running, blocked)
        return result

    initial = (
        jnp.zeros((query_rows, heads_here, HD), jnp.float32),
        jnp.zeros((query_rows, heads_here), jnp.float32),
    )

    def cycle_turn(turn_index, partial_value):
        running_num, running_tot, current = partial_value
        current = from_behind(current, "sp", 1)
        numerator_new, totals_new = attend((running_num, running_tot), current)
        return (numerator_new, totals_new, current)

    first_num, first_tot = attend(initial, keyval)
    numerator, totals, unused = lax.fori_loop(
        0, lax.axis_size("sp") - 1, cycle_turn, (first_num, first_tot, keyval)
    )
    attended = (numerator / totals[:, :, None]).astype(jnp.bfloat16).reshape(query_rows, head_cols)
    partial_sum = jnp.dot(attended, out_weight, preferred_element_type=jnp.float32).astype(
        jnp.bfloat16
    )
    partial_sum = lax.optimization_barrier(partial_sum)
    summed = lax.psum_scatter(
        partial_sum.astype(jnp.float32).astype(jnp.bfloat16), "grp", scatter_dimension=0, tiled=True
    ).astype(jnp.float32)
    return (summed * out_gate).astype(jnp.bfloat16)


def solution(mesh):
    return jax.shard_map(
        local,
        mesh=mesh,
        in_specs=(
            P(("grp", "sp"), None),
            P(),
            P(),
            P(None, None, "grp"),
            P(),
            P(),
            P("grp", None),
            P(),
        ),
        out_specs=P(("grp", "sp"), None),
        check_vma=False,
    )
```

profile of v0, /device:TPU:1, one launch (start us, length us, event | category | flops | bytes accessed | tf_op | source)
XLA Modules:
  0.0 803.9 jit_solution(3171239654456654367)
XLA Ops:
  10.6 101.7 %all-gather.2.cloned.1.call-done = bf16[384,3072]{1,0:T(8,128)(2,1)} async-done(((bf16[24,3072]{1,0:T(8,128)(2,1)}), bf16[384,3072]{1,0:T(8,128)(2,1)}) %all-gather.2.cloned.1.call-update) | async-done | bytes 2359312 | tf_op jit(solution)/shard_map/all_gather | solution.py:40
  112.3 3.4 multiply_reduce_fusion.1
  115.8 2.0 multiply_reduce_fusion
  122.6 523.6 %while.40 = (s32[]{:T(128)}, f32[384,1,128]{0,2,1:T(8,128)S(1)}, f32[384,1]{0,1:T(1,128)S(1)}, bf16[384,256]{1,0:T(8,128)(2,1)S(1)}, bf16[384,1,128]{2,0,1:T(8,128)(2,1)S(1)}, /*index=5*/s32[]{:T(128)}, s32[]{:T(128)}, s32[]{:T(128)}) while((s32[]{:T(128)}, f32[384,1,128]{0,2,1:T(8,128)S(1)}, f32[384,1]{0,1:T(1,128)S(1)}, ...), condition=%wide.region_11.12_spmd, body=%wide.region_7.11_spmd.sunk | while | flops 25362432 | bytes 2070782 | solution.py:93
  122.6 3.1 collective-permute-start
  125.7 13.7 %collective-permute-done = bf16[384,256]{1,0:T(8,128)(2,1)S(1)} collective-permute-done((bf16[384,256]{1,0:T(8,128)(2,1)S(1)}, bf16[384,256]{1,0:T(8,128)(2,1)S(1)}, u32[]{:S(2)}, u32[]{:S(2)}) %collective-permute-start) | collective-permute-done | bytes 196640 | tf_op jit(solution)/shard_map/while/body/eval_jaxpr/ppermute | solution.py:17
  141.0 1.9 collective-permute-start
  142.9 14.0 %collective-permute-done = bf16[384,256]{1,0:T(8,128)(2,1)S(1)} collective-permute-done((bf16[384,256]{1,0:T(8,128)(2,1)S(1)}, bf16[384,256]{1,0:T(8,128)(2,1)S(1)}, u32[]{:S(2)}, u32[]{:S(2)}) %collective-permute-start) | collective-permute-done | bytes 196640 | tf_op jit(solution)/shard_map/while/body/eval_jaxpr/ppermute | solution.py:17
  158.4 1.9 collective-permute-start
  160.3 13.2 %collective-permute-done = bf16[384,256]{1,0:T(8,128)(2,1)S(1)} collective-permute-done((bf16[384,256]{1,0:T(8,128)(2,1)S(1)}, bf16[384,256]{1,0:T(8,128)(2,1)S(1)}, u32[]{:S(2)}, u32[]{:S(2)}) %collective-permute-start) | collective-permute-done | bytes 196640 | tf_op jit(solution)/shard_map/while/body/eval_jaxpr/ppermute | solution.py:17
  175.1 1.9 collective-permute-start
  177.0 13.2 %collective-permute-done = bf16[384,256]{1,0:T(8,128)(2,1)S(1)} collective-permute-done((bf16[384,256]{1,0:T(8,128)(2,1)S(1)}, bf16[384,256]{1,0:T(8,128)(2,1)S(1)}, u32[]{:S(2)}, u32[]{:S(2)}) %collective-permute-start) | collective-permute-done | bytes 196640 | tf_op jit(solution)/shard_map/while/body/eval_jaxpr/ppermute | solution.py:17
  191.7 1.9 collective-permute-start
  193.6 13.2 %collective-permute-done = bf16[384,256]{1,0:T(8,128)(2,1)S(1)} collective-permute-done((bf16[384,256]{1,0:T(8,128)(2,1)S(1)}, bf16[384,256]{1,0:T(8,128)(2,1)S(1)}, u32[]{:S(2)}, u32[]{:S(2)}) %collective-permute-start) | collective-permute-done | bytes 196640 | tf_op jit(solution)/shard_map/while/body/eval_jaxpr/ppermute | solution.py:17
  208.3 1.9 collective-permute-start
  210.3 13.2 %collective-permute-done = bf16[384,256]{1,0:T(8,128)(2,1)S(1)} collective-permute-done((bf16[384,256]{1,0:T(8,128)(2,1)S(1)}, bf16[384,256]{1,0:T(8,128)(2,1)S(1)}, u32[]{:S(2)}, u32[]{:S(2)}) %collective-permute-start) | collective-permute-done | bytes 196640 | tf_op jit(solution)/shard_map/while/body/eval_jaxpr/ppermute | solution.py:17
  225.0 1.9 collective-permute-start
  226.9 13.2 %collective-permute-done = bf16[384,256]{1,0:T(8,128)(2,1)S(1)} collective-permute-done((bf16[384,256]{1,0:T(8,128)(2,1)S(1)}, bf16[384,256]{1,0:T(8,128)(2,1)S(1)}, u32[]{:S(2)}, u32[]{:S(2)}) %collective-permute-start) | collective-permute-done | bytes 196640 | tf_op jit(solution)/shard_map/while/body/eval_jaxpr/ppermute | solution.py:17
  241.6 1.9 collective-permute-start
  243.6 13.2 %collective-permute-done = bf16[384,256]{1,0:T(8,128)(2,1)S(1)} collective-permute-done((bf16[384,256]{1,0:T(8,128)(2,1)S(1)}, bf16[384,256]{1,0:T(8,128)(2,1)S(1)}, u32[]{:S(2)}, u32[]{:S(2)}) %collective-permute-start) | collective-permute-done | bytes 196640 | tf_op jit(solution)/shard_map/while/body/eval_jaxpr/ppermute | solution.py:17
  258.3 1.9 collective-permute-start
  260.2 13.2 %collective-permute-done = bf16[384,256]{1,0:T(8,128)(2,1)S(1)} collective-permute-done((bf16[384,256]{1,0:T(8,128)(2,1)S(1)}, bf16[384,256]{1,0:T(8,128)(2,1)S(1)}, u32[]{:S(2)}, u32[]{:S(2)}) %collective-permute-start) | collective-permute-done | bytes 196640 | tf_op jit(solution)/shard_map/while/body/eval_jaxpr/ppermute | solution.py:17
  274.9 1.9 collective-permute-start
  276.8 13.2 %collective-permute-done = bf16[384,256]{1,0:T(8,128)(2,1)S(1)} collective-permute-done((bf16[384,256]{1,0:T(8,128)(2,1)S(1)}, bf16[384,256]{1,0:T(8,128)(2,1)S(1)}, u32[]{:S(2)}, u32[]{:S(2)}) %collective-permute-start) | collective-permute-done | bytes 196640 | tf_op jit(solution)/shard_map/while/body/eval_jaxpr/ppermute | solution.py:17
  291.5 1.9 collective-permute-start
  293.5 13.2 %collective-permute-done = bf16[384,256]{1,0:T(8,128)(2,1)S(1)} collective-permute-done((bf16[384,256]{1,0:T(8,128)(2,1)S(1)}, bf16[384,256]{1,0:T(8,128)(2,1)S(1)}, u32[]{:S(2)}, u32[]{:S(2)}) %collective-permute-start) | collective-permute-done | bytes 196640 | tf_op jit(solution)/shard_map/while/body/eval_jaxpr/ppermute | solution.py:17
  308.2 1.9 collective-permute-start
  310.1 13.2 %collective-permute-done = bf16[384,256]{1,0:T(8,128)(2,1)S(1)} collective-permute-done((bf16[384,256]{1,0:T(8,128)(2,1)S(1)}, bf16[384,256]{1,0:T(8,128)(2,1)S(1)}, u32[]{:S(2)}, u32[]{:S(2)}) %collective-permute-start) | collective-permute-done | bytes 196640 | tf_op jit(solution)/shard_map/while/body/eval_jaxpr/ppermute | solution.py:17
  324.8 1.9 collective-permute-start
  326.8 13.2 %collective-permute-done = bf16[384,256]{1,0:T(8,128)(2,1)S(1)} collective-permute-done((bf16[384,256]{1,0:T(8,128)(2,1)S(1)}, bf16[384,256]{1,0:T(8,128)(2,1)S(1)}, u32[]{:S(2)}, u32[]{:S(2)}) %collective-permute-start) | collective-permute-done | bytes 196640 | tf_op jit(solution)/shard_map/while/body/eval_jaxpr/ppermute | solution.py:17
  341.5 1.9 collective-permute-start
  343.4 13.2 %collective-permute-done = bf16[384,256]{1,0:T(8,128)(2,1)S(1)} collective-permute-done((bf16[384,256]{1,0:T(8,128)(2,1)S(1)}, bf16[384,256]{1,0:T(8,128)(2,1)S(1)}, u32[]{:S(2)}, u32[]{:S(2)}) %collective-permute-start) | collective-permute-done | bytes 196640 | tf_op jit(solution)/shard_map/while/body/eval_jaxpr/ppermute | solution.py:17
  358.1 1.9 collective-permute-start
  360.0 13.8 %collective-permute-done = bf16[384,256]{1,0:T(8,128)(2,1)S(1)} collective-permute-done((bf16[384,256]{1,0:T(8,128)(2,1)S(1)}, bf16[384,256]{1,0:T(8,128)(2,1)S(1)}, u32[]{:S(2)}, u32[]{:S(2)}) %collective-permute-start) | collective-permute-done | bytes 196640 | tf_op jit(solution)/shard_map/while/body/eval_jaxpr/ppermute | solution.py:17
  377.2 14.9 %collective-permute-done = bf16[384,256]{1,0:T(8,128)(2,1)S(1)} collective-permute-done((bf16[384,256]{1,0:T(8,128)(2,1)S(1)}, bf16[384,256]{1,0:T(8,128)(2,1)S(1)}, u32[]{:S(2)}, u32[]{:S(2)}) %collective-permute-start) | collective-permute-done | bytes 196640 | tf_op jit(solution)/shard_map/while/body/eval_jaxpr/ppermute | solution.py:17
  393.6 1.9 collective-permute-start
  395.5 14.9 %collective-permute-done = bf16[384,256]{1,0:T(8,128)(2,1)S(1)} collective-permute-done((bf16[384,256]{1,0:T(8,128)(2,1)S(1)}, bf16[384,256]{1,0:T(8,128)(2,1)S(1)}, u32[]{:S(2)}, u32[]{:S(2)}) %collective-permute-start) | collective-permute-done | bytes 196640 | tf_op jit(solution)/shard_map/while/body/eval_jaxpr/ppermute | solution.py:17
  411.9 1.9 collective-permute-start
  413.8 13.9 %collective-permute-done = bf16[384,256]{1,0:T(8,128)(2,1)S(1)} collective-permute-done((bf16[384,256]{1,0:T(8,128)(2,1)S(1)}, bf16[384,256]{1,0:T(8,128)(2,1)S(1)}, u32[]{:S(2)}, u32[]{:S(2)}) %collective-permute-start) | collective-permute-done | bytes 196640 | tf_op jit(solution)/shard_map/while/body/eval_jaxpr/ppermute | solution.py:17
  431.2 13.2 %collective-permute-done = bf16[384,256]{1,0:T(8,128)(2,1)S(1)} collective-permute-done((bf16[384,256]{1,0:T(8,128)(2,1)S(1)}, bf16[384,256]{1,0:T(8,128)(2,1)S(1)}, u32[]{:S(2)}, u32[]{:S(2)}) %collective-permute-start) | collective-permute-done | bytes 196640 | tf_op jit(solution)/shard_map/while/body/eval_jaxpr/ppermute | solution.py:17
  447.9 13.2 %collective-permute-done = bf16[384,256]{1,0:T(8,128)(2,1)S(1)} collective-permute-done((bf16[384,256]{1,0:T(8,128)(2,1)S(1)}, bf16[384,256]{1,0:T(8,128)(2,1)S(1)}, u32[]{:S(2)}, u32[]{:S(2)}) %collective-permute-start) | collective-permute-done | bytes 196640 | tf_op jit(solution)/shard_map/while/body/eval_jaxpr/ppermute | solution.py:17
  464.5 13.2 %collective-permute-done = bf16[384,256]{1,0:T(8,128)(2,1)S(1)} collective-permute-done((bf16[384,256]{1,0:T(8,128)(2,1)S(1)}, bf16[384,256]{1,0:T(8,128)(2,1)S(1)}, u32[]{:S(2)}, u32[]{:S(2)}) %collective-permute-start) | collective-permute-done | bytes 196640 | tf_op jit(solution)/shard_map/while/body/eval_jaxpr/ppermute | solution.py:17
  479.2 1.9 collective-permute-start
  481.1 13.2 %collective-permute-done = bf16[384,256]{1,0:T(8,128)(2,1)S(1)} collective-permute-done((bf16[384,256]{1,0:T(8,128)(2,1)S(1)}, bf16[384,256]{1,0:T(8,128)(2,1)S(1)}, u32[]{:S(2)}, u32[]{:S(2)}) %collective-permute-start) | collective-permute-done | bytes 196640 | tf_op jit(solution)/shard_map/while/body/eval_jaxpr/ppermute | solution.py:17
  495.9 1.9 collective-permute-start
  497.8 13.2 %collective-permute-done = bf16[384,256]{1,0:T(8,128)(2,1)S(1)} collective-permute-done((bf16[384,256]{1,0:T(8,128)(2,1)S(1)}, bf16[384,256]{1,0:T(8,128)(2,1)S(1)}, u32[]{:S(2)}, u32[]{:S(2)}) %collective-permute-start) | collective-permute-done | bytes 196640 | tf_op jit(solution)/shard_map/while/body/eval_jaxpr/ppermute | solution.py:17
  512.5 1.9 collective-permute-start
  514.4 13.2 %collective-permute-done = bf16[384,256]{1,0:T(8,128)(2,1)S(1)} collective-permute-done((bf16[384,256]{1,0:T(8,128)(2,1)S(1)}, bf16[384,256]{1,0:T(8,128)(2,1)S(1)}, u32[]{:S(2)}, u32[]{:S(2)}) %collective-permute-start) | collective-permute-done | bytes 196640 | tf_op jit(solution)/shard_map/while/body/eval_jaxpr/ppermute | solution.py:17
  529.1 1.9 collective-permute-start
  531.1 13.2 %collective-permute-done = bf16[384,256]{1,0:T(8,128)(2,1)S(1)} collective-permute-done((bf16[384,256]{1,0:T(8,128)(2,1)S(1)}, bf16[384,256]{1,0:T(8,128)(2,1)S(1)}, u32[]{:S(2)}, u32[]{:S(2)}) %collective-permute-start) | collective-permute-done | bytes 196640 | tf_op jit(solution)/shard_map/while/body/eval_jaxpr/ppermute | solution.py:17
  545.8 1.9 collective-permute-start
  547.7 13.2 %collective-permute-done = bf16[384,256]{1,0:T(8,128)(2,1)S(1)} collective-permute-done((bf16[384,256]{1,0:T(8,128)(2,1)S(1)}, bf16[384,256]{1,0:T(8,128)(2,1)S(1)}, u32[]{:S(2)}, u32[]{:S(2)}) %collective-permute-start) | collective-permute-done | bytes 196640 | tf_op jit(solution)/shard_map/while/body/eval_jaxpr/ppermute | solution.py:17
  562.4 1.9 collective-permute-start
  564.3 13.2 %collective-permute-done = bf16[384,256]{1,0:T(8,128)(2,1)S(1)} collective-permute-done((bf16[384,256]{1,0:T(8,128)(2,1)S(1)}, bf16[384,256]{1,0:T(8,128)(2,1)S(1)}, u32[]{:S(2)}, u32[]{:S(2)}) %collective-permute-start) | collective-permute-done | bytes 196640 | tf_op jit(solution)/shard_map/while/body/eval_jaxpr/ppermute | solution.py:17
  579.1 1.9 collective-permute-start
  581.0 13.2 %collective-permute-done = bf16[384,256]{1,0:T(8,128)(2,1)S(1)} collective-permute-done((bf16[384,256]{1,0:T(8,128)(2,1)S(1)}, bf16[384,256]{1,0:T(8,128)(2,1)S(1)}, u32[]{:S(2)}, u32[]{:S(2)}) %collective-permute-start) | collective-permute-done | bytes 196640 | tf_op jit(solution)/shard_map/while/body/eval_jaxpr/ppermute | solution.py:17
  595.7 1.9 collective-permute-start
  597.6 13.2 %collective-permute-done = bf16[384,256]{1,0:T(8,128)(2,1)S(1)} collective-permute-done((bf16[384,256]{1,0:T(8,128)(2,1)S(1)}, bf16[384,256]{1,0:T(8,128)(2,1)S(1)}, u32[]{:S(2)}, u32[]{:S(2)}) %collective-permute-start) | collective-permute-done | bytes 196640 | tf_op jit(solution)/shard_map/while/body/eval_jaxpr/ppermute | solution.py:17
  612.3 1.9 collective-permute-start
  614.3 13.2 %collective-permute-done = bf16[384,256]{1,0:T(8,128)(2,1)S(1)} collective-permute-done((bf16[384,256]{1,0:T(8,128)(2,1)S(1)}, bf16[384,256]{1,0:T(8,128)(2,1)S(1)}, u32[]{:S(2)}, u32[]{:S(2)}) %collective-permute-start) | collective-permute-done | bytes 196640 | tf_op jit(solution)/shard_map/while/body/eval_jaxpr/ppermute | solution.py:17
  629.0 1.9 collective-permute-start
  630.9 13.8 %collective-permute-done = bf16[384,256]{1,0:T(8,128)(2,1)S(1)} collective-permute-done((bf16[384,256]{1,0:T(8,128)(2,1)S(1)}, bf16[384,256]{1,0:T(8,128)(2,1)S(1)}, u32[]{:S(2)}, u32[]{:S(2)}) %collective-permute-start) | collective-permute-done | bytes 196640 | tf_op jit(solution)/shard_map/while/body/eval_jaxpr/ppermute | solution.py:17
  646.3 2.2 convolution_convert_fusion
  648.5 147.0 %reduce-scatter.2.cloned.1.call-done = bf16[24,3072]{1,0:T(8,128)(2,1)} async-done(((bf16[384,3072]{1,0:T(8,128)(2,1)}), bf16[24,3072]{1,0:T(8,128)(2,1)}) %reduce-scatter.2.cloned.1.call-update) | async-done | bytes 147472 | tf_op jit(solution)/shard_map/reduce_scatter | solution.py:101
  (482 shorter events, 108.2 us)
Async XLA Ops:
  6.5 639.7 %copy-start = (bf16[128,3072]{1,0:T(8,128)(2,1)S(1)}, bf16[128,3072]{1,0:T(8,128)(2,1)}, u32[]{:S(2)}) copy-start(bf16[128,3072]{1,0:T(8,128)(2,1)} %param.20) | copy-start | bytes 2359300
  6.5 105.8 %all-gather.2.cloned.1.call-start = ((), (), s32[]{:S(2)}) async-start(), calls=%async_computation.1 | async-start | bytes 2506752 | tf_op jit(solution)/shard_map/all_gather | solution.py:40
  10.5 784.9 %reduce-scatter.2.cloned.1.call-start = ((), (), s32[]{:S(2)}) async-start(), calls=%async_computation.2 | async-start | bytes 2506752 | tf_op jit(solution)/shard_map/reduce_scatter | solution.py:101
  112.3 3.5 copy-start.1
  115.8 2.0 copy-start.3
  115.8 2.2 copy-start.4
  122.6 16.8 %collective-permute-start = (bf16[384,256]{1,0:T(8,128)(2,1)S(1)}, bf16[384,256]{1,0:T(8,128)(2,1)S(1)}, u32[]{:S(2)}, u32[]{:S(2)}) collective-permute-start(bf16[384,256]{1,0:T(8,128)(2,1)S(1)} %get-tuple-element.339), channel_id=1, source_target_pairs={{31,0},{0,1},{1,2},{2,3},{3,4},{4,5},{5,6},{6,7},{7,8},{8,9},{9,10... | collective-permute-start | bytes 589832 | tf_op jit(solution)/shard_map/while/body/eval_jaxpr/ppermute | solution.py:17
  141.0 15.9 %collective-permute-start = (bf16[384,256]{1,0:T(8,128)(2,1)S(1)}, bf16[384,256]{1,0:T(8,128)(2,1)S(1)}, u32[]{:S(2)}, u32[]{:S(2)}) collective-permute-start(bf16[384,256]{1,0:T(8,128)(2,1)S(1)} %get-tuple-element.339), channel_id=1, source_target_pairs={{31,0},{0,1},{1,2},{2,3},{3,4},{4,5},{5,6},{6,7},{7,8},{8,9},{9,10... | collective-permute-start | bytes 589832 | tf_op jit(solution)/shard_map/while/body/eval_jaxpr/ppermute | solution.py:17
  158.4 15.1 %collective-permute-start = (bf16[384,256]{1,0:T(8,128)(2,1)S(1)}, bf16[384,256]{1,0:T(8,128)(2,1)S(1)}, u32[]{:S(2)}, u32[]{:S(2)}) collective-permute-start(bf16[384,256]{1,0:T(8,128)(2,1)S(1)} %get-tuple-element.339), channel_id=1, source_target_pairs={{31,0},{0,1},{1,2},{2,3},{3,4},{4,5},{5,6},{6,7},{7,8},{8,9},{9,10... | collective-permute-start | bytes 589832 | tf_op jit(solution)/shard_map/while/body/eval_jaxpr/ppermute | solution.py:17
  175.1 15.1 %collective-permute-start = (bf16[384,256]{1,0:T(8,128)(2,1)S(1)}, bf16[384,256]{1,0:T(8,128)(2,1)S(1)}, u32[]{:S(2)}, u32[]{:S(2)}) collective-permute-start(bf16[384,256]{1,0:T(8,128)(2,1)S(1)} %get-tuple-element.339), channel_id=1, source_target_pairs={{31,0},{0,1},{1,2},{2,3},{3,4},{4,5},{5,6},{6,7},{7,8},{8,9},{9,10... | collective-permute-start | bytes 589832 | tf_op jit(solution)/shard_map/while/body/eval_jaxpr/ppermute | solution.py:17
  191.7 15.1 %collective-permute-start = (bf16[384,256]{1,0:T(8,128)(2,1)S(1)}, bf16[384,256]{1,0:T(8,128)(2,1)S(1)}, u32[]{:S(2)}, u32[]{:S(2)}) collective-permute-start(bf16[384,256]{1,0:T(8,128)(2,1)S(1)} %get-tuple-element.339), channel_id=1, source_target_pairs={{31,0},{0,1},{1,2},{2,3},{3,4},{4,5},{5,6},{6,7},{7,8},{8,9},{9,10... | collective-permute-start | bytes 589832 | tf_op jit(solution)/shard_map/while/body/eval_jaxpr/ppermute | solution.py:17
  208.3 15.1 %collective-permute-start = (bf16[384,256]{1,0:T(8,128)(2,1)S(1)}, bf16[384,256]{1,0:T(8,128)(2,1)S(1)}, u32[]{:S(2)}, u32[]{:S(2)}) collective-permute-start(bf16[384,256]{1,0:T(8,128)(2,1)S(1)} %get-tuple-element.339), channel_id=1, source_target_pairs={{31,0},{0,1},{1,2},{2,3},{3,4},{4,5},{5,6},{6,7},{7,8},{8,9},{9,10... | collective-permute-start | bytes 589832 | tf_op jit(solution)/shard_map/while/body/eval_jaxpr/ppermute | solution.py:17
  225.0 15.1 %collective-permute-start = (bf16[384,256]{1,0:T(8,128)(2,1)S(1)}, bf16[384,256]{1,0:T(8,128)(2,1)S(1)}, u32[]{:S(2)}, u32[]{:S(2)}) collective-permute-start(bf16[384,256]{1,0:T(8,128)(2,1)S(1)} %get-tuple-element.339), channel_id=1, source_target_pairs={{31,0},{0,1},{1,2},{2,3},{3,4},{4,5},{5,6},{6,7},{7,8},{8,9},{9,10... | collective-permute-start | bytes 589832 | tf_op jit(solution)/shard_map/while/body/eval_jaxpr/ppermute | solution.py:17
  241.6 15.1 %collective-permute-start = (bf16[384,256]{1,0:T(8,128)(2,1)S(1)}, bf16[384,256]{1,0:T(8,128)(2,1)S(1)}, u32[]{:S(2)}, u32[]{:S(2)}) collective-permute-start(bf16[384,256]{1,0:T(8,128)(2,1)S(1)} %get-tuple-element.339), channel_id=1, source_target_pairs={{31,0},{0,1},{1,2},{2,3},{3,4},{4,5},{5,6},{6,7},{7,8},{8,9},{9,10... | collective-permute-start | bytes 589832 | tf_op jit(solution)/shard_map/while/body/eval_jaxpr/ppermute | solution.py:17
  258.3 15.1 %collective-permute-start = (bf16[384,256]{1,0:T(8,128)(2,1)S(1)}, bf16[384,256]{1,0:T(8,128)(2,1)S(1)}, u32[]{:S(2)}, u32[]{:S(2)}) collective-permute-start(bf16[384,256]{1,0:T(8,128)(2,1)S(1)} %get-tuple-element.339), channel_id=1, source_target_pairs={{31,0},{0,1},{1,2},{2,3},{3,4},{4,5},{5,6},{6,7},{7,8},{8,9},{9,10... | collective-permute-start | bytes 589832 | tf_op jit(solution)/shard_map/while/body/eval_jaxpr/ppermute | solution.py:17
  274.9 15.1 %collective-permute-start = (bf16[384,256]{1,0:T(8,128)(2,1)S(1)}, bf16[384,256]{1,0:T(8,128)(2,1)S(1)}, u32[]{:S(2)}, u32[]{:S(2)}) collective-permute-start(bf16[384,256]{1,0:T(8,128)(2,1)S(1)} %get-tuple-element.339), channel_id=1, source_target_pairs={{31,0},{0,1},{1,2},{2,3},{3,4},{4,5},{5,6},{6,7},{7,8},{8,9},{9,10... | collective-permute-start | bytes 589832 | tf_op jit(solution)/shard_map/while/body/eval_jaxpr/ppermute | solution.py:17
  291.5 15.1 %collective-permute-start = (bf16[384,256]{1,0:T(8,128)(2,1)S(1)}, bf16[384,256]{1,0:T(8,128)(2,1)S(1)}, u32[]{:S(2)}, u32[]{:S(2)}) collective-permute-start(bf16[384,256]{1,0:T(8,128)(2,1)S(1)} %get-tuple-element.339), channel_id=1, source_target_pairs={{31,0},{0,1},{1,2},{2,3},{3,4},{4,5},{5,6},{6,7},{7,8},{8,9},{9,10... | collective-permute-start | bytes 589832 | tf_op jit(solution)/shard_map/while/body/eval_jaxpr/ppermute | solution.py:17
  308.2 15.1 %collective-permute-start = (bf16[384,256]{1,0:T(8,128)(2,1)S(1)}, bf16[384,256]{1,0:T(8,128)(2,1)S(1)}, u32[]{:S(2)}, u32[]{:S(2)}) collective-permute-start(bf16[384,256]{1,0:T(8,128)(2,1)S(1)} %get-tuple-element.339), channel_id=1, source_target_pairs={{31,0},{0,1},{1,2},{2,3},{3,4},{4,5},{5,6},{6,7},{7,8},{8,9},{9,10... | collective-permute-start | bytes 589832 | tf_op jit(solution)/shard_map/while/body/eval_jaxpr/ppermute | solution.py:17
  324.8 15.1 %collective-permute-start = (bf16[384,256]{1,0:T(8,128)(2,1)S(1)}, bf16[384,256]{1,0:T(8,128)(2,1)S(1)}, u32[]{:S(2)}, u32[]{:S(2)}) collective-permute-start(bf16[384,256]{1,0:T(8,128)(2,1)S(1)} %get-tuple-element.339), channel_id=1, source_target_pairs={{31,0},{0,1},{1,2},{2,3},{3,4},{4,5},{5,6},{6,7},{7,8},{8,9},{9,10... | collective-permute-start | bytes 589832 | tf_op jit(solution)/shard_map/while/body/eval_jaxpr/ppermute | solution.py:17
  341.5 15.1 %collective-permute-start = (bf16[384,256]{1,0:T(8,128)(2,1)S(1)}, bf16[384,256]{1,0:T(8,128)(2,1)S(1)}, u32[]{:S(2)}, u32[]{:S(2)}) collective-permute-start(bf16[384,256]{1,0:T(8,128)(2,1)S(1)} %get-tuple-element.339), channel_id=1, source_target_pairs={{31,0},{0,1},{1,2},{2,3},{3,4},{4,5},{5,6},{6,7},{7,8},{8,9},{9,10... | collective-permute-start | bytes 589832 | tf_op jit(solution)/shard_map/while/body/eval_jaxpr/ppermute | solution.py:17
  358.1 15.7 %collective-permute-start = (bf16[384,256]{1,0:T(8,128)(2,1)S(1)}, bf16[384,256]{1,0:T(8,128)(2,1)S(1)}, u32[]{:S(2)}, u32[]{:S(2)}) collective-permute-start(bf16[384,256]{1,0:T(8,128)(2,1)S(1)} %get-tuple-element.339), channel_id=1, source_target_pairs={{31,0},{0,1},{1,2},{2,3},{3,4},{4,5},{5,6},{6,7},{7,8},{8,9},{9,10... | collective-permute-start | bytes 589832 | tf_op jit(solution)/shard_map/while/body/eval_jaxpr/ppermute | solution.py:17
  375.3 16.8 %collective-permute-start = (bf16[384,256]{1,0:T(8,128)(2,1)S(1)}, bf16[384,256]{1,0:T(8,128)(2,1)S(1)}, u32[]{:S(2)}, u32[]{:S(2)}) collective-permute-start(bf16[384,256]{1,0:T(8,128)(2,1)S(1)} %get-tuple-element.339), channel_id=1, source_target_pairs={{31,0},{0,1},{1,2},{2,3},{3,4},{4,5},{5,6},{6,7},{7,8},{8,9},{9,10... | collective-permute-start | bytes 589832 | tf_op jit(solution)/shard_map/while/body/eval_jaxpr/ppermute | solution.py:17
  393.6 16.8 %collective-permute-start = (bf16[384,256]{1,0:T(8,128)(2,1)S(1)}, bf16[384,256]{1,0:T(8,128)(2,1)S(1)}, u32[]{:S(2)}, u32[]{:S(2)}) collective-permute-start(bf16[384,256]{1,0:T(8,128)(2,1)S(1)} %get-tuple-element.339), channel_id=1, source_target_pairs={{31,0},{0,1},{1,2},{2,3},{3,4},{4,5},{5,6},{6,7},{7,8},{8,9},{9,10... | collective-permute-start | bytes 589832 | tf_op jit(solution)/shard_map/while/body/eval_jaxpr/ppermute | solution.py:17
  411.9 15.9 %collective-permute-start = (bf16[384,256]{1,0:T(8,128)(2,1)S(1)}, bf16[384,256]{1,0:T(8,128)(2,1)S(1)}, u32[]{:S(2)}, u32[]{:S(2)}) collective-permute-start(bf16[384,256]{1,0:T(8,128)(2,1)S(1)} %get-tuple-element.339), channel_id=1, source_target_pairs={{31,0},{0,1},{1,2},{2,3},{3,4},{4,5},{5,6},{6,7},{7,8},{8,9},{9,10... | collective-permute-start | bytes 589832 | tf_op jit(solution)/shard_map/while/body/eval_jaxpr/ppermute | solution.py:17
  429.3 15.1 %collective-permute-start = (bf16[384,256]{1,0:T(8,128)(2,1)S(1)}, bf16[384,256]{1,0:T(8,128)(2,1)S(1)}, u32[]{:S(2)}, u32[]{:S(2)}) collective-permute-start(bf16[384,256]{1,0:T(8,128)(2,1)S(1)} %get-tuple-element.339), channel_id=1, source_target_pairs={{31,0},{0,1},{1,2},{2,3},{3,4},{4,5},{5,6},{6,7},{7,8},{8,9},{9,10... | collective-permute-start | bytes 589832 | tf_op jit(solution)/shard_map/while/body/eval_jaxpr/ppermute | solution.py:17
  445.9 15.1 %collective-permute-start = (bf16[384,256]{1,0:T(8,128)(2,1)S(1)}, bf16[384,256]{1,0:T(8,128)(2,1)S(1)}, u32[]{:S(2)}, u32[]{:S(2)}) collective-permute-start(bf16[384,256]{1,0:T(8,128)(2,1)S(1)} %get-tuple-element.339), channel_id=1, source_target_pairs={{31,0},{0,1},{1,2},{2,3},{3,4},{4,5},{5,6},{6,7},{7,8},{8,9},{9,10... | collective-permute-start | bytes 589832 | tf_op jit(solution)/shard_map/while/body/eval_jaxpr/ppermute | solution.py:17
  462.6 15.1 %collective-permute-start = (bf16[384,256]{1,0:T(8,128)(2,1)S(1)}, bf16[384,256]{1,0:T(8,128)(2,1)S(1)}, u32[]{:S(2)}, u32[]{:S(2)}) collective-permute-start(bf16[384,256]{1,0:T(8,128)(2,1)S(1)} %get-tuple-element.339), channel_id=1, source_target_pairs={{31,0},{0,1},{1,2},{2,3},{3,4},{4,5},{5,6},{6,7},{7,8},{8,9},{9,10... | collective-permute-start | bytes 589832 | tf_op jit(solution)/shard_map/while/body/eval_jaxpr/ppermute | solution.py:17
  479.2 15.1 %collective-permute-start = (bf16[384,256]{1,0:T(8,128)(2,1)S(1)}, bf16[384,256]{1,0:T(8,128)(2,1)S(1)}, u32[]{:S(2)}, u32[]{:S(2)}) collective-permute-start(bf16[384,256]{1,0:T(8,128)(2,1)S(1)} %get-tuple-element.339), channel_id=1, source_target_pairs={{31,0},{0,1},{1,2},{2,3},{3,4},{4,5},{5,6},{6,7},{7,8},{8,9},{9,10... | collective-permute-start | bytes 589832 | tf_op jit(solution)/shard_map/while/body/eval_jaxpr/ppermute | solution.py:17
  495.9 15.1 %collective-permute-start = (bf16[384,256]{1,0:T(8,128)(2,1)S(1)}, bf16[384,256]{1,0:T(8,128)(2,1)S(1)}, u32[]{:S(2)}, u32[]{:S(2)}) collective-permute-start(bf16[384,256]{1,0:T(8,128)(2,1)S(1)} %get-tuple-element.339), channel_id=1, source_target_pairs={{31,0},{0,1},{1,2},{2,3},{3,4},{4,5},{5,6},{6,7},{7,8},{8,9},{9,10... | collective-permute-start | bytes 589832 | tf_op jit(solution)/shard_map/while/body/eval_jaxpr/ppermute | solution.py:17
  512.5 15.1 %collective-permute-start = (bf16[384,256]{1,0:T(8,128)(2,1)S(1)}, bf16[384,256]{1,0:T(8,128)(2,1)S(1)}, u32[]{:S(2)}, u32[]{:S(2)}) collective-permute-start(bf16[384,256]{1,0:T(8,128)(2,1)S(1)} %get-tuple-element.339), channel_id=1, source_target_pairs={{31,0},{0,1},{1,2},{2,3},{3,4},{4,5},{5,6},{6,7},{7,8},{8,9},{9,10... | collective-permute-start | bytes 589832 | tf_op jit(solution)/shard_map/while/body/eval_jaxpr/ppermute | solution.py:17
  529.1 15.1 %collective-permute-start = (bf16[384,256]{1,0:T(8,128)(2,1)S(1)}, bf16[384,256]{1,0:T(8,128)(2,1)S(1)}, u32[]{:S(2)}, u32[]{:S(2)}) collective-permute-start(bf16[384,256]{1,0:T(8,128)(2,1)S(1)} %get-tuple-element.339), channel_id=1, source_target_pairs={{31,0},{0,1},{1,2},{2,3},{3,4},{4,5},{5,6},{6,7},{7,8},{8,9},{9,10... | collective-permute-start | bytes 589832 | tf_op jit(solution)/shard_map/while/body/eval_jaxpr/ppermute | solution.py:17
  545.8 15.1 %collective-permute-start = (bf16[384,256]{1,0:T(8,128)(2,1)S(1)}, bf16[384,256]{1,0:T(8,128)(2,1)S(1)}, u32[]{:S(2)}, u32[]{:S(2)}) collective-permute-start(bf16[384,256]{1,0:T(8,128)(2,1)S(1)} %get-tuple-element.339), channel_id=1, source_target_pairs={{31,0},{0,1},{1,2},{2,3},{3,4},{4,5},{5,6},{6,7},{7,8},{8,9},{9,10... | collective-permute-start | bytes 589832 | tf_op jit(solution)/shard_map/while/body/eval_jaxpr/ppermute | solution.py:17
  562.4 15.1 %collective-permute-start = (bf16[384,256]{1,0:T(8,128)(2,1)S(1)}, bf16[384,256]{1,0:T(8,128)(2,1)S(1)}, u32[]{:S(2)}, u32[]{:S(2)}) collective-permute-start(bf16[384,256]{1,0:T(8,128)(2,1)S(1)} %get-tuple-element.339), channel_id=1, source_target_pairs={{31,0},{0,1},{1,2},{2,3},{3,4},{4,5},{5,6},{6,7},{7,8},{8,9},{9,10... | collective-permute-start | bytes 589832 | tf_op jit(solution)/shard_map/while/body/eval_jaxpr/ppermute | solution.py:17
  579.1 15.1 %collective-permute-start = (bf16[384,256]{1,0:T(8,128)(2,1)S(1)}, bf16[384,256]{1,0:T(8,128)(2,1)S(1)}, u32[]{:S(2)}, u32[]{:S(2)}) collective-permute-start(bf16[384,256]{1,0:T(8,128)(2,1)S(1)} %get-tuple-element.339), channel_id=1, source_target_pairs={{31,0},{0,1},{1,2},{2,3},{3,4},{4,5},{5,6},{6,7},{7,8},{8,9},{9,10... | collective-permute-start | bytes 589832 | tf_op jit(solution)/shard_map/while/body/eval_jaxpr/ppermute | solution.py:17
  595.7 15.1 %collective-permute-start = (bf16[384,256]{1,0:T(8,128)(2,1)S(1)}, bf16[384,256]{1,0:T(8,128)(2,1)S(1)}, u32[]{:S(2)}, u32[]{:S(2)}) collective-permute-start(bf16[384,256]{1,0:T(8,128)(2,1)S(1)} %get-tuple-element.339), channel_id=1, source_target_pairs={{31,0},{0,1},{1,2},{2,3},{3,4},{4,5},{5,6},{6,7},{7,8},{8,9},{9,10... | collective-permute-start | bytes 589832 | tf_op jit(solution)/shard_map/while/body/eval_jaxpr/ppermute | solution.py:17
  612.3 15.1 %collective-permute-start = (bf16[384,256]{1,0:T(8,128)(2,1)S(1)}, bf16[384,256]{1,0:T(8,128)(2,1)S(1)}, u32[]{:S(2)}, u32[]{:S(2)}) collective-permute-start(bf16[384,256]{1,0:T(8,128)(2,1)S(1)} %get-tuple-element.339), channel_id=1, source_target_pairs={{31,0},{0,1},{1,2},{2,3},{3,4},{4,5},{5,6},{6,7},{7,8},{8,9},{9,10... | collective-permute-start | bytes 589832 | tf_op jit(solution)/shard_map/while/body/eval_jaxpr/ppermute | solution.py:17
  629.0 15.8 %collective-permute-start = (bf16[384,256]{1,0:T(8,128)(2,1)S(1)}, bf16[384,256]{1,0:T(8,128)(2,1)S(1)}, u32[]{:S(2)}, u32[]{:S(2)}) collective-permute-start(bf16[384,256]{1,0:T(8,128)(2,1)S(1)} %get-tuple-element.339), channel_id=1, source_target_pairs={{31,0},{0,1},{1,2},{2,3},{3,4},{4,5},{5,6},{6,7},{7,8},{8,9},{9,10... | collective-permute-start | bytes 589832 | tf_op jit(solution)/shard_map/while/body/eval_jaxpr/ppermute | solution.py:17
  646.3 149.2 %copy-start.2 = (f32[3072]{0:T(1024)S(1)}, f32[3072]{0:T(1024)}, u32[]{:S(2)}) copy-start(f32[3072]{0:T(1024)} %param.21) | copy-start | bytes 36868
Sparse Core Ops, SparseCore 0:
  10.7 101.6 all-gather.1
  648.6 146.7 reduce-scatter.1
where the time goes:
time: 806 us; the launch traced here: 804 us
  waiting for transfers between devices  664 us (82%)
  starting transfers between devices  60.8 us (8%)
  matrix products  51.7 us (6%)
  between operations  13.5 us (2%)
    ppermute x31, waiting for transfers between devices, from_behind(): return lax.ppermute(block, axis, route)  416 us
    reduce_scatter x1, waiting for transfers between devices, local(): lax.psum_scatter(partial_sum.astype(jnp.float32).astype(jnp.bfloat16), 'g...  147 us
    all_gather x1, waiting for transfers between devices, local(): incoming = lax.all_gather(modulated, 'grp', axis=0, tiled=True)  102 us
    ppermute x31, starting transfers between devices, from_behind(): return lax.ppermute(block, axis, route)  60.7 us
    dot_general x96, matrix products, one_block(): jnp.einsum('hqk,khd->qhd', weights.astype(jnp.bfloat16), block_values, pr...  22.2 us
    dot_general x96, matrix products, one_block(): jnp.einsum('qhd,khd->hqk', queries, block_keys, preferred_element_type=jn...  20 us
  transfers between devices with their start and end apart: 33, of which 33 were waited for; matrix products, arithmetic and copies ran while one was open for 0% of the time, Pallas kernels for 0%

commit v1 on v0

v1 whole, which is shorter than its diff:
```python
import math

import jax
import jax.numpy as jnp
from jax import lax
from jax.experimental import pallas as pl
from jax.experimental.pallas import tpu as pltpu
from jax.sharding import Mesh, PartitionSpec as P

HD = 128
epsilon = 1e-06
AXES = {"y": 4, "zh": 2, "core": 2, "za": 2, "zb": 2, "zc": 2, "x": 4}
ALL = tuple(AXES)
QUAD = ("zb", "zc")
ROWS = 24
F32 = jnp.float32
BF16 = jnp.bfloat16
MIB = 1 << 20


def params(mib):
    return pltpu.CompilerParams(vmem_limit_bytes=mib * MIB)


def swap(block, axis):
    return lax.ppermute(block, axis, [(0, 1), (1, 0)])


def gather_all(block, axis, count):
    copies = jnp.broadcast_to(block[None], (count, *block.shape))
    return lax.all_to_all(copies, axis, 0, 0)


def modulate_kernel(tokens_ref, shift_ref, scale_ref, out_ref):
    widened = tokens_ref[...].astype(F32)
    center = widened - jnp.mean(widened, axis=-1, keepdims=True)
    spread = jnp.mean(center * center, axis=-1, keepdims=True)
    normed = center * lax.rsqrt(spread + epsilon)
    out_ref[...] = (normed * scale_ref[...] + shift_ref[...]).astype(BF16)


def modulate(tokens, shift, scale):
    return pl.pallas_call(
        modulate_kernel,
        out_shape=jax.ShapeDtypeStruct(tokens.shape, BF16),
        compiler_params=params(8),
    )(tokens, shift[None], scale[None])


def project_kernel(steps, tokens_ref, weight_ref, q_gain_ref, k_gain_ref, q_ref, kv_ref, total):
    step = pl.program_id(0)

    @pl.when(step == 0)
    def _():
        total[...] = jnp.zeros_like(total)

    for i in range(3):
        total[i] += jnp.dot(tokens_ref[...], weight_ref[i], preferred_element_type=F32)

    @pl.when(step == steps - 1)
    def _():
        def normed(i, gain):
            part = total[i]
            meansq = jnp.mean(part * part, axis=-1, keepdims=True)
            return part * lax.rsqrt(meansq + epsilon) * gain

        q_ref[...] = normed(0, q_gain_ref[...] * (math.log2(math.e) / math.sqrt(HD))).astype(BF16)
        kv_ref[:, :HD] = normed(1, k_gain_ref[...]).astype(BF16)
        kv_ref[:, HD:] = total[2].astype(BF16)


def project(tokens, weight, q_gain, k_gain):
    rows, width = tokens.shape
    steps = 4
    depth = width // steps
    return pl.pallas_call(
        lambda *refs: project_kernel(steps, *refs),
        grid=(steps,),
        in_specs=[
            pl.BlockSpec((rows, depth), lambda i: (0, i)),
            pl.BlockSpec((3, depth, HD), lambda i: (0, i, 0)),
            pl.BlockSpec((1, HD), lambda i: (0, 0)),
            pl.BlockSpec((1, HD), lambda i: (0, 0)),
        ],
        out_specs=[
            pl.BlockSpec((rows, HD), lambda i: (0, 0)),
            pl.BlockSpec((rows, 2 * HD), lambda i: (0, 0)),
        ],
        out_shape=[
            jax.ShapeDtypeStruct((rows, HD), BF16),
            jax.ShapeDtypeStruct((rows, 2 * HD), BF16),
        ],
        scratch_shapes=[pltpu.VMEM((3, rows, HD), F32)],
        compiler_params=params(16),
        cost_estimate=pl.CostEstimate(
            flops=2 * rows * width * 3 * HD, bytes_accessed=3 * width * HD * 2, transcendentals=0
        ),
    )(tokens, weight, q_gain[None], k_gain[None])


TAIL = 16


def diagonal():
    rows = lax.broadcasted_iota(jnp.int32, (HD, HD), 0)
    return rows == lax.broadcasted_iota(jnp.int32, (HD, HD), 1)


def attend_kernel(q_ref, kv_ref, out_ref):
    rows = q_ref.shape[1]
    keys = kv_ref.shape[0]
    step = 512
    queries = q_ref[0]
    ones = jnp.ones((step, HD), BF16)
    total = jnp.zeros((rows, 2 * HD), F32)
    for at in range(0, keys, step):
        scores = lax.dot_general(
            queries,
            kv_ref[at : at + step, :HD],
            (((1,), (1,)), ((), ())),
            preferred_element_type=F32,
        )
        weights = jnp.exp2(scores).astype(BF16)
        values = jnp.concatenate([kv_ref[at : at + step, HD:], ones], axis=1)
        total += jnp.dot(weights, values, preferred_element_type=F32)
    out_ref[0, :rows] = total[:, :HD].astype(BF16)
    on_diagonal = diagonal()
    row_of = lax.broadcasted_iota(jnp.int32, (TAIL, HD), 0)
    tail = jnp.zeros((TAIL, HD), F32)
    blocks = rows // HD
    for j in range(blocks):
        square = total[j * HD : (j + 1) * HD, HD:]
        row = jnp.sum(jnp.where(on_diagonal, square, 0.0), axis=0, keepdims=True)
        high = row.astype(BF16).astype(F32)
        tail = jnp.where(row_of == j, high, tail)
        tail = jnp.where(row_of == blocks + j, row - high, tail)
    out_ref[0, rows:] = tail.astype(BF16)


def attend(queries, keyval):
    blocks, rows, _ = queries.shape
    keys = keyval.shape[0]
    return pl.pallas_call(
        attend_kernel,
        grid=(blocks,),
        in_specs=[
            pl.BlockSpec((1, rows, HD), lambda i: (i, 0, 0)),
            pl.BlockSpec((keys, 2 * HD), lambda i: (0, 0)),
        ],
        out_specs=pl.BlockSpec((1, rows + TAIL, HD), lambda i: (i, 0, 0)),
        out_shape=jax.ShapeDtypeStruct((blocks, rows + TAIL, HD), BF16),
        compiler_params=params(24),
        cost_estimate=pl.CostEstimate(
            flops=4 * blocks * rows * keys * HD,
            bytes_accessed=4 * keys * HD,
            transcendentals=blocks * rows * keys,
        ),
    )(queries, keyval)


def combine_kernel(partial_ref, weight_ref, own_ref, other_ref):
    rows = partial_ref.shape[1] - TAIL
    blocks = rows // HD
    summed = jnp.sum(partial_ref[...].astype(F32), axis=0)
    on_diagonal = diagonal()
    attended = []
    for j in range(blocks):
        row = summed[rows + j : rows + j + 1] + summed[rows + blocks + j : rows + blocks + j + 1]
        square = jnp.broadcast_to(row, (HD, HD))
        column = jnp.sum(jnp.where(on_diagonal, square, 0.0), axis=1, keepdims=True)
        attended.append((summed[j * HD : (j + 1) * HD] / column).astype(BF16))
    attended = jnp.concatenate(attended, axis=0)
    half = rows // 2
    other_ref[...] = jnp.dot(
        attended[half:], weight_ref[...], preferred_element_type=F32
    ).astype(BF16)
    own_ref[...] = jnp.dot(
        attended[:half], weight_ref[...], preferred_element_type=F32
    ).astype(BF16)


def combine(partial, weight):
    rows = partial.shape[1] - TAIL
    width = weight.shape[1]
    steps = 4
    half = jax.ShapeDtypeStruct((rows // 2, width), BF16)
    return pl.pallas_call(
        combine_kernel,
        grid=(steps,),
        in_specs=[
            pl.BlockSpec(partial.shape, lambda i: (0, 0, 0)),
            pl.BlockSpec((HD, width // steps), lambda i: (0, i)),
        ],
        out_specs=[pl.BlockSpec((rows // 2, width // steps), lambda i: (0, i))] * 2,
        out_shape=[half, half],
        compiler_params=params(16),
        cost_estimate=pl.CostEstimate(
            flops=2 * rows * width * HD, bytes_accessed=2 * rows * width, transcendentals=0
        ),
    )(partial, weight)


def local(tokens, mod_shift, mod_scale, qkv_weight, q_gain, k_gain, out_weight, out_gate):
    width = tokens.shape[1]
    modulated = modulate(tokens, mod_shift, mod_scale)
    both = jnp.concatenate([modulated, swap(modulated, "zh")], axis=0)
    own = gather_all(both, "y", 4).reshape(-1, width)
    other = swap(own, "core")
    q_own, kv_own = project(own, qkv_weight, q_gain, k_gain)
    q_other, kv_other = project(other, qkv_weight, q_gain, k_gain)
    queries = jnp.concatenate([q_own, q_other], axis=0)
    keyval = jnp.concatenate([kv_own, kv_other], axis=0)
    keyval = jnp.concatenate([keyval, swap(keyval, "za")], axis=0)
    queries = gather_all(queries, QUAD, 4)
    keyval = gather_all(keyval, "x", 4).reshape(-1, 2 * HD)
    partial = attend(queries, keyval)
    partial = lax.all_to_all(partial, QUAD, 0, 0)
    own, other = combine(partial, out_weight)
    summed = (own.astype(F32) + swap(other, "core").astype(F32)).astype(BF16)
    summed = lax.all_to_all(summed.reshape(4, -1, width), "y", 0, 0).astype(F32)
    summed = jnp.sum(summed, axis=0)
    arrived = swap(summed[ROWS:].astype(BF16), "zh").astype(F32)
    return ((summed[:ROWS] + arrived) * out_gate).astype(BF16)


def solution(mesh):
    fine = Mesh(mesh.devices.reshape(tuple(AXES.values())), ALL)
    heads = ("y", "zh", "core")
    return jax.shard_map(
        local,
        mesh=fine,
        in_specs=(
            P(ALL, None),
            P(),
            P(),
            P(None, None, heads),
            P(),
            P(),
            P(heads, None),
            P(),
        ),
        out_specs=P(ALL, None),
        check_vma=False,
    )
```

time: 806 us -> 185 us (0.23)
  the two profiles are of different devices: /device:TPU:1 before, /device:TPU:161 now
where the time goes in v1:
time: 185 us; the launch traced here: 184 us
  blocking collectives  75.4 us (41%)
  starting transfers between devices  47.6 us (26%)
  waiting for transfers between devices  43.1 us (23%)
  Pallas kernels  12.9 us (7%)
  local copies, waits for them, and re-layouts  3.39 us (2%)
    ppermute x5, waiting for transfers between devices, swap(): return lax.ppermute(block, axis, [(0, 1), (1, 0)])  43.1 us
    all_to_all x2, blocking collectives, gather_all(): return lax.all_to_all(copies, axis, 0, 0)  38 us
    ppermute x5, starting transfers between devices, swap(): return lax.ppermute(block, axis, [(0, 1), (1, 0)])  37.2 us
    all_to_all x1, blocking collectives, local(): partial = lax.all_to_all(partial, QUAD, 0, 0)  18.7 us
    all_to_all x1, blocking collectives, local(): summed = lax.all_to_all(summed.reshape(4, -1, width), 'y', 0, 0).astype(F32)  18.7 us
    all_to_all x1, starting transfers between devices, gather_all(): return lax.all_to_all(copies, axis, 0, 0)  10.5 us
    pallas_call x1, Pallas kernels, attend(): pl.pallas_call(attend_kernel, grid=(blocks,), in_specs=[pl.BlockSpec((1,...  6.86 us
    pallas_call x2, Pallas kernels, project(): pl.pallas_call(lambda *refs: project_kernel(steps, *refs), grid=(steps,),...  4.02 us
  transfers between devices with their start and end apart: 6, of which 5 were waited for; matrix products, arithmetic and copies ran while one was open for 0% of the time, Pallas kernels for 1%

profile of v1, /device:TPU:161, one launch (start us, length us, event | category | flops | bytes accessed | tf_op | source)
XLA Modules:
  0.0 184.0 jit_solution(583030573233765944)
XLA Ops:
  0.0 0.0 copy-start.2
  0.0 0.9 copy-done.2
  0.9 0.0 copy-start.3
  0.9 0.7 copy-done.3
  1.6 0.0 copy-start.4
  1.6 0.7 copy-done.4
  2.3 0.3 shard_map.82
  2.6 9.7 %collective-permute-start = (bf16[24,3072]{1,0:T(8,128)(2,1)S(1)}, bf16[24,3072]{1,0:T(8,128)(2,1)S(1)}, u32[]{:S(2)}, u32[]{:S(2)}) collective-permute-start(bf16[24,3072]{1,0:T(8,128)(2,1)S(1)} %shard_map.82), channel_id=1, source_target_pairs={{0,64},{64,0},{1,65},{65,1},{2,66},{66,2},{3,67},{67,3},{4,68},{68... | collective-permute-start | bytes 442376 | tf_op jit(solution)/shard_map/ppermute | solution.py:26
  12.3 5.7 %collective-permute-done = bf16[24,3072]{1,0:T(8,128)(2,1)S(1)} collective-permute-done((bf16[24,3072]{1,0:T(8,128)(2,1)S(1)}, bf16[24,3072]{1,0:T(8,128)(2,1)S(1)}, u32[]{:S(2)}, u32[]{:S(2)}) %collective-permute-start) | collective-permute-done | bytes 147488 | tf_op jit(solution)/shard_map/ppermute | solution.py:26
  18.0 0.1 broadcast_in_dim.16
  18.2 0.0 copy-start
  18.2 0.0 copy-start.5
  18.2 0.0 copy-start.6
  18.2 14.6 %all_to_all.25 = bf16[4,48,3072]{2,1,0:T(8,128)(2,1)S(1)} all-to-all(bf16[4,48,3072]{2,1,0:T(8,128)(2,1)S(1)} %broadcast_in_dim.16), channel_id=1, replica_groups=mesh['y'=4,'zh'=2,'core'=2,'za'=2,'zb'=2,'zc'=2,'x'=4] {'y'}, dimensions={0} | all-to-all | bytes 2359296 | tf_op jit(solution)/shard_map/all_to_all | solution.py:31
  32.8 12.0 %collective-permute-start.1 = (bf16[192,3072]{1,0:T(8,128)(2,1)S(1)}, bf16[192,3072]{1,0:T(8,128)(2,1)S(1)}, u32[]{:S(2)}, u32[]{:S(2)}) collective-permute-start(bf16[192,3072]{1,0:T(8,128)(2,1)S(1)} %bitcast.7), channel_id=1, source_target_pairs={{0,32},{32,0},{1,33},{33,1},{2,34},{34,2},{3,35},{35,3},{4,36},{36... | collective-permute-start | bytes 3538952 | tf_op jit(solution)/shard_map/ppermute | solution.py:26
  44.8 0.0 copy-done
  44.8 0.0 copy-done.5
  44.8 0.0 copy-done.6
  44.8 2.0 %shard_map.83 = (bf16[192,128]{1,0:T(8,128)(2,1)S(1)}, bf16[192,256]{1,0:T(8,128)(2,1)S(1)}) custom-call(bf16[192,3072]{1,0:T(8,128)(2,1)S(1)} %bitcast.8, bf16[3,3072,128]{2,1,0:T(8,128)(2,1)S(1)} %copy-done, f32[1,128]{1,0:T(1,128)S(1)} %bitcast.12, f32[1,128]{1,0:T(1,128)S(1)} %bitcast.14), custom_call_target="tpu_custom_call" | custom-call | flops 452984832 | bytes 2359296 | tf_op jit(solution)/shard_map/pallas_call | solution.py:76
  46.9 0.4 collective-permute-done.1.refs_0_
  47.3 2.0 %shard_map.84 = (bf16[192,128]{1,0:T(8,128)(2,1)S(1)}, bf16[192,256]{1,0:T(8,128)(2,1)S(1)}) custom-call(bf16[192,3072]{1,0:T(8,128)(2,1)S(1)} %collective-permute-done.1.refs_0_, bf16[3,3072,128]{2,1,0:T(8,128)(2,1)S(1)} %copy-done, f32[1,128]{1,0:T(1,128)S(1)} %bitcast.13, f32[1,128]{1,0:T(1,128)S(1)} %bitcast.15), custom_call_target="tpu_custom_call" | custom-call | flops 452984832 | bytes 2359296 | tf_op jit(solution)/shard_map/pallas_call | solution.py:76
  49.3 0.8 broadcast_in_dim.38
  50.1 10.5 %all-to-all-start.1 = ((bf16[4,384,128]{2,1,0:T(8,128)(2,1)}), bf16[4,384,128]{2,1,0:T(8,128)(2,1)S(1)}, u32[]{:S(2)}, u32[]{:S(2)}) async-start(bf16[4,384,128]{2,1,0:T(8,128)(2,1)} %broadcast_in_dim.38), calls=%async_computation.1 | async-start | bytes 786432 | tf_op jit(solution)/shard_map/all_to_all | solution.py:31
  60.6 2.0 %collective-permute-start.2 = (bf16[384,256]{1,0:T(8,128)(2,1)S(1)}, bf16[384,256]{1,0:T(8,128)(2,1)S(1)}, u32[]{:S(2)}, u32[]{:S(2)}) collective-permute-start(bf16[384,256]{1,0:T(8,128)(2,1)S(1)} %pad_maximum_fusion.2), channel_id=1, source_target_pairs={{0,16},{16,0},{1,17},{17,1},{2,18},{18,2},{3,19},{19,3},{4,20},{20... | collective-permute-start | bytes 589832 | tf_op jit(solution)/shard_map/ppermute | solution.py:26
  62.6 17.3 %collective-permute-done.2 = bf16[384,256]{1,0:T(8,128)(2,1)S(1)} collective-permute-done((bf16[384,256]{1,0:T(8,128)(2,1)S(1)}, bf16[384,256]{1,0:T(8,128)(2,1)S(1)}, u32[]{:S(2)}, u32[]{:S(2)}) %collective-permute-start.2) | collective-permute-done | bytes 196640 | tf_op jit(solution)/shard_map/ppermute | solution.py:26
  79.9 0.0 all-to-all-done.1.q_ref
  79.9 0.1 broadcast_in_dim.39
  80.0 23.5 %all_to_all.26 = bf16[4,768,256]{2,1,0:T(8,128)(2,1)S(1)} all-to-all(bf16[4,768,256]{2,1,0:T(8,128)(2,1)S(1)} %broadcast_in_dim.39), channel_id=1, replica_groups=mesh['y'=4,'zh'=2,'core'=2,'za'=2,'zb'=2,'zc'=2,'x'=4] {'x'}, dimensions={0} | all-to-all | bytes 3145728 | tf_op jit(solution)/shard_map/all_to_all | solution.py:31
  103.5 0.0 copy-start.1
  103.5 6.9 %shard_map.85 = bf16[4,400,128]{2,1,0:T(8,128)(2,1)S(1)} custom-call(bf16[4,384,128]{2,1,0:T(8,128)(2,1)S(1)} %all-to-all-done.1.q_ref, bf16[3072,256]{1,0:T(8,128)(2,1)S(1)} %bitcast.9), custom_call_target="tpu_custom_call" | custom-call | flops 2415919104 | bytes 1572864 | tf_op jit(solution)/shard_map/pallas_call | solution.py:143
  110.4 18.7 %all_to_all.27.partial_ref = bf16[4,400,128]{2,1,0:T(8,128)(2,1)S(1)} all-to-all(bf16[4,400,128]{2,1,0:T(8,128)(2,1)S(1)} %shard_map.85), channel_id=1, replica_groups=mesh['y'=4,'zh'=2,'core'=2,'za'=2,'zb'=2,'zc'=2,'x'=4] {'zb','zc'}, dimensions={0} | all-to-all | bytes 819200 | tf_op jit(solution)/shard_map/all_to_all | solution.py:217
  129.1 0.0 copy-done.1
  129.1 1.8 shard_map.86
  130.9 5.2 %collective-permute-start.3 = (bf16[192,3072]{1,0:T(8,128)(2,1)S(1)}, bf16[192,3072]{1,0:T(8,128)(2,1)S(1)}, u32[]{:S(2)}, u32[]{:S(2)}) collective-permute-start(bf16[192,3072]{1,0:T(8,128)(2,1)S(1)} %get-tuple-element.16), channel_id=1, source_target_pairs={{0,32},{32,0},{1,33},{33,1},{2,34},{34,2},{3,35},{35,3},{4,36},{36... | collective-permute-start | bytes 3538952 | tf_op jit(solution)/shard_map/ppermute | solution.py:26
  136.0 2.5 %collective-permute-done.3 = bf16[192,3072]{1,0:T(8,128)(2,1)S(1)} collective-permute-done((bf16[192,3072]{1,0:T(8,128)(2,1)S(1)}, bf16[192,3072]{1,0:T(8,128)(2,1)S(1)}, u32[]{:S(2)}, u32[]{:S(2)}) %collective-permute-start.3) | collective-permute-done | bytes 1179680 | tf_op jit(solution)/shard_map/ppermute | solution.py:26
  138.5 0.4 add_convert_fusion
  138.9 18.7 %all_to_all.28 = bf16[4,48,3072]{2,1,0:T(8,128)(2,1)S(1)} all-to-all(bf16[4,48,3072]{2,1,0:T(8,128)(2,1)S(1)} %bitcast.16), channel_id=1, replica_groups=mesh['y'=4,'zh'=2,'core'=2,'za'=2,'zb'=2,'zc'=2,'x'=4] {'y'}, dimensions={0} | all-to-all | bytes 2359296 | tf_op jit(solution)/shard_map/all_to_all | solution.py:220
  157.6 0.0 copy-start.7
  157.6 0.2 convert_reduce_fusion
  157.8 8.2 %collective-permute-start.4 = (bf16[24,3072]{1,0:T(8,128)(2,1)S(1)}, bf16[24,3072]{1,0:T(8,128)(2,1)S(1)}, u32[]{:S(2)}, u32[]{:S(2)}) collective-permute-start(bf16[24,3072]{1,0:T(8,128)(2,1)S(1)} %slice.17), channel_id=1, source_target_pairs={{0,64},{64,0},{1,65},{65,1},{2,66},{66,2},{3,67},{67,3},{4,68},{68... | collective-permute-start | bytes 442376 | tf_op jit(solution)/shard_map/ppermute | solution.py:26
  166.1 17.3 %collective-permute-done.4 = bf16[24,3072]{1,0:T(8,128)(2,1)S(1)} collective-permute-done((bf16[24,3072]{1,0:T(8,128)(2,1)S(1)}, bf16[24,3072]{1,0:T(8,128)(2,1)S(1)}, u32[]{:S(2)}, u32[]{:S(2)}) %collective-permute-start.4) | collective-permute-done | bytes 147488 | tf_op jit(solution)/shard_map/ppermute | solution.py:26
  183.3 0.0 copy-done.7
  183.3 0.7 fusion.1
  (5 shorter events, 0.1 us)
Async XLA Ops:
  0.0 0.9 copy-start.2
  0.9 0.7 copy-start.3
  1.6 0.7 copy-start.4
  2.6 15.4 %collective-permute-start = (bf16[24,3072]{1,0:T(8,128)(2,1)S(1)}, bf16[24,3072]{1,0:T(8,128)(2,1)S(1)}, u32[]{:S(2)}, u32[]{:S(2)}) collective-permute-start(bf16[24,3072]{1,0:T(8,128)(2,1)S(1)} %shard_map.82), channel_id=1, source_target_pairs={{0,64},{64,0},{1,65},{65,1},{2,66},{66,2},{3,67},{67,3},{4,68},{68... | collective-permute-start | bytes 442376 | tf_op jit(solution)/shard_map/ppermute | solution.py:26
  18.2 26.6 %copy-start = (bf16[3,3072,128]{2,1,0:T(8,128)(2,1)S(1)}, bf16[3,3072,128]{2,1,0:T(8,128)(2,1)}, u32[]{:S(2)}) copy-start(bf16[3,3072,128]{2,1,0:T(8,128)(2,1)} %refs_1_.3) | copy-start | bytes 7077892
  18.2 26.6 %copy-start.5 = (f32[128]{0:T(128)S(1)}, f32[128]{0:T(128)}, u32[]{:S(2)}) copy-start(f32[128]{0:T(128)} %param.12) | copy-start | bytes 1540
  18.2 26.6 %copy-start.6 = (f32[128]{0:T(128)S(1)}, f32[128]{0:T(128)}, u32[]{:S(2)}) copy-start(f32[128]{0:T(128)} %param.13) | copy-start | bytes 1540
  32.8 14.5 %collective-permute-start.1 = (bf16[192,3072]{1,0:T(8,128)(2,1)S(1)}, bf16[192,3072]{1,0:T(8,128)(2,1)S(1)}, u32[]{:S(2)}, u32[]{:S(2)}) collective-permute-start(bf16[192,3072]{1,0:T(8,128)(2,1)S(1)} %bitcast.7), channel_id=1, source_target_pairs={{0,32},{32,0},{1,33},{33,1},{2,34},{34,2},{3,35},{35,3},{4,36},{36... | collective-permute-start | bytes 3538952 | tf_op jit(solution)/shard_map/ppermute | solution.py:26
  50.1 29.8 %all-to-all-start.1 = ((bf16[4,384,128]{2,1,0:T(8,128)(2,1)}), bf16[4,384,128]{2,1,0:T(8,128)(2,1)S(1)}, u32[]{:S(2)}, u32[]{:S(2)}) async-start(bf16[4,384,128]{2,1,0:T(8,128)(2,1)} %broadcast_in_dim.38), calls=%async_computation.1 | async-start | bytes 786432 | tf_op jit(solution)/shard_map/all_to_all | solution.py:31
  60.6 19.3 %collective-permute-start.2 = (bf16[384,256]{1,0:T(8,128)(2,1)S(1)}, bf16[384,256]{1,0:T(8,128)(2,1)S(1)}, u32[]{:S(2)}, u32[]{:S(2)}) collective-permute-start(bf16[384,256]{1,0:T(8,128)(2,1)S(1)} %pad_maximum_fusion.2), channel_id=1, source_target_pairs={{0,16},{16,0},{1,17},{17,1},{2,18},{18,2},{3,19},{19,3},{4,20},{20... | collective-permute-start | bytes 589832 | tf_op jit(solution)/shard_map/ppermute | solution.py:26
  103.5 25.6 %copy-start.1 = (bf16[128,3072]{1,0:T(8,128)(2,1)S(1)}, bf16[128,3072]{1,0:T(8,128)(2,1)}, u32[]{:S(2)}) copy-start(bf16[128,3072]{1,0:T(8,128)(2,1)} %weight_ref.1) | copy-start | bytes 2359300
  130.9 7.6 %collective-permute-start.3 = (bf16[192,3072]{1,0:T(8,128)(2,1)S(1)}, bf16[192,3072]{1,0:T(8,128)(2,1)S(1)}, u32[]{:S(2)}, u32[]{:S(2)}) collective-permute-start(bf16[192,3072]{1,0:T(8,128)(2,1)S(1)} %get-tuple-element.16), channel_id=1, source_target_pairs={{0,32},{32,0},{1,33},{33,1},{2,34},{34,2},{3,35},{35,3},{4,36},{36... | collective-permute-start | bytes 3538952 | tf_op jit(solution)/shard_map/ppermute | solution.py:26
  157.6 25.7 %copy-start.7 = (f32[3072]{0:T(1024)S(1)}, f32[3072]{0:T(1024)}, u32[]{:S(2)}) copy-start(f32[3072]{0:T(1024)} %param.15) | copy-start | bytes 36868
  157.8 25.5 %collective-permute-start.4 = (bf16[24,3072]{1,0:T(8,128)(2,1)S(1)}, bf16[24,3072]{1,0:T(8,128)(2,1)S(1)}, u32[]{:S(2)}, u32[]{:S(2)}) collective-permute-start(bf16[24,3072]{1,0:T(8,128)(2,1)S(1)} %slice.17), channel_id=1, source_target_pairs={{0,64},{64,0},{1,65},{65,1},{2,66},{66,2},{3,67},{67,3},{4,68},{68... | collective-permute-start | bytes 442376 | tf_op jit(solution)/shard_map/ppermute | solution.py:26

commit v2 on v1

v2 whole, which is shorter than its diff:
```python
import math

import jax
import jax.numpy as jnp
from jax import lax
from jax.experimental import pallas as pl
from jax.experimental.pallas import tpu as pltpu
from jax.sharding import Mesh, PartitionSpec as P

HD = 128
epsilon = 1e-06
AXES = {"y": 4, "zh": 2, "core": 2, "za": 2, "zb": 2, "zc": 2, "x": 4}
ALL = tuple(AXES)
QUAD = ("zb", "zc")
F32 = jnp.float32
BF16 = jnp.bfloat16
MIB = 1 << 20


def params(mib):
    return pltpu.CompilerParams(vmem_limit_bytes=mib * MIB)


def swap(block, axis):
    return lax.ppermute(block, axis, [(0, 1), (1, 0)])


def across(block, distance):
    return lax.ppermute(block, QUAD, [(i, i ^ distance) for i in range(4)])


def gather_all(block, axis, count):
    copies = jnp.broadcast_to(block[None], (count, *block.shape))
    return lax.all_to_all(copies, axis, 0, 0)


def modulate_kernel(tokens_ref, shift_ref, scale_ref, out_ref):
    widened = tokens_ref[...].astype(F32)
    center = widened - jnp.mean(widened, axis=-1, keepdims=True)
    spread = jnp.mean(center * center, axis=-1, keepdims=True)
    normed = center * lax.rsqrt(spread + epsilon)
    out_ref[...] = (normed * scale_ref[...] + shift_ref[...]).astype(BF16)


def modulate(tokens, shift, scale):
    return pl.pallas_call(
        modulate_kernel,
        out_shape=jax.ShapeDtypeStruct(tokens.shape, BF16),
        compiler_params=params(8),
    )(tokens, shift[None], scale[None])


def project_kernel(
    steps, own_ref, other_ref, weight_ref, q_gain_ref, k_gain_ref, q_ref, kv_ref, total
):
    step = pl.program_id(0)

    @pl.when(step == 0)
    def _():
        total[...] = jnp.zeros_like(total)

    tokens = jnp.concatenate([own_ref[...], other_ref[...]], axis=0)
    weight = jnp.concatenate([weight_ref[i] for i in range(3)], axis=1)
    total[...] += jnp.dot(tokens, weight, preferred_element_type=F32)

    @pl.when(step == steps - 1)
    def _():
        def normed(i, gain):
            part = total[:, i * HD : (i + 1) * HD]
            meansq = jnp.mean(part * part, axis=-1, keepdims=True)
            return part * lax.rsqrt(meansq + epsilon) * gain

        q_ref[...] = normed(0, q_gain_ref[...] * (math.log2(math.e) / math.sqrt(HD))).astype(BF16)
        kv_ref[:, :HD] = normed(1, k_gain_ref[...]).astype(BF16)
        kv_ref[:, HD:] = total[:, 2 * HD :].astype(BF16)


def project(own, other, weight, q_gain, k_gain):
    half, width = own.shape
    rows = 2 * half
    steps = 4
    depth = width // steps
    return pl.pallas_call(
        lambda *refs: project_kernel(steps, *refs),
        grid=(steps,),
        in_specs=[
            pl.BlockSpec((half, depth), lambda i: (0, i)),
            pl.BlockSpec((half, depth), lambda i: (0, i)),
            pl.BlockSpec((3, depth, HD), lambda i: (0, i, 0)),
            pl.BlockSpec((1, HD), lambda i: (0, 0)),
            pl.BlockSpec((1, HD), lambda i: (0, 0)),
        ],
        out_specs=[
            pl.BlockSpec((rows, HD), lambda i: (0, 0)),
            pl.BlockSpec((rows, 2 * HD), lambda i: (0, 0)),
        ],
        out_shape=[
            jax.ShapeDtypeStruct((rows, HD), BF16),
            jax.ShapeDtypeStruct((rows, 2 * HD), BF16),
        ],
        scratch_shapes=[pltpu.VMEM((rows, 3 * HD), F32)],
        compiler_params=params(16),
        cost_estimate=pl.CostEstimate(
            flops=2 * rows * width * 3 * HD, bytes_accessed=3 * width * HD * 2, transcendentals=0
        ),
    )(own, other, weight, q_gain[None], k_gain[None])


TAIL = 16


def diagonal(rows):
    down = lax.broadcasted_iota(jnp.int32, (rows, HD), 0)
    return down == lax.broadcasted_iota(jnp.int32, (rows, HD), 1)


def row_blocks(rows):
    return [(at, min(HD, rows - at)) for at in range(0, rows, HD)]


def add_keys(queries, kv_ref, total):
    step = 512
    ones = jnp.ones((step, HD), BF16)
    for at in range(0, kv_ref.shape[0], step):
        scores = lax.dot_general(
            queries,
            kv_ref[at : at + step, :HD],
            (((1,), (1,)), ((), ())),
            preferred_element_type=F32,
        )
        weights = jnp.exp2(scores).astype(BF16)
        values = jnp.concatenate([kv_ref[at : at + step, HD:], ones], axis=1)
        product = jnp.dot(weights, values, preferred_element_type=F32)
        total = product if total is None else total + product
    return total


def attend_first_kernel(q_ref, kv_ref, total_ref):
    total_ref[0] = add_keys(q_ref[0], kv_ref, None)


def attend_last_kernel(me_ref, q_ref, kv_ref, total_ref, out_ref):
    rows = q_ref.shape[1]
    total = add_keys(q_ref[0], kv_ref, total_ref[0])
    out_ref[0, :rows] = total[:, :HD].astype(BF16)
    row_of = lax.broadcasted_iota(jnp.int32, (TAIL, HD), 0)
    tail = jnp.zeros((TAIL, HD), F32)
    blocks = row_blocks(rows)
    for j, (at, size) in enumerate(blocks):
        square = total[at : at + size, HD:]
        row = jnp.sum(jnp.where(diagonal(size), square, 0.0), axis=0, keepdims=True)
        high = row.astype(BF16).astype(F32)
        tail = jnp.where(row_of == j, high, tail)
        tail = jnp.where(row_of == len(blocks) + j, row - high, tail)
    out_ref[0, rows:] = tail.astype(BF16)


def attend_cost(blocks, rows, keys):
    return pl.CostEstimate(
        flops=4 * blocks * rows * keys * HD,
        bytes_accessed=4 * keys * HD,
        transcendentals=blocks * rows * keys,
    )


def attend_first(queries, keyval):
    blocks, rows, _ = queries.shape
    keys = keyval.shape[0]
    return pl.pallas_call(
        attend_first_kernel,
        grid=(blocks,),
        in_specs=[
            pl.BlockSpec((1, rows, HD), lambda i: (i, 0, 0)),
            pl.BlockSpec((keys, 2 * HD), lambda i: (0, 0)),
        ],
        out_specs=pl.BlockSpec((1, rows, 2 * HD), lambda i: (i, 0, 0)),
        out_shape=jax.ShapeDtypeStruct((blocks, rows, 2 * HD), F32),
        compiler_params=params(24),
        cost_estimate=attend_cost(blocks, rows, keys),
    )(queries, keyval)


def attend_last(me, queries, keyval, total, part):
    blocks, rows, _ = queries.shape
    rows //= 2
    keys = keyval.shape[0]
    return pl.pallas_call(
        attend_last_kernel,
        grid_spec=pltpu.PrefetchScalarGridSpec(
            num_scalar_prefetch=1,
            grid=(blocks,),
            in_specs=[
                pl.BlockSpec((1, rows, HD), lambda i, me: (i ^ me[0], part, 0)),
                pl.BlockSpec((keys, 2 * HD), lambda i, me: (0, 0)),
                pl.BlockSpec((1, rows, 2 * HD), lambda i, me: (i ^ me[0], part, 0)),
            ],
            out_specs=pl.BlockSpec((1, rows + TAIL, HD), lambda i, me: (i, 0, 0)),
        ),
        out_shape=jax.ShapeDtypeStruct((blocks, rows + TAIL, HD), BF16),
        compiler_params=params(24),
        cost_estimate=attend_cost(blocks, rows, keys),
    )(me, queries, keyval, total)


def combine_kernel(partial_ref, weight_ref, own_ref, other_ref):
    rows = partial_ref.shape[1] - TAIL
    summed = jnp.sum(partial_ref[...].astype(F32), axis=0)
    blocks = row_blocks(rows)
    attended = []
    for j, (at, size) in enumerate(blocks):
        low = rows + len(blocks) + j
        row = summed[rows + j : rows + j + 1] + summed[low : low + 1]
        square = jnp.broadcast_to(row, (size, HD))
        column = jnp.sum(jnp.where(diagonal(size), square, 0.0), axis=1, keepdims=True)
        attended.append((summed[at : at + size] / column).astype(BF16))
    attended = jnp.concatenate(attended, axis=0)
    mixed = jnp.dot(attended, weight_ref[...], preferred_element_type=F32).astype(BF16)
    half = rows // 2
    own_ref[...] = mixed[:half]
    other_ref[...] = mixed[half:]


def combine(partial, weight):
    rows = partial.shape[1] - TAIL
    width = weight.shape[1]
    steps = 4
    half = jax.ShapeDtypeStruct((rows // 2, width), BF16)
    return pl.pallas_call(
        combine_kernel,
        grid=(steps,),
        in_specs=[
            pl.BlockSpec(partial.shape, lambda i: (0, 0, 0)),
            pl.BlockSpec((HD, width // steps), lambda i: (0, i)),
        ],
        out_specs=[pl.BlockSpec((rows // 2, width // steps), lambda i: (0, i))] * 2,
        out_shape=[half, half],
        compiler_params=params(16),
        cost_estimate=pl.CostEstimate(
            flops=2 * rows * width * HD, bytes_accessed=2 * rows * width, transcendentals=0
        ),
    )(partial, weight)


def local(tokens, mod_shift, mod_scale, qkv_weight, q_gain, k_gain, out_weight, out_gate):
    width = tokens.shape[1]

    def spread(part):
        own = gather_all(modulate(part, mod_shift, mod_scale), "y", 4).reshape(-1, width)
        return project(own, swap(own, "core"), qkv_weight, q_gain, k_gain)

    def share(keyval):
        keyval = jnp.concatenate([keyval, swap(keyval, "za")], axis=0)
        return gather_all(keyval, "x", 4).reshape(-1, 2 * HD)

    def collect(partial):
        own, other = combine(lax.all_to_all(partial, QUAD, 0, 0), out_weight)
        summed = (own.astype(F32) + swap(other, "core").astype(F32)).astype(BF16)
        summed = lax.all_to_all(summed.reshape(4, -1, width), "y", 0, 0).astype(F32)
        return jnp.sum(summed, axis=0)

    far = swap(tokens, "zh")
    near_q, near_kv = spread(tokens)
    far_q, far_kv = spread(far)
    near_kv = share(near_kv)
    queries = jnp.concatenate([near_q, far_q], axis=0)
    queries = jnp.stack([queries] + [across(queries, i) for i in (1, 2, 3)])
    far_kv = share(far_kv)
    me = lax.axis_index(QUAD).astype(jnp.int32).reshape(1)
    total = attend_first(queries, near_kv)
    far_sum = collect(attend_last(me, queries, far_kv, total, 1))
    near_sum = collect(attend_last(me, queries, far_kv, total, 0))
    arrived = swap(far_sum.astype(BF16), "zh").astype(F32)
    return ((near_sum + arrived) * out_gate).astype(BF16)


def solution(mesh):
    fine = Mesh(mesh.devices.reshape(tuple(AXES.values())), ALL)
    heads = ("y", "zh", "core")
    return jax.shard_map(
        local,
        mesh=fine,
        in_specs=(
            P(ALL, None),
            P(),
            P(),
            P(None, None, heads),
            P(),
            P(),
            P(heads, None),
            P(),
        ),
        out_specs=P(ALL, None),
        check_vma=False,
    )
```

time: 185 us -> 189 us (1.022)
  the two profiles are of different devices: /device:TPU:161 before, /device:TPU:42 now
where the time goes in v2:
time: 189 us; the launch traced here: 188 us
  starting transfers between devices  86.7 us (46%)
  waiting for transfers between devices  58.8 us (31%)
  Pallas kernels  20.9 us (11%)
  blocking collectives  12.3 us (7%)
  local copies, waits for them, and re-layouts  5.9 us (3%)
  other arithmetic  2.94 us (2%)
    ppermute x8, waiting for transfers between devices, swap(): return lax.ppermute(block, axis, [(0, 1), (1, 0)])  43.1 us
    ppermute x8, starting transfers between devices, swap(): return lax.ppermute(block, axis, [(0, 1), (1, 0)])  43 us
    all_to_all x3, starting transfers between devices, gather_all(): return lax.all_to_all(copies, axis, 0, 0)  14.7 us
    all_to_all x1, blocking collectives, gather_all(): return lax.all_to_all(copies, axis, 0, 0)  12.3 us
    all_to_all x2, starting transfers between devices, collect(): summed = lax.all_to_all(summed.reshape(4, -1, width), 'y', 0, 0).astype(F32)  9.94 us
    all_to_all x2, starting transfers between devices, collect(): own, other = combine(lax.all_to_all(partial, QUAD, 0, 0), out_weight)  9.88 us
    ppermute x3, starting transfers between devices, across(): return lax.ppermute(block, QUAD, [(i, i ^ distance) for i in range(4)])  9.21 us
    all_to_all x2, waiting for transfers between devices, collect(): summed = lax.all_to_all(summed.reshape(4, -1, width), 'y', 0, 0).astype(F32)  8.66 us
  transfers between devices with their start and end apart: 18, of which 9 were waited for; matrix products, arithmetic and copies ran while one was open for 2% of the time, Pallas kernels for 9%

profile of v2, /device:TPU:42, one launch (start us, length us, event | category | flops | bytes accessed | tf_op | source)
XLA Modules:
  0.0 187.9 jit_solution(17822212513905977823)
XLA Ops:
  0.0 0.9 copy-done.3
  0.9 0.7 copy-done.5
  1.6 0.7 copy-done.7
  2.3 0.3 shard_map.82
  2.6 0.9 broadcast_in_dim.18
  3.5 5.0 %all-to-all-start = ((bf16[4,24,3072]{2,1,0:T(8,128)(2,1)}), bf16[4,24,3072]{2,1,0:T(8,128)(2,1)S(1)}, u32[]{:S(2)}, u32[]{:S(2)}) async-start(bf16[4,24,3072]{2,1,0:T(8,128)(2,1)} %broadcast_in_dim.18), calls=%async_computation | async-start | bytes 1179648 | tf_op jit(solution)/shard_map/all_to_all | solution.py:34
  8.5 0.0 copy-done.4
  8.5 15.0 %collective-permute-start.1 = (bf16[24,3072]{1,0:T(8,128)(2,1)S(1)}, bf16[24,3072]{1,0:T(8,128)(2,1)S(1)}, u32[]{:S(2)}, u32[]{:S(2)}) collective-permute-start(bf16[24,3072]{1,0:T(8,128)(2,1)S(1)} %copy-done.4), channel_id=1, source_target_pairs={{0,64},{64,0},{1,65},{65,1},{2,66},{66,2},{3,67},{67,3},{4,68},{68... | collective-permute-start | bytes 442376 | tf_op jit(solution)/shard_map/ppermute | solution.py:25
  23.5 0.0 all-to-all-done
  23.5 1.9 %collective-permute-start = (bf16[96,3072]{1,0:T(8,128)(2,1)S(1)}, bf16[96,3072]{1,0:T(8,128)(2,1)S(1)}, u32[]{:S(2)}, u32[]{:S(2)}) collective-permute-start(bf16[96,3072]{1,0:T(8,128)(2,1)S(1)} %bitcast.17), channel_id=1, source_target_pairs={{0,32},{32,0},{1,33},{33,1},{2,34},{34,2},{3,35},{35,3},{4,36},{36... | collective-permute-start | bytes 1769480 | tf_op jit(solution)/shard_map/ppermute | solution.py:25
  25.4 10.4 %collective-permute-done.1.tokens_ref = bf16[24,3072]{1,0:T(8,128)(2,1)S(1)} collective-permute-done((bf16[24,3072]{1,0:T(8,128)(2,1)S(1)}, bf16[24,3072]{1,0:T(8,128)(2,1)S(1)}, u32[]{:S(2)}, u32[]{:S(2)}) %collective-permute-start.1) | collective-permute-done | bytes 147488 | tf_op jit(solution)/shard_map/ppermute | solution.py:25
  35.9 0.0 copy-done.6
  35.9 0.0 copy-done.8
  35.9 0.3 shard_map.84
  36.2 12.3 %all_to_all.40 = bf16[4,24,3072]{2,1,0:T(8,128)(2,1)S(1)} all-to-all(bf16[4,24,3072]{2,1,0:T(8,128)(2,1)S(1)} %broadcast_in_dim.21), channel_id=1, replica_groups=mesh['y'=4,'zh'=2,'core'=2,'za'=2,'zb'=2,'zc'=2,'x'=4] {'y'}, dimensions={0} | all-to-all | bytes 1179648 | tf_op jit(solution)/shard_map/all_to_all | solution.py:34
  48.5 1.9 %collective-permute-start.2 = (bf16[96,3072]{1,0:T(8,128)(2,1)S(1)}, bf16[96,3072]{1,0:T(8,128)(2,1)}, u32[]{:S(2)}, u32[]{:S(2)}) collective-permute-start(bf16[96,3072]{1,0:T(8,128)(2,1)S(1)} %bitcast.19), channel_id=1, source_target_pairs={{0,32},{32,0},{1,33},{33,1},{2,34},{34,2},{3,35},{35,3},{4,36},{36... | collective-permute-start | bytes 1769480 | tf_op jit(solution)/shard_map/ppermute | solution.py:25
  50.4 0.0 collective-permute-done.refs_1_
  50.4 1.8 shard_map.83
  52.2 0.0 copy-start.9
  52.2 4.0 %collective-permute-start.7 = (bf16[192,256]{1,0:T(8,128)(2,1)S(1)}, bf16[192,256]{1,0:T(8,128)(2,1)S(1)}, u32[]{:S(2)}, u32[]{:S(2)}) collective-permute-start(bf16[192,256]{1,0:T(8,128)(2,1)S(1)} %get-tuple-element.16), channel_id=1, source_target_pairs={{0,16},{16,0},{1,17},{17,1},{2,18},{18,2},{3,19},{19,3},{4,20},{20... | collective-permute-start | bytes 294920 | tf_op jit(solution)/shard_map/ppermute | solution.py:25
  56.3 10.2 %collective-permute-done.7 = bf16[192,256]{1,0:T(8,128)(2,1)S(1)} collective-permute-done((bf16[192,256]{1,0:T(8,128)(2,1)S(1)}, bf16[192,256]{1,0:T(8,128)(2,1)S(1)}, u32[]{:S(2)}, u32[]{:S(2)}) %collective-permute-start.7) | collective-permute-done | bytes 98336 | tf_op jit(solution)/shard_map/ppermute | solution.py:25
  66.4 1.0 broadcast_in_dim.23
  67.4 4.8 %all-to-all-start.3 = ((bf16[4,384,256]{2,1,0:T(8,128)(2,1)}), bf16[4,384,256]{2,1,0:T(8,128)(2,1)}, u32[]{:S(2)}, u32[]{:S(2)}) async-start(bf16[4,384,256]{2,1,0:T(8,128)(2,1)} %broadcast_in_dim.23), calls=%async_computation.3 | async-start | bytes 1572864 | tf_op jit(solution)/shard_map/all_to_all | solution.py:34
  72.2 0.0 collective-permute-done.2.refs_1_
  72.2 3.1 %shard_map.85 = (bf16[192,128]{1,0:T(8,128)(2,1)S(1)}, bf16[192,256]{1,0:T(8,128)(2,1)S(1)}) custom-call(bf16[96,3072]{1,0:T(8,128)(2,1)S(1)} %bitcast.20, bf16[96,3072]{1,0:T(8,128)(2,1)} %collective-permute-done.2.refs_1_, bf16[3,3072,128]{2,1,0:T(8,128)(2,1)S(1)} %copy-done, f32[1,128]{1,0:T(1,128)S(1)} %bitcast.26, f32[1,128]{1,0:T(1,128)S(1)} %bitcast.28), custom_call_target="tpu_custom_call" | custom-call | flops 452984832 | bytes 2359296 | tf_op jit(solution)/shard_map/pallas_call | solution.py:83
  75.3 3.1 %collective-permute-start.6 = (bf16[192,256]{1,0:T(8,128)(2,1)S(1)}, bf16[192,256]{1,0:T(8,128)(2,1)S(1)}, u32[]{:S(2)}, u32[]{:S(2)}) collective-permute-start(bf16[192,256]{1,0:T(8,128)(2,1)S(1)} %get-tuple-element.15), channel_id=1, source_target_pairs={{0,16},{16,0},{1,17},{17,1},{2,18},{18,2},{3,19},{19,3},{4,20},{20... | collective-permute-start | bytes 294920 | tf_op jit(solution)/shard_map/ppermute | solution.py:25
  78.4 9.7 %collective-permute-done.6 = bf16[192,256]{1,0:T(8,128)(2,1)S(1)} collective-permute-done((bf16[192,256]{1,0:T(8,128)(2,1)S(1)}, bf16[192,256]{1,0:T(8,128)(2,1)S(1)}, u32[]{:S(2)}, u32[]{:S(2)}) %collective-permute-start.6) | collective-permute-done | bytes 98336 | tf_op jit(solution)/shard_map/ppermute | solution.py:25
  88.2 0.0 copy-start.10
  88.2 0.0 all-to-all-done.3
  88.2 1.0 broadcast_in_dim.22
  89.1 4.8 %all-to-all-start.2 = ((bf16[4,384,256]{2,1,0:T(8,128)(2,1)}), bf16[4,384,256]{2,1,0:T(8,128)(2,1)S(1)}, u32[]{:S(2)}, u32[]{:S(2)}) async-start(bf16[4,384,256]{2,1,0:T(8,128)(2,1)} %broadcast_in_dim.22), calls=%async_computation.2 | async-start | bytes 1572864 | tf_op jit(solution)/shard_map/all_to_all | solution.py:34
  94.0 1.9 %collective-permute-start.5 = (bf16[384,128]{1,0:T(8,128)(2,1)S(1)}, bf16[384,128]{1,0:T(8,128)(2,1)S(1)}, u32[]{:S(2)}, u32[]{:S(2)}) collective-permute-start(bf16[384,128]{1,0:T(8,128)(2,1)S(1)} %constant_dynamic-update-slice_fusion), channel_id=1, source_target_pairs={{0,12},{4,8},{8,4},{12,0},{1,13},{5,9},{9,5},{13,1},{2,14},{6,10},... | collective-permute-start | bytes 294920 | tf_op jit(solution)/shard_map/ppermute | solution.py:29
  95.9 1.9 %collective-permute-start.4 = (bf16[384,128]{1,0:T(8,128)(2,1)S(1)}, bf16[384,128]{1,0:T(8,128)(2,1)S(1)}, u32[]{:S(2)}, u32[]{:S(2)}) collective-permute-start(bf16[384,128]{1,0:T(8,128)(2,1)S(1)} %constant_dynamic-update-slice_fusion), channel_id=1, source_target_pairs={{0,8},{4,12},{8,0},{12,4},{1,9},{5,13},{9,1},{13,5},{2,10},{6,14},... | collective-permute-start | bytes 294920 | tf_op jit(solution)/shard_map/ppermute | solution.py:29
  97.8 5.4 %collective-permute-start.3 = (bf16[384,128]{1,0:T(8,128)(2,1)S(1)}, bf16[384,128]{1,0:T(8,128)(2,1)S(1)}, u32[]{:S(2)}, u32[]{:S(2)}) collective-permute-start(bf16[384,128]{1,0:T(8,128)(2,1)S(1)} %constant_dynamic-update-slice_fusion), channel_id=1, source_target_pairs={{0,4},{4,0},{8,12},{12,8},{1,5},{5,1},{9,13},{13,9},{2,6},{6,2},{1... | collective-permute-start | bytes 294920 | tf_op jit(solution)/shard_map/ppermute | solution.py:29
  103.2 0.0 collective-permute-done.5
  103.2 1.1 collective-permute-done.4
  104.3 1.4 collective-permute-done.3
  105.8 0.1 pad_maximum_fusion.q_ref
  105.8 5.5 %shard_map.86.total_ref = f32[4,384,256]{2,1,0:T(8,128)S(1)} custom-call(bf16[4,384,128]{2,1,0:T(8,128)(2,1)S(1)} %pad_maximum_fusion.q_ref, bf16[1536,256]{1,0:T(8,128)(2,1)} %bitcast.12.kv_ref), custom_call_target="tpu_custom_call" | custom-call | flops 1207959552 | bytes 786432 | tf_op jit(solution)/shard_map/pallas_call | solution.py:169
  111.4 0.0 all-to-all-done.2
  111.4 3.0 %shard_map.89 = bf16[4,208,128]{2,1,0:T(8,128)(2,1)} custom-call(s32[1]{0:T(128)} %bitcast.me_ref, bf16[4,384,128]{2,1,0:T(8,128)(2,1)S(1)} %pad_maximum_fusion.q_ref, bf16[1536,256]{1,0:T(8,128)(2,1)S(1)} %bitcast.15, f32[4,384,256]{2,1,0:T(8,128)S(1)} %shard_map.86.total_ref), custom_call_target="tpu_custom_call" | custom-call | flops 603979776 | bytes 786432 | tf_op jit(solution)/shard_map/pallas_call | solution.py:187
  114.4 6.0 %all-to-all-start.6 = ((bf16[4,208,128]{2,1,0:T(8,128)(2,1)}), bf16[4,208,128]{2,1,0:T(8,128)(2,1)}, u32[]{:S(2)}, u32[]{:S(2)}) async-start(bf16[4,208,128]{2,1,0:T(8,128)(2,1)} %shard_map.89), calls=%async_computation.6 | async-start | bytes 425984 | tf_op jit(solution)/shard_map/all_to_all | solution.py:256
  120.4 2.4 %shard_map.87 = bf16[4,208,128]{2,1,0:T(8,128)(2,1)S(1)} custom-call(s32[1]{0:T(128)} %bitcast.me_ref, bf16[4,384,128]{2,1,0:T(8,128)(2,1)S(1)} %pad_maximum_fusion.q_ref, bf16[1536,256]{1,0:T(8,128)(2,1)S(1)} %bitcast.16, f32[4,384,256]{2,1,0:T(8,128)S(1)} %shard_map.86.total_ref), custom_call_target="tpu_custom_call" | custom-call | flops 603979776 | bytes 786432 | tf_op jit(solution)/shard_map/pallas_call | solution.py:187
  122.8 0.7 copy-done.2
  123.5 2.8 %all-to-all-done.6.partial_ref = bf16[4,208,128]{2,1,0:T(8,128)(2,1)} async-done(((bf16[4,208,128]{2,1,0:T(8,128)(2,1)}), bf16[4,208,128]{2,1,0:T(8,128)(2,1)}, u32[]{:S(2)}, u32[]{:S(2)}) %all-to-all-start.6) | async-done | bytes 213024 | tf_op jit(solution)/shard_map/all_to_all | solution.py:256
  126.3 3.9 %all-to-all-start.4 = ((bf16[4,208,128]{2,1,0:T(8,128)(2,1)}), bf16[4,208,128]{2,1,0:T(8,128)(2,1)S(1)}, u32[]{:S(2)}, u32[]{:S(2)}) async-start(bf16[4,208,128]{2,1,0:T(8,128)(2,1)} %copy-done.2), calls=%async_computation.4 | async-start | bytes 425984 | tf_op jit(solution)/shard_map/all_to_all | solution.py:256
  130.2 2.3 %shard_map.90 = (bf16[96,3072]{1,0:T(8,128)(2,1)S(1)}, bf16[96,3072]{1,0:T(8,128)(2,1)S(1)}) custom-call(bf16[4,208,128]{2,1,0:T(8,128)(2,1)} %all-to-all-done.6.partial_ref, bf16[128,3072]{1,0:T(8,128)(2,1)S(1)} %copy-done.1), custom_call_target="tpu_custom_call" | custom-call | flops 150994944 | bytes 1179648 | tf_op jit(solution)/shard_map/pallas_call | solution.py:228
  132.5 1.9 %collective-permute-start.9 = (bf16[96,3072]{1,0:T(8,128)(2,1)S(1)}, bf16[96,3072]{1,0:T(8,128)(2,1)S(1)}, u32[]{:S(2)}, u32[]{:S(2)}) collective-permute-start(bf16[96,3072]{1,0:T(8,128)(2,1)S(1)} %get-tuple-element.20), channel_id=1, source_target_pairs={{0,32},{32,0},{1,33},{33,1},{2,34},{34,2},{3,35},{35,3},{4,36},{36... | collective-permute-start | bytes 1769480 | tf_op jit(solution)/shard_map/ppermute | solution.py:25
  134.5 1.6 all-to-all-done.4.partial_ref
  136.1 2.3 %shard_map.88 = (bf16[96,3072]{1,0:T(8,128)(2,1)S(1)}, bf16[96,3072]{1,0:T(8,128)(2,1)}) custom-call(bf16[4,208,128]{2,1,0:T(8,128)(2,1)S(1)} %all-to-all-done.4.partial_ref, bf16[128,3072]{1,0:T(8,128)(2,1)S(1)} %copy-done.1), custom_call_target="tpu_custom_call" | custom-call | flops 150994944 | bytes 1179648 | tf_op jit(solution)/shard_map/pallas_call | solution.py:228
  138.4 1.9 %collective-permute-start.8 = (bf16[96,3072]{1,0:T(8,128)(2,1)}, bf16[96,3072]{1,0:T(8,128)(2,1)S(1)}, u32[]{:S(2)}, u32[]{:S(2)}) collective-permute-start(bf16[96,3072]{1,0:T(8,128)(2,1)} %get-tuple-element.18), channel_id=1, source_target_pairs={{0,32},{32,0},{1,33},{33,1},{2,34},{34,2},{3,35},{35,3},{4,36},{36... | collective-permute-start | bytes 1769480 | tf_op jit(solution)/shard_map/ppermute | solution.py:25
  140.3 0.0 collective-permute-done.9
  140.3 1.0 add_convert_fusion
  141.3 4.9 %all-to-all-start.7 = ((bf16[4,24,3072]{2,1,0:T(8,128)(2,1)}), bf16[4,24,3072]{2,1,0:T(8,128)(2,1)S(1)}, u32[]{:S(2)}, u32[]{:S(2)}) async-start(bf16[4,24,3072]{2,1,0:T(8,128)(2,1)} %bitcast.14), calls=%async_computation.7 | async-start | bytes 1179648 | tf_op jit(solution)/shard_map/all_to_all | solution.py:258
  146.2 0.0 collective-permute-done.8
  146.2 1.0 add_convert_fusion.1
  147.2 8.7 %all-to-all-done.7 = bf16[4,24,3072]{2,1,0:T(8,128)(2,1)S(1)} async-done(((bf16[4,24,3072]{2,1,0:T(8,128)(2,1)}), bf16[4,24,3072]{2,1,0:T(8,128)(2,1)S(1)}, u32[]{:S(2)}, u32[]{:S(2)}) %all-to-all-start.7) | async-done | bytes 589856 | tf_op jit(solution)/shard_map/all_to_all | solution.py:258
  155.8 5.0 %all-to-all-start.5 = ((bf16[4,24,3072]{2,1,0:T(8,128)(2,1)}), bf16[4,24,3072]{2,1,0:T(8,128)(2,1)S(1)}, u32[]{:S(2)}, u32[]{:S(2)}) async-start(bf16[4,24,3072]{2,1,0:T(8,128)(2,1)} %bitcast.13), calls=%async_computation.5 | async-start | bytes 1179648 | tf_op jit(solution)/shard_map/all_to_all | solution.py:258
  160.9 0.1 reduce_sum.22
  161.0 13.3 %collective-permute-start.10 = (bf16[24,3072]{1,0:T(8,128)(2,1)S(1)}, bf16[24,3072]{1,0:T(8,128)(2,1)S(1)}, u32[]{:S(2)}, u32[]{:S(2)}) collective-permute-start(bf16[24,3072]{1,0:T(8,128)(2,1)S(1)} %reduce_sum.22), channel_id=1, source_target_pairs={{0,64},{64,0},{1,65},{65,1},{2,66},{66,2},{3,67},{67,3},{4,68},{68... | collective-permute-start | bytes 442376 | tf_op jit(solution)/shard_map/ppermute | solution.py:25
  174.3 0.0 all-to-all-done.5
  174.3 0.1 convert_reduce_fusion
  174.4 12.8 %collective-permute-done.10 = bf16[24,3072]{1,0:T(8,128)(2,1)S(1)} collective-permute-done((bf16[24,3072]{1,0:T(8,128)(2,1)S(1)}, bf16[24,3072]{1,0:T(8,128)(2,1)S(1)}, u32[]{:S(2)}, u32[]{:S(2)}) %collective-permute-start.10) | collective-permute-done | bytes 147488 | tf_op jit(solution)/shard_map/ppermute | solution.py:25
  187.2 0.7 multiply_convert_fusion
  (24 shorter events, 0.1 us)
Async XLA Ops:
  0.0 0.9 copy-start.3
  0.9 0.7 copy-start.5
  1.6 0.7 copy-start.7
  2.3 6.2 %copy-start.4 = (bf16[24,3072]{1,0:T(8,128)(2,1)S(1)}, bf16[24,3072]{1,0:T(8,128)(2,1)}, u32[]{:S(2)}) copy-start(bf16[24,3072]{1,0:T(8,128)(2,1)} %tokens_ref.1) | copy-start | bytes 442372
  2.3 33.5 %copy-start.6 = (f32[3072]{0:T(1024)S(1)}, f32[3072]{0:T(1024)}, u32[]{:S(2)}) copy-start(f32[3072]{0:T(1024)} %param.9) | copy-start | bytes 36868
  2.3 33.5 %copy-start.8 = (f32[3072]{0:T(1024)S(1)}, f32[3072]{0:T(1024)}, u32[]{:S(2)}) copy-start(f32[3072]{0:T(1024)} %param.10) | copy-start | bytes 36868
  3.5 47.0 %copy-start = (bf16[3,3072,128]{2,1,0:T(8,128)(2,1)S(1)}, bf16[3,3072,128]{2,1,0:T(8,128)(2,1)}, u32[]{:S(2)}) copy-start(bf16[3,3072,128]{2,1,0:T(8,128)(2,1)} %refs_2_.3) | copy-start | bytes 7077892
  3.5 20.0 %all-to-all-start = ((bf16[4,24,3072]{2,1,0:T(8,128)(2,1)}), bf16[4,24,3072]{2,1,0:T(8,128)(2,1)S(1)}, u32[]{:S(2)}, u32[]{:S(2)}) async-start(bf16[4,24,3072]{2,1,0:T(8,128)(2,1)} %broadcast_in_dim.18), calls=%async_computation | async-start | bytes 1179648 | tf_op jit(solution)/shard_map/all_to_all | solution.py:34
  8.5 41.9 %copy-start.11 = (f32[128]{0:T(128)S(1)}, f32[128]{0:T(128)}, u32[]{:S(2)}) copy-start(f32[128]{0:T(128)} %param.12) | copy-start | bytes 1540
  8.5 41.9 %copy-start.12 = (f32[128]{0:T(128)S(1)}, f32[128]{0:T(128)}, u32[]{:S(2)}) copy-start(f32[128]{0:T(128)} %param.13) | copy-start | bytes 1540
  8.5 27.3 %collective-permute-start.1 = (bf16[24,3072]{1,0:T(8,128)(2,1)S(1)}, bf16[24,3072]{1,0:T(8,128)(2,1)S(1)}, u32[]{:S(2)}, u32[]{:S(2)}) collective-permute-start(bf16[24,3072]{1,0:T(8,128)(2,1)S(1)} %copy-done.4), channel_id=1, source_target_pairs={{0,64},{64,0},{1,65},{65,1},{2,66},{66,2},{3,67},{67,3},{4,68},{68... | collective-permute-start | bytes 442376 | tf_op jit(solution)/shard_map/ppermute | solution.py:25
  23.5 26.9 %collective-permute-start = (bf16[96,3072]{1,0:T(8,128)(2,1)S(1)}, bf16[96,3072]{1,0:T(8,128)(2,1)S(1)}, u32[]{:S(2)}, u32[]{:S(2)}) collective-permute-start(bf16[96,3072]{1,0:T(8,128)(2,1)S(1)} %bitcast.17), channel_id=1, source_target_pairs={{0,32},{32,0},{1,33},{33,1},{2,34},{34,2},{3,35},{35,3},{4,36},{36... | collective-permute-start | bytes 1769480 | tf_op jit(solution)/shard_map/ppermute | solution.py:25
  48.5 23.7 %collective-permute-start.2 = (bf16[96,3072]{1,0:T(8,128)(2,1)S(1)}, bf16[96,3072]{1,0:T(8,128)(2,1)}, u32[]{:S(2)}, u32[]{:S(2)}) collective-permute-start(bf16[96,3072]{1,0:T(8,128)(2,1)S(1)} %bitcast.19), channel_id=1, source_target_pairs={{0,32},{32,0},{1,33},{33,1},{2,34},{34,2},{3,35},{35,3},{4,36},{36... | collective-permute-start | bytes 1769480 | tf_op jit(solution)/shard_map/ppermute | solution.py:25
  52.2 14.2 %copy-start.9 = (bf16[192,128]{1,0:T(8,128)(2,1)}, bf16[192,128]{1,0:T(8,128)(2,1)S(1)}, u32[]{:S(2)}) copy-start(bf16[192,128]{1,0:T(8,128)(2,1)S(1)} %get-tuple-element.13) | copy-start | bytes 147460
  52.2 14.2 %collective-permute-start.7 = (bf16[192,256]{1,0:T(8,128)(2,1)S(1)}, bf16[192,256]{1,0:T(8,128)(2,1)S(1)}, u32[]{:S(2)}, u32[]{:S(2)}) collective-permute-start(bf16[192,256]{1,0:T(8,128)(2,1)S(1)} %get-tuple-element.16), channel_id=1, source_target_pairs={{0,16},{16,0},{1,17},{17,1},{2,18},{18,2},{3,19},{19,3},{4,20},{20... | collective-permute-start | bytes 294920 | tf_op jit(solution)/shard_map/ppermute | solution.py:25
  67.4 20.8 %all-to-all-start.3 = ((bf16[4,384,256]{2,1,0:T(8,128)(2,1)}), bf16[4,384,256]{2,1,0:T(8,128)(2,1)}, u32[]{:S(2)}, u32[]{:S(2)}) async-start(bf16[4,384,256]{2,1,0:T(8,128)(2,1)} %broadcast_in_dim.23), calls=%async_computation.3 | async-start | bytes 1572864 | tf_op jit(solution)/shard_map/all_to_all | solution.py:34
  75.3 12.9 %collective-permute-start.6 = (bf16[192,256]{1,0:T(8,128)(2,1)S(1)}, bf16[192,256]{1,0:T(8,128)(2,1)S(1)}, u32[]{:S(2)}, u32[]{:S(2)}) collective-permute-start(bf16[192,256]{1,0:T(8,128)(2,1)S(1)} %get-tuple-element.15), channel_id=1, source_target_pairs={{0,16},{16,0},{1,17},{17,1},{2,18},{18,2},{3,19},{19,3},{4,20},{20... | collective-permute-start | bytes 294920 | tf_op jit(solution)/shard_map/ppermute | solution.py:25
  88.2 5.8 %copy-start.10 = (bf16[192,128]{1,0:T(8,128)(2,1)S(1)}, bf16[192,128]{1,0:T(8,128)(2,1)}, u32[]{:S(2)}) copy-start(bf16[192,128]{1,0:T(8,128)(2,1)} %copy-done.9) | copy-start | bytes 147460
  89.1 22.2 %all-to-all-start.2 = ((bf16[4,384,256]{2,1,0:T(8,128)(2,1)}), bf16[4,384,256]{2,1,0:T(8,128)(2,1)S(1)}, u32[]{:S(2)}, u32[]{:S(2)}) async-start(bf16[4,384,256]{2,1,0:T(8,128)(2,1)} %broadcast_in_dim.22), calls=%async_computation.2 | async-start | bytes 1572864 | tf_op jit(solution)/shard_map/all_to_all | solution.py:34
  94.0 9.2 %collective-permute-start.5 = (bf16[384,128]{1,0:T(8,128)(2,1)S(1)}, bf16[384,128]{1,0:T(8,128)(2,1)S(1)}, u32[]{:S(2)}, u32[]{:S(2)}) collective-permute-start(bf16[384,128]{1,0:T(8,128)(2,1)S(1)} %constant_dynamic-update-slice_fusion), channel_id=1, source_target_pairs={{0,12},{4,8},{8,4},{12,0},{1,13},{5,9},{9,5},{13,1},{2,14},{6,10},... | collective-permute-start | bytes 294920 | tf_op jit(solution)/shard_map/ppermute | solution.py:29
  95.9 8.4 %collective-permute-start.4 = (bf16[384,128]{1,0:T(8,128)(2,1)S(1)}, bf16[384,128]{1,0:T(8,128)(2,1)S(1)}, u32[]{:S(2)}, u32[]{:S(2)}) collective-permute-start(bf16[384,128]{1,0:T(8,128)(2,1)S(1)} %constant_dynamic-update-slice_fusion), channel_id=1, source_target_pairs={{0,8},{4,12},{8,0},{12,4},{1,9},{5,13},{9,1},{13,5},{2,10},{6,14},... | collective-permute-start | bytes 294920 | tf_op jit(solution)/shard_map/ppermute | solution.py:29
  97.8 8.0 %collective-permute-start.3 = (bf16[384,128]{1,0:T(8,128)(2,1)S(1)}, bf16[384,128]{1,0:T(8,128)(2,1)S(1)}, u32[]{:S(2)}, u32[]{:S(2)}) collective-permute-start(bf16[384,128]{1,0:T(8,128)(2,1)S(1)} %constant_dynamic-update-slice_fusion), channel_id=1, source_target_pairs={{0,4},{4,0},{8,12},{12,8},{1,5},{5,1},{9,13},{13,9},{2,6},{6,2},{1... | collective-permute-start | bytes 294920 | tf_op jit(solution)/shard_map/ppermute | solution.py:29
  114.4 11.9 %all-to-all-start.6 = ((bf16[4,208,128]{2,1,0:T(8,128)(2,1)}), bf16[4,208,128]{2,1,0:T(8,128)(2,1)}, u32[]{:S(2)}, u32[]{:S(2)}) async-start(bf16[4,208,128]{2,1,0:T(8,128)(2,1)} %shard_map.89), calls=%async_computation.6 | async-start | bytes 425984 | tf_op jit(solution)/shard_map/all_to_all | solution.py:256
  120.4 9.8 %copy-start.1 = (bf16[128,3072]{1,0:T(8,128)(2,1)S(1)}, bf16[128,3072]{1,0:T(8,128)(2,1)}, u32[]{:S(2)}) copy-start(bf16[128,3072]{1,0:T(8,128)(2,1)} %weight_ref.3) | copy-start | bytes 2359300
  122.8 0.7 copy-start.2
  126.3 9.7 %all-to-all-start.4 = ((bf16[4,208,128]{2,1,0:T(8,128)(2,1)}), bf16[4,208,128]{2,1,0:T(8,128)(2,1)S(1)}, u32[]{:S(2)}, u32[]{:S(2)}) async-start(bf16[4,208,128]{2,1,0:T(8,128)(2,1)} %copy-done.2), calls=%async_computation.4 | async-start | bytes 425984 | tf_op jit(solution)/shard_map/all_to_all | solution.py:256
  132.5 7.8 %collective-permute-start.9 = (bf16[96,3072]{1,0:T(8,128)(2,1)S(1)}, bf16[96,3072]{1,0:T(8,128)(2,1)S(1)}, u32[]{:S(2)}, u32[]{:S(2)}) collective-permute-start(bf16[96,3072]{1,0:T(8,128)(2,1)S(1)} %get-tuple-element.20), channel_id=1, source_target_pairs={{0,32},{32,0},{1,33},{33,1},{2,34},{34,2},{3,35},{35,3},{4,36},{36... | collective-permute-start | bytes 1769480 | tf_op jit(solution)/shard_map/ppermute | solution.py:25
  138.4 7.8 %collective-permute-start.8 = (bf16[96,3072]{1,0:T(8,128)(2,1)}, bf16[96,3072]{1,0:T(8,128)(2,1)S(1)}, u32[]{:S(2)}, u32[]{:S(2)}) collective-permute-start(bf16[96,3072]{1,0:T(8,128)(2,1)} %get-tuple-element.18), channel_id=1, source_target_pairs={{0,32},{32,0},{1,33},{33,1},{2,34},{34,2},{3,35},{35,3},{4,36},{36... | collective-permute-start | bytes 1769480 | tf_op jit(solution)/shard_map/ppermute | solution.py:25
  141.3 14.6 %all-to-all-start.7 = ((bf16[4,24,3072]{2,1,0:T(8,128)(2,1)}), bf16[4,24,3072]{2,1,0:T(8,128)(2,1)S(1)}, u32[]{:S(2)}, u32[]{:S(2)}) async-start(bf16[4,24,3072]{2,1,0:T(8,128)(2,1)} %bitcast.14), calls=%async_computation.7 | async-start | bytes 1179648 | tf_op jit(solution)/shard_map/all_to_all | solution.py:258
  155.8 31.3 %copy-start.13 = (f32[3072]{0:T(1024)S(1)}, f32[3072]{0:T(1024)}, u32[]{:S(2)}) copy-start(f32[3072]{0:T(1024)} %param.15) | copy-start | bytes 36868
  155.8 18.4 %all-to-all-start.5 = ((bf16[4,24,3072]{2,1,0:T(8,128)(2,1)}), bf16[4,24,3072]{2,1,0:T(8,128)(2,1)S(1)}, u32[]{:S(2)}, u32[]{:S(2)}) async-start(bf16[4,24,3072]{2,1,0:T(8,128)(2,1)} %bitcast.13), calls=%async_computation.5 | async-start | bytes 1179648 | tf_op jit(solution)/shard_map/all_to_all | solution.py:258
  161.0 26.2 %collective-permute-start.10 = (bf16[24,3072]{1,0:T(8,128)(2,1)S(1)}, bf16[24,3072]{1,0:T(8,128)(2,1)S(1)}, u32[]{:S(2)}, u32[]{:S(2)}) collective-permute-start(bf16[24,3072]{1,0:T(8,128)(2,1)S(1)} %reduce_sum.22), channel_id=1, source_target_pairs={{0,64},{64,0},{1,65},{65,1},{2,66},{66,2},{3,67},{67,3},{4,68},{68... | collective-permute-start | bytes 442376 | tf_op jit(solution)/shard_map/ppermute | solution.py:25

commit v3 on v2

--- a/solution.py
+++ b/solution.py
@@ -11,7 +11,7 @@
 epsilon = 1e-06
 AXES = {"y": 4, "zh": 2, "core": 2, "za": 2, "zb": 2, "zc": 2, "x": 4}
 ALL = tuple(AXES)
-QUAD = ("zb", "zc")
+NEAR = ("zc", "x")
 F32 = jnp.float32
 BF16 = jnp.bfloat16
 MIB = 1 << 20
@@ -25,29 +25,27 @@
     return lax.ppermute(block, axis, [(0, 1), (1, 0)])
 
 
-def across(block, distance):
-    return lax.ppermute(block, QUAD, [(i, i ^ distance) for i in range(4)])
-
-
-def gather_all(block, axis, count):
-    copies = jnp.broadcast_to(block[None], (count, *block.shape))
-    return lax.all_to_all(copies, axis, 0, 0)
-
-
-def modulate_kernel(tokens_ref, shift_ref, scale_ref, out_ref):
-    widened = tokens_ref[...].astype(F32)
+def trade_halves(block):
+    return lax.ppermute(block, ("zh", "za"), [(i, i ^ 3) for i in range(4)])
+
+
+def modulate_kernel(near_ref, far_ref, shift_ref, scale_ref, out_ref):
+    widened = jnp.concatenate([near_ref[...], far_ref[...]], axis=0).astype(F32)
     center = widened - jnp.mean(widened, axis=-1, keepdims=True)
     spread = jnp.mean(center * center, axis=-1, keepdims=True)
     normed = center * lax.rsqrt(spread + epsilon)
-    out_ref[...] = (normed * scale_ref[...] + shift_ref[...]).astype(BF16)
-
-
-def modulate(tokens, shift, scale):
+    modulated = (normed * scale_ref[...] + shift_ref[...]).astype(BF16)
+    for i in range(out_ref.shape[0]):
+        out_ref[i] = modulated
+
+
+def modulate(near, far, shift, scale, copies):
+    rows, width = near.shape
     return pl.pallas_call(
         modulate_kernel,
-        out_shape=jax.ShapeDtypeStruct(tokens.shape, BF16),
+        out_shape=jax.ShapeDtypeStruct((copies, 2 * rows, width), BF16),
         compiler_params=params(8),
-    )(tokens, shift[None], scale[None])
+    )(near, far, shift[None], scale[None])
 
 
 def project_kernel(
@@ -70,12 +68,14 @@
             meansq = jnp.mean(part * part, axis=-1, keepdims=True)
             return part * lax.rsqrt(meansq + epsilon) * gain
 
-        q_ref[...] = normed(0, q_gain_ref[...] * (math.log2(math.e) / math.sqrt(HD))).astype(BF16)
+        queries = normed(0, q_gain_ref[...] * (math.log2(math.e) / math.sqrt(HD))).astype(BF16)
+        for i in range(q_ref.shape[0]):
+            q_ref[i] = queries
         kv_ref[:, :HD] = normed(1, k_gain_ref[...]).astype(BF16)
         kv_ref[:, HD:] = total[:, 2 * HD :].astype(BF16)
 
 
-def project(own, other, weight, q_gain, k_gain):
+def project(own, other, weight, q_gain, k_gain, copies):
     half, width = own.shape
     rows = 2 * half
     steps = 4
@@ -91,11 +91,11 @@
             pl.BlockSpec((1, HD), lambda i: (0, 0)),
         ],
         out_specs=[
-            pl.BlockSpec((rows, HD), lambda i: (0, 0)),
+            pl.BlockSpec((copies, rows, HD), lambda i: (0, 0, 0)),
             pl.BlockSpec((rows, 2 * HD), lambda i: (0, 0)),
         ],
         out_shape=[
-            jax.ShapeDtypeStruct((rows, HD), BF16),
+            jax.ShapeDtypeStruct((copies, rows, HD), BF16),
             jax.ShapeDtypeStruct((rows, 2 * HD), BF16),
         ],
         scratch_shapes=[pltpu.VMEM((rows, 3 * HD), F32)],
@@ -119,7 +119,7 @@
 
 
 def add_keys(queries, kv_ref, total):
-    step = 512
+    step = 384
     ones = jnp.ones((step, HD), BF16)
     for at in range(0, kv_ref.shape[0], step):
         scores = lax.dot_general(
@@ -139,7 +139,7 @@
     total_ref[0] = add_keys(q_ref[0], kv_ref, None)
 
 
-def attend_last_kernel(me_ref, q_ref, kv_ref, total_ref, out_ref):
+def attend_last_kernel(q_ref, kv_ref, total_ref, out_ref):
     rows = q_ref.shape[1]
     total = add_keys(q_ref[0], kv_ref, total_ref[0])
     out_ref[0, :rows] = total[:, :HD].astype(BF16)
@@ -180,41 +180,39 @@
     )(queries, keyval)
 
 
-def attend_last(me, queries, keyval, total, part):
+def attend_last(queries, keyval, total):
     blocks, rows, _ = queries.shape
-    rows //= 2
     keys = keyval.shape[0]
     return pl.pallas_call(
         attend_last_kernel,
-        grid_spec=pltpu.PrefetchScalarGridSpec(
-            num_scalar_prefetch=1,
-            grid=(blocks,),
-            in_specs=[
-                pl.BlockSpec((1, rows, HD), lambda i, me: (i ^ me[0], part, 0)),
-                pl.BlockSpec((keys, 2 * HD), lambda i, me: (0, 0)),
-                pl.BlockSpec((1, rows, 2 * HD), lambda i, me: (i ^ me[0], part, 0)),
-            ],
-            out_specs=pl.BlockSpec((1, rows + TAIL, HD), lambda i, me: (i, 0, 0)),
-        ),
+        grid=(blocks,),
+        in_specs=[
+            pl.BlockSpec((1, rows, HD), lambda i: (i, 0, 0)),
+            pl.BlockSpec((keys, 2 * HD), lambda i: (0, 0)),
+            pl.BlockSpec((1, rows, 2 * HD), lambda i: (i, 0, 0)),
+        ],
+        out_specs=pl.BlockSpec((1, rows + TAIL, HD), lambda i: (i, 0, 0)),
         out_shape=jax.ShapeDtypeStruct((blocks, rows + TAIL, HD), BF16),
         compiler_params=params(24),
         cost_estimate=attend_cost(blocks, rows, keys),
-    )(me, queries, keyval, total)
-
-
-def combine_kernel(partial_ref, weight_ref, own_ref, other_ref):
-    rows = partial_ref.shape[1] - TAIL
-    summed = jnp.sum(partial_ref[...].astype(F32), axis=0)
-    blocks = row_blocks(rows)
-    attended = []
-    for j, (at, size) in enumerate(blocks):
-        low = rows + len(blocks) + j
-        row = summed[rows + j : rows + j + 1] + summed[low : low + 1]
-        square = jnp.broadcast_to(row, (size, HD))
-        column = jnp.sum(jnp.where(diagonal(size), square, 0.0), axis=1, keepdims=True)
-        attended.append((summed[at : at + size] / column).astype(BF16))
-    attended = jnp.concatenate(attended, axis=0)
-    mixed = jnp.dot(attended, weight_ref[...], preferred_element_type=F32).astype(BF16)
+    )(queries, keyval, total)
+
+
+def combine_kernel(partial_ref, weight_ref, own_ref, other_ref, attended):
+    rows = attended.shape[0]
+
+    @pl.when(pl.program_id(0) == 0)
+    def _():
+        summed = jnp.sum(partial_ref[...].astype(F32), axis=0)
+        blocks = row_blocks(rows)
+        for j, (at, size) in enumerate(blocks):
+            low = rows + len(blocks) + j
+            row = summed[rows + j : rows + j + 1] + summed[low : low + 1]
+            square = jnp.broadcast_to(row, (size, HD))
+            column = jnp.sum(jnp.where(diagonal(size), square, 0.0), axis=1, keepdims=True)
+            attended[at : at + size] = (summed[at : at + size] / column).astype(BF16)
+
+    mixed = jnp.dot(attended[...], weight_ref[...], preferred_element_type=F32).astype(BF16)
     half = rows // 2
     own_ref[...] = mixed[:half]
     other_ref[...] = mixed[half:]
@@ -234,6 +232,7 @@
         ],
         out_specs=[pl.BlockSpec((rows // 2, width // steps), lambda i: (0, i))] * 2,
         out_shape=[half, half],
+        scratch_shapes=[pltpu.VMEM((rows, HD), BF16)],
         compiler_params=params(16),
         cost_estimate=pl.CostEstimate(
             flops=2 * rows * width * HD, bytes_accessed=2 * rows * width, transcendentals=0
@@ -242,35 +241,21 @@
 
 
 def local(tokens, mod_shift, mod_scale, qkv_weight, q_gain, k_gain, out_weight, out_gate):
-    width = tokens.shape[1]
-
-    def spread(part):
-        own = gather_all(modulate(part, mod_shift, mod_scale), "y", 4).reshape(-1, width)
-        return project(own, swap(own, "core"), qkv_weight, q_gain, k_gain)
-
-    def share(keyval):
-        keyval = jnp.concatenate([keyval, swap(keyval, "za")], axis=0)
-        return gather_all(keyval, "x", 4).reshape(-1, 2 * HD)
-
-    def collect(partial):
-        own, other = combine(lax.all_to_all(partial, QUAD, 0, 0), out_weight)
-        summed = (own.astype(F32) + swap(other, "core").astype(F32)).astype(BF16)
-        summed = lax.all_to_all(summed.reshape(4, -1, width), "y", 0, 0).astype(F32)
-        return jnp.sum(summed, axis=0)
-
-    far = swap(tokens, "zh")
-    near_q, near_kv = spread(tokens)
-    far_q, far_kv = spread(far)
-    near_kv = share(near_kv)
-    queries = jnp.concatenate([near_q, far_q], axis=0)
-    queries = jnp.stack([queries] + [across(queries, i) for i in (1, 2, 3)])
-    far_kv = share(far_kv)
-    me = lax.axis_index(QUAD).astype(jnp.int32).reshape(1)
-    total = attend_first(queries, near_kv)
-    far_sum = collect(attend_last(me, queries, far_kv, total, 1))
-    near_sum = collect(attend_last(me, queries, far_kv, total, 0))
-    arrived = swap(far_sum.astype(BF16), "zh").astype(F32)
-    return ((near_sum + arrived) * out_gate).astype(BF16)
+    rows, width = tokens.shape
+    far = trade_halves(tokens)
+    own = lax.all_to_all(modulate(tokens, far, mod_shift, mod_scale, 4), "y", 0, 0)
+    own = own.reshape(-1, width)
+    queries, keyval = project(own, swap(own, "core"), qkv_weight, q_gain, k_gain, 8)
+    queries = lax.all_to_all(queries, NEAR, 0, 0)
+    first = jnp.concatenate([keyval, swap(keyval, "za")], axis=0)
+    last = swap(first, "zb")
+    partial = attend_last(queries, last, attend_first(queries, first))
+    own, other = combine(lax.all_to_all(partial, NEAR, 0, 0), out_weight)
+    summed = (own.astype(F32) + swap(other, "core").astype(F32)).astype(BF16)
+    summed = lax.all_to_all(summed.reshape(4, -1, width), "y", 0, 0).astype(F32)
+    summed = jnp.sum(summed, axis=0)
+    arrived = trade_halves(summed[rows:].astype(BF16)).astype(F32)
+    return ((summed[:rows] + arrived) * out_gate).astype(BF16)
 
 
 def solution(mesh):

time: 189 us -> 178 us (0.942)
  the two profiles are of different devices: /device:TPU:42 before, /device:TPU:1 now
where the time goes in v3:
time: 178 us
  waiting for transfers between devices  59.1 us (33%)
  blocking collectives  53.3 us (30%)
  starting transfers between devices  45.4 us (26%)
  Pallas kernels  16.1 us (9%)
  local copies, waits for them, and re-layouts  2.4 us (1%)
    ppermute x4, waiting for transfers between devices, swap(): return lax.ppermute(block, axis, [(0, 1), (1, 0)])  33.2 us
    ppermute x2, waiting for transfers between devices, trade_halves(): return lax.ppermute(block, ('zh', 'za'), [(i, i ^ 3) for i in range(4)])  25.9 us
    ppermute x2, starting transfers between devices, trade_halves(): return lax.ppermute(block, ('zh', 'za'), [(i, i ^ 3) for i in range(4)])  21.5 us
    ppermute x4, starting transfers between devices, swap(): return lax.ppermute(block, axis, [(0, 1), (1, 0)])  19.9 us
    all_to_all x1, blocking collectives, local(): lax.all_to_all(modulate(tokens, far, mod_shift, mod_scale, 4), 'y', 0, 0)  19.1 us
    all_to_all x1, blocking collectives, local(): summed = lax.all_to_all(summed.reshape(4, -1, width), 'y', 0, 0).astype(F32)  18.7 us
    all_to_all x1, blocking collectives, local(): own, other = combine(lax.all_to_all(partial, NEAR, 0, 0), out_weight)  15.5 us
    pallas_call x1, Pallas kernels, attend_last(): pl.pallas_call(attend_last_kernel, grid=(blocks,), in_specs=[pl.BlockSpec...  5.93 us
  transfers between devices with their start and end apart: 7, of which 6 were waited for; matrix products, arithmetic and copies ran while one was open for 0% of the time, Pallas kernels for 3%

profile of v3, /device:TPU:1, one launch (start us, length us, event | category | flops | bytes accessed | tf_op | source)
XLA Modules:
  0.0 177.7 jit_solution(3380071734710377817)
XLA Ops:
  0.0 13.3 %collective-permute-start = (bf16[24,3072]{1,0:T(8,128)(2,1)}, bf16[24,3072]{1,0:T(8,128)(2,1)S(1)}, u32[]{:S(2)}, u32[]{:S(2)}) collective-permute-start(bf16[24,3072]{1,0:T(8,128)(2,1)} %near_ref.1), channel_id=1, source_target_pairs={{0,80},{16,64},{64,16},{80,0},{1,81},{17,65},{65,17},{81,1},{2,82}... | collective-permute-start | bytes 442376 | tf_op jit(solution)/shard_map/ppermute | solution.py:29
  13.3 12.9 %collective-permute-done.far_ref = bf16[24,3072]{1,0:T(8,128)(2,1)S(1)} collective-permute-done((bf16[24,3072]{1,0:T(8,128)(2,1)}, bf16[24,3072]{1,0:T(8,128)(2,1)S(1)}, u32[]{:S(2)}, u32[]{:S(2)}) %collective-permute-start) | collective-permute-done | bytes 147488 | tf_op jit(solution)/shard_map/ppermute | solution.py:29
  26.2 0.0 copy-start.2
  26.2 0.9 copy-done.2
  27.1 0.0 copy-start.3
  27.1 0.7 copy-done.3
  27.8 0.0 copy-start.4
  27.8 0.7 copy-done.4
  28.5 0.4 shard_map.82
  28.9 0.0 copy-start
  28.9 0.0 copy-start.5
  28.9 0.0 copy-start.6
  28.9 19.1 %all_to_all.20 = bf16[4,48,3072]{2,1,0:T(8,128)(2,1)S(1)} all-to-all(bf16[4,48,3072]{2,1,0:T(8,128)(2,1)S(1)} %shard_map.82), channel_id=1, replica_groups=mesh['y'=4,'zh'=2,'core'=2,'za'=2,'zb'=2,'zc'=2,'x'=4] {'y'}, dimensions={0} | all-to-all | bytes 2359296 | tf_op jit(solution)/shard_map/all_to_all | solution.py:246
  48.0 4.4 %collective-permute-start.1 = (bf16[192,3072]{1,0:T(8,128)(2,1)S(1)}, bf16[192,3072]{1,0:T(8,128)(2,1)S(1)}, u32[]{:S(2)}, u32[]{:S(2)}) collective-permute-start(bf16[192,3072]{1,0:T(8,128)(2,1)S(1)} %bitcast.6), channel_id=1, source_target_pairs={{0,32},{32,0},{1,33},{33,1},{2,34},{34,2},{3,35},{35,3},{4,36},{36... | collective-permute-start | bytes 3538952 | tf_op jit(solution)/shard_map/ppermute | solution.py:25
  52.4 2.5 %collective-permute-done.1.refs_1_ = bf16[192,3072]{1,0:T(8,128)(2,1)S(1)} collective-permute-done((bf16[192,3072]{1,0:T(8,128)(2,1)S(1)}, bf16[192,3072]{1,0:T(8,128)(2,1)S(1)}, u32[]{:S(2)}, u32[]{:S(2)}) %collective-permute-start.1) | collective-permute-done | bytes 1179680 | tf_op jit(solution)/shard_map/ppermute | solution.py:25
  54.8 0.0 copy-done
  54.8 0.0 copy-done.5
  54.8 0.0 copy-done.6
  54.8 3.4 %shard_map.83 = (bf16[8,384,128]{2,1,0:T(8,128)(2,1)}, bf16[384,256]{1,0:T(8,128)(2,1)S(1)}) custom-call(bf16[192,3072]{1,0:T(8,128)(2,1)S(1)} %bitcast.7, bf16[192,3072]{1,0:T(8,128)(2,1)S(1)} %collective-permute-done.1.refs_1_, bf16[3,3072,128]{2,1,0:T(8,128)(2,1)S(1)} %copy-done, f32[1,128]{1,0:T(1,128)S(1)} %bitcast.10, f32[1,128]{1,0:T(1,128)S(1)} %bitcast.11), custom_call_target="tpu_custom_call" | custom-call | flops 905969664 | bytes 2359296 | tf_op jit(solution)/shard_map/pallas_call | solution.py:83
  58.3 4.0 %all-to-all-start.1 = ((bf16[8,384,128]{2,1,0:T(8,128)(2,1)}), bf16[8,384,128]{2,1,0:T(8,128)(2,1)S(1)}, u32[]{:S(2)}, u32[]{:S(2)}) async-start(bf16[8,384,128]{2,1,0:T(8,128)(2,1)} %get-tuple-element.9), calls=%async_computation.1 | async-start | bytes 1572864 | tf_op jit(solution)/shard_map/all_to_all | solution.py:249
  62.3 5.8 %collective-permute-start.2 = (bf16[384,256]{1,0:T(8,128)(2,1)S(1)}, bf16[384,256]{1,0:T(8,128)(2,1)S(1)}, u32[]{:S(2)}, u32[]{:S(2)}) collective-permute-start(bf16[384,256]{1,0:T(8,128)(2,1)S(1)} %get-tuple-element.10), channel_id=1, source_target_pairs={{0,16},{16,0},{1,17},{17,1},{2,18},{18,2},{3,19},{19,3},{4,20},{20... | collective-permute-start | bytes 589832 | tf_op jit(solution)/shard_map/ppermute | solution.py:25
  68.2 14.2 %collective-permute-done.2 = bf16[384,256]{1,0:T(8,128)(2,1)S(1)} collective-permute-done((bf16[384,256]{1,0:T(8,128)(2,1)S(1)}, bf16[384,256]{1,0:T(8,128)(2,1)S(1)}, u32[]{:S(2)}, u32[]{:S(2)}) %collective-permute-start.2) | collective-permute-done | bytes 196640 | tf_op jit(solution)/shard_map/ppermute | solution.py:25
  82.3 5.3 %collective-permute-start.3 = (bf16[768,256]{1,0:T(8,128)(2,1)S(1)}, bf16[768,256]{1,0:T(8,128)(2,1)S(1)}, u32[]{:S(2)}, u32[]{:S(2)}) collective-permute-start(bf16[768,256]{1,0:T(8,128)(2,1)S(1)} %constant_dynamic-update-slice_fusion.kv_ref), channel_id=1, source_target_pairs={{0,8},{8,0},{1,9},{9,1},{2,10},{10,2},{3,11},{11,3},{4,12},{12,4},... | collective-permute-start | bytes 1179656 | tf_op jit(solution)/shard_map/ppermute | solution.py:25
  87.6 0.0 all-to-all-done.1.q_ref
  87.6 4.8 %shard_map.84.total_ref = f32[8,384,256]{2,1,0:T(8,128)S(1)} custom-call(bf16[8,384,128]{2,1,0:T(8,128)(2,1)S(1)} %all-to-all-done.1.q_ref, bf16[768,256]{1,0:T(8,128)(2,1)S(1)} %constant_dynamic-update-slice_fusion.kv_ref), custom_call_target="tpu_custom_call" | custom-call | flops 1207959552 | bytes 393216 | tf_op jit(solution)/shard_map/pallas_call | solution.py:169
  92.5 14.1 %collective-permute-done.3.kv_ref = bf16[768,256]{1,0:T(8,128)(2,1)S(1)} collective-permute-done((bf16[768,256]{1,0:T(8,128)(2,1)S(1)}, bf16[768,256]{1,0:T(8,128)(2,1)S(1)}, u32[]{:S(2)}, u32[]{:S(2)}) %collective-permute-start.3) | collective-permute-done | bytes 393248 | tf_op jit(solution)/shard_map/ppermute | solution.py:25
  106.6 5.9 %shard_map.85 = bf16[8,400,128]{2,1,0:T(8,128)(2,1)S(1)} custom-call(bf16[8,384,128]{2,1,0:T(8,128)(2,1)S(1)} %all-to-all-done.1.q_ref, bf16[768,256]{1,0:T(8,128)(2,1)S(1)} %collective-permute-done.3.kv_ref, f32[8,384,256]{2,1,0:T(8,128)S(1)} %shard_map.84.total_ref), custom_call_target="tpu_custom_call" | custom-call | flops 1207959552 | bytes 393216 | tf_op jit(solution)/shard_map/pallas_call | solution.py:186
  112.5 0.0 copy-start.1
  112.5 15.5 %all_to_all.21.partial_ref = bf16[8,400,128]{2,1,0:T(8,128)(2,1)S(1)} all-to-all(bf16[8,400,128]{2,1,0:T(8,128)(2,1)S(1)} %shard_map.85), channel_id=1, replica_groups=mesh['y'=4,'zh'=2,'core'=2,'za'=2,'zb'=2,'zc'=2,'x'=4] {'zc','x'}, dimensions={0} | all-to-all | bytes 1638400 | tf_op jit(solution)/shard_map/all_to_all | solution.py:253
  128.0 0.0 copy-done.1
  128.0 1.6 shard_map.86
  129.6 4.4 %collective-permute-start.4 = (bf16[192,3072]{1,0:T(8,128)(2,1)S(1)}, bf16[192,3072]{1,0:T(8,128)(2,1)S(1)}, u32[]{:S(2)}, u32[]{:S(2)}) collective-permute-start(bf16[192,3072]{1,0:T(8,128)(2,1)S(1)} %get-tuple-element.12), channel_id=1, source_target_pairs={{0,32},{32,0},{1,33},{33,1},{2,34},{34,2},{3,35},{35,3},{4,36},{36... | collective-permute-start | bytes 3538952 | tf_op jit(solution)/shard_map/ppermute | solution.py:25
  134.0 2.5 %collective-permute-done.4 = bf16[192,3072]{1,0:T(8,128)(2,1)S(1)} collective-permute-done((bf16[192,3072]{1,0:T(8,128)(2,1)S(1)}, bf16[192,3072]{1,0:T(8,128)(2,1)S(1)}, u32[]{:S(2)}, u32[]{:S(2)}) %collective-permute-start.4) | collective-permute-done | bytes 1179680 | tf_op jit(solution)/shard_map/ppermute | solution.py:25
  136.5 0.4 add_convert_fusion
  136.9 18.7 %all_to_all.22 = bf16[4,48,3072]{2,1,0:T(8,128)(2,1)S(1)} all-to-all(bf16[4,48,3072]{2,1,0:T(8,128)(2,1)S(1)} %bitcast.12), channel_id=1, replica_groups=mesh['y'=4,'zh'=2,'core'=2,'za'=2,'zb'=2,'zc'=2,'x'=4] {'y'}, dimensions={0} | all-to-all | bytes 2359296 | tf_op jit(solution)/shard_map/all_to_all | solution.py:255
  155.6 0.0 copy-start.7
  155.6 0.2 convert_reduce_fusion
  155.8 8.2 %collective-permute-start.5 = (bf16[24,3072]{1,0:T(8,128)(2,1)S(1)}, bf16[24,3072]{1,0:T(8,128)(2,1)S(1)}, u32[]{:S(2)}, u32[]{:S(2)}) collective-permute-start(bf16[24,3072]{1,0:T(8,128)(2,1)S(1)} %slice.17), channel_id=1, source_target_pairs={{0,80},{16,64},{64,16},{80,0},{1,81},{17,65},{65,17},{81,1},{2,82}... | collective-permute-start | bytes 442376 | tf_op jit(solution)/shard_map/ppermute | solution.py:29
  164.0 13.0 %collective-permute-done.5 = bf16[24,3072]{1,0:T(8,128)(2,1)S(1)} collective-permute-done((bf16[24,3072]{1,0:T(8,128)(2,1)S(1)}, bf16[24,3072]{1,0:T(8,128)(2,1)S(1)}, u32[]{:S(2)}, u32[]{:S(2)}) %collective-permute-start.5) | collective-permute-done | bytes 147488 | tf_op jit(solution)/shard_map/ppermute | solution.py:29
  177.0 0.0 copy-done.7
  177.0 0.7 fusion.1
  (3 shorter events, 0.0 us)
Async XLA Ops:
  0.0 26.2 %collective-permute-start = (bf16[24,3072]{1,0:T(8,128)(2,1)}, bf16[24,3072]{1,0:T(8,128)(2,1)S(1)}, u32[]{:S(2)}, u32[]{:S(2)}) collective-permute-start(bf16[24,3072]{1,0:T(8,128)(2,1)} %near_ref.1), channel_id=1, source_target_pairs={{0,80},{16,64},{64,16},{80,0},{1,81},{17,65},{65,17},{81,1},{2,82}... | collective-permute-start | bytes 442376 | tf_op jit(solution)/shard_map/ppermute | solution.py:29
  26.2 0.9 copy-start.2
  27.1 0.7 copy-start.3
  27.8 0.7 copy-start.4
  28.9 26.0 %copy-start = (bf16[3,3072,128]{2,1,0:T(8,128)(2,1)S(1)}, bf16[3,3072,128]{2,1,0:T(8,128)(2,1)}, u32[]{:S(2)}) copy-start(bf16[3,3072,128]{2,1,0:T(8,128)(2,1)} %refs_2_.1) | copy-start | bytes 7077892
  28.9 26.0 %copy-start.5 = (f32[128]{0:T(128)S(1)}, f32[128]{0:T(128)}, u32[]{:S(2)}) copy-start(f32[128]{0:T(128)} %param.12) | copy-start | bytes 1540
  28.9 25.9 %copy-start.6 = (f32[128]{0:T(128)S(1)}, f32[128]{0:T(128)}, u32[]{:S(2)}) copy-start(f32[128]{0:T(128)} %param.13) | copy-start | bytes 1540
  48.0 6.8 %collective-permute-start.1 = (bf16[192,3072]{1,0:T(8,128)(2,1)S(1)}, bf16[192,3072]{1,0:T(8,128)(2,1)S(1)}, u32[]{:S(2)}, u32[]{:S(2)}) collective-permute-start(bf16[192,3072]{1,0:T(8,128)(2,1)S(1)} %bitcast.6), channel_id=1, source_target_pairs={{0,32},{32,0},{1,33},{33,1},{2,34},{34,2},{3,35},{35,3},{4,36},{36... | collective-permute-start | bytes 3538952 | tf_op jit(solution)/shard_map/ppermute | solution.py:25
  58.3 29.3 %all-to-all-start.1 = ((bf16[8,384,128]{2,1,0:T(8,128)(2,1)}), bf16[8,384,128]{2,1,0:T(8,128)(2,1)S(1)}, u32[]{:S(2)}, u32[]{:S(2)}) async-start(bf16[8,384,128]{2,1,0:T(8,128)(2,1)} %get-tuple-element.9), calls=%async_computation.1 | async-start | bytes 1572864 | tf_op jit(solution)/shard_map/all_to_all | solution.py:249
  62.3 20.0 %collective-permute-start.2 = (bf16[384,256]{1,0:T(8,128)(2,1)S(1)}, bf16[384,256]{1,0:T(8,128)(2,1)S(1)}, u32[]{:S(2)}, u32[]{:S(2)}) collective-permute-start(bf16[384,256]{1,0:T(8,128)(2,1)S(1)} %get-tuple-element.10), channel_id=1, source_target_pairs={{0,16},{16,0},{1,17},{17,1},{2,18},{18,2},{3,19},{19,3},{4,20},{20... | collective-permute-start | bytes 589832 | tf_op jit(solution)/shard_map/ppermute | solution.py:25
  82.3 24.2 %collective-permute-start.3 = (bf16[768,256]{1,0:T(8,128)(2,1)S(1)}, bf16[768,256]{1,0:T(8,128)(2,1)S(1)}, u32[]{:S(2)}, u32[]{:S(2)}) collective-permute-start(bf16[768,256]{1,0:T(8,128)(2,1)S(1)} %constant_dynamic-update-slice_fusion.kv_ref), channel_id=1, source_target_pairs={{0,8},{8,0},{1,9},{9,1},{2,10},{10,2},{3,11},{11,3},{4,12},{12,4},... | collective-permute-start | bytes 1179656 | tf_op jit(solution)/shard_map/ppermute | solution.py:25
  112.5 15.5 %copy-start.1 = (bf16[128,3072]{1,0:T(8,128)(2,1)S(1)}, bf16[128,3072]{1,0:T(8,128)(2,1)}, u32[]{:S(2)}) copy-start(bf16[128,3072]{1,0:T(8,128)(2,1)} %weight_ref.1) | copy-start | bytes 2359300
  129.6 6.9 %collective-permute-start.4 = (bf16[192,3072]{1,0:T(8,128)(2,1)S(1)}, bf16[192,3072]{1,0:T(8,128)(2,1)S(1)}, u32[]{:S(2)}, u32[]{:S(2)}) collective-permute-start(bf16[192,3072]{1,0:T(8,128)(2,1)S(1)} %get-tuple-element.12), channel_id=1, source_target_pairs={{0,32},{32,0},{1,33},{33,1},{2,34},{34,2},{3,35},{35,3},{4,36},{36... | collective-permute-start | bytes 3538952 | tf_op jit(solution)/shard_map/ppermute | solution.py:25
  155.6 21.5 %copy-start.7 = (f32[3072]{0:T(1024)S(1)}, f32[3072]{0:T(1024)}, u32[]{:S(2)}) copy-start(f32[3072]{0:T(1024)} %param.15) | copy-start | bytes 36868
  155.8 21.2 %collective-permute-start.5 = (bf16[24,3072]{1,0:T(8,128)(2,1)S(1)}, bf16[24,3072]{1,0:T(8,128)(2,1)S(1)}, u32[]{:S(2)}, u32[]{:S(2)}) collective-permute-start(bf16[24,3072]{1,0:T(8,128)(2,1)S(1)} %slice.17), channel_id=1, source_target_pairs={{0,80},{16,64},{64,16},{80,0},{1,81},{17,65},{65,17},{81,1},{2,82}... | collective-permute-start | bytes 442376 | tf_op jit(solution)/shard_map/ppermute | solution.py:29

commit v4 on v1

v4 whole, which is shorter than its diff:
```python
import math

import jax
import jax.numpy as jnp
from jax import lax
from jax.experimental import pallas as pl
from jax.experimental.pallas import tpu as pltpu
from jax.sharding import Mesh, PartitionSpec as P

HD = 128
epsilon = 1e-06
AXES = {"y": 4, "zh": 2, "core": 2, "za": 2, "zb": 2, "zc": 2, "x": 4}
ALL = tuple(AXES)
NEAR = ("zc", "x")
F32 = jnp.float32
BF16 = jnp.bfloat16
MIB = 1 << 20


def params(mib):
    return pltpu.CompilerParams(vmem_limit_bytes=mib * MIB)


def swap(block, axis):
    return lax.ppermute(block, axis, [(0, 1), (1, 0)])


def trade_halves(block):
    return lax.ppermute(block, ("zh", "za"), [(i, i ^ 3) for i in range(4)])


def normalize(tokens, shift, scale):
    widened = tokens.astype(F32)
    center = widened - jnp.mean(widened, axis=-1, keepdims=True)
    spread = jnp.mean(center * center, axis=-1, keepdims=True)
    normed = center * lax.rsqrt(spread + epsilon)
    return (normed * scale + shift).astype(BF16)


def modulate_near_kernel(tokens_ref, shift_ref, scale_ref, out_ref, pair_ref, tokens, sem):
    copies = [
        pltpu.make_async_copy(tokens_ref, tokens, sem.at[0]),
        pltpu.make_async_copy(shift_ref, pair_ref.at[0], sem.at[1]),
        pltpu.make_async_copy(scale_ref, pair_ref.at[1], sem.at[2]),
    ]
    for copy in copies:
        copy.start()
    for copy in copies:
        copy.wait()
    out_ref[...] = normalize(tokens[...], pair_ref[0], pair_ref[1])


def modulate_near(tokens, shift, scale):
    width = tokens.shape[1]
    return pl.pallas_call(
        modulate_near_kernel,
        in_specs=[pl.BlockSpec(memory_space=pltpu.HBM)] * 3,
        out_specs=[pl.BlockSpec(memory_space=pltpu.VMEM)] * 2,
        out_shape=[
            jax.ShapeDtypeStruct(tokens.shape, BF16),
            jax.ShapeDtypeStruct((2, 1, width), F32),
        ],
        scratch_shapes=[pltpu.VMEM(tokens.shape, BF16), pltpu.SemaphoreType.DMA((3,))],
        compiler_params=params(60),
    )(tokens, shift[None], scale[None])


def modulate_far_kernel(tokens_ref, pair_ref, out_ref):
    out_ref[...] = normalize(tokens_ref[...], pair_ref[0], pair_ref[1])


def modulate_far(tokens, pair):
    return pl.pallas_call(
        modulate_far_kernel,
        out_shape=jax.ShapeDtypeStruct(tokens.shape, BF16),
        compiler_params=params(8),
    )(tokens, pair)


STEPS = 4


def project_kernel(tokens_refs, weight_ref, q_gain_ref, k_gain_ref, q_ref, kv_ref, *scratch):
    total, weights, gains, weight_sem, gain_sem = scratch
    step = pl.program_id(0)
    depth = tokens_refs[0].shape[1]

    def weight_copy(i):
        rows = pl.ds(pl.multiple_of(i * depth, depth), depth)
        return pltpu.make_async_copy(weight_ref.at[:, rows], weights.at[i], weight_sem.at[i])

    gain_copies = [
        pltpu.make_async_copy(source, gains.at[i], gain_sem.at[i])
        for i, source in enumerate((q_gain_ref, k_gain_ref))
    ]

    @pl.when(step == 0)
    def _():
        for i in range(STEPS):
            weight_copy(i).start()
        for copy in gain_copies:
            copy.start()
        total[...] = jnp.zeros_like(total)

    weight_copy(step).wait()
    tokens = jnp.concatenate([ref[...] for ref in tokens_refs], axis=0)
    weight = jnp.concatenate([weights[step, i] for i in range(3)], axis=1)
    total[...] += jnp.dot(tokens, weight, preferred_element_type=F32)

    @pl.when(step == STEPS - 1)
    def _():
        for copy in gain_copies:
            copy.wait()

        def normed(i, gain):
            part = total[:, i * HD : (i + 1) * HD]
            meansq = jnp.mean(part * part, axis=-1, keepdims=True)
            return part * lax.rsqrt(meansq + epsilon) * gain

        queries = normed(0, gains[0] * (math.log2(math.e) / math.sqrt(HD))).astype(BF16)
        for i in range(q_ref.shape[0]):
            q_ref[i] = queries
        kv_ref[:, :HD] = normed(1, gains[1]).astype(BF16)
        kv_ref[:, HD:] = total[:, 2 * HD :].astype(BF16)


def project(tokens, weight, q_gain, k_gain, copies):
    width = tokens[0].shape[1]
    rows = sum(part.shape[0] for part in tokens)
    depth = width // STEPS
    count = len(tokens)
    return pl.pallas_call(
        lambda *refs: project_kernel(refs[:count], *refs[count:]),
        grid=(STEPS,),
        in_specs=[pl.BlockSpec((part.shape[0], depth), lambda i: (0, i)) for part in tokens]
        + [pl.BlockSpec(memory_space=pltpu.HBM)] * 3,
        out_specs=[
            pl.BlockSpec((copies, rows, HD), lambda i: (0, 0, 0)),
            pl.BlockSpec((rows, 2 * HD), lambda i: (0, 0)),
        ],
        out_shape=[
            jax.ShapeDtypeStruct((copies, rows, HD), BF16),
            jax.ShapeDtypeStruct((rows, 2 * HD), BF16),
        ],
        scratch_shapes=[
            pltpu.VMEM((rows, 3 * HD), F32),
            pltpu.VMEM((STEPS, 3, depth, HD), BF16),
            pltpu.VMEM((2, 1, HD), F32),
            pltpu.SemaphoreType.DMA((STEPS,)),
            pltpu.SemaphoreType.DMA((2,)),
        ],
        compiler_params=params(16),
        cost_estimate=pl.CostEstimate(
            flops=2 * rows * width * 3 * HD, bytes_accessed=3 * width * HD * 2, transcendentals=0
        ),
    )(*tokens, weight, q_gain[None], k_gain[None])


TAIL = 16


def diagonal(rows):
    down = lax.broadcasted_iota(jnp.int32, (rows, HD), 0)
    return down == lax.broadcasted_iota(jnp.int32, (rows, HD), 1)


def row_blocks(rows):
    return [(at, min(HD, rows - at)) for at in range(0, rows, HD)]


def tail_of(rows):
    row_of = lax.broadcasted_iota(jnp.int32, (TAIL, HD), 0)
    tail = jnp.zeros((TAIL, HD), F32)
    for j, row in enumerate(rows):
        high = row.astype(BF16).astype(F32)
        tail = jnp.where(row_of == j, high, tail)
        tail = jnp.where(row_of == len(rows) + j, row - high, tail)
    return tail.astype(BF16)


def totals_of(block, rows):
    count = len(row_blocks(rows))
    starts = [rows + j for j in range(count)]
    return [block[at : at + 1] + block[at + count : at + count + 1] for at in starts]


def attend_kernel(q_ref, kv_ref, out_ref):
    blocks, rows, _ = q_ref.shape
    step = kv_ref.shape[0] // 2
    totals = [0.0] * blocks
    for at in range(0, kv_ref.shape[0], step):
        values = jnp.concatenate([kv_ref[at : at + step, HD:], jnp.ones((step, HD), BF16)], axis=1)
        for i in range(blocks):
            scores = lax.dot_general(
                q_ref[i],
                kv_ref[at : at + step, :HD],
                (((1,), (1,)), ((), ())),
                preferred_element_type=F32,
            )
            weights = jnp.exp2(scores).astype(BF16)
            totals[i] += jnp.dot(weights, values, preferred_element_type=F32)
    for i, total in enumerate(totals):
        out_ref[i, :rows] = total[:, :HD].astype(BF16)
        sums = [
            jnp.where(diagonal(size), total[at : at + size, HD:], 0.0)
            for at, size in row_blocks(rows)
        ]
        out_ref[i, rows:] = tail_of([jnp.sum(square, axis=0, keepdims=True) for square in sums])


def attend(queries, keyval):
    blocks, rows, _ = queries.shape
    keys = keyval.shape[0]
    return pl.pallas_call(
        attend_kernel,
        grid=(blocks // 2,),
        in_specs=[
            pl.BlockSpec((2, rows, HD), lambda i: (i, 0, 0)),
            pl.BlockSpec(keyval.shape, lambda i: (0, 0)),
        ],
        out_specs=pl.BlockSpec((2, rows + TAIL, HD), lambda i: (i, 0, 0)),
        out_shape=jax.ShapeDtypeStruct((blocks, rows + TAIL, HD), BF16),
        compiler_params=params(16),
        cost_estimate=pl.CostEstimate(
            flops=5 * blocks * rows * keys * HD,
            bytes_accessed=4 * keys * HD,
            transcendentals=blocks * rows * keys,
        ),
    )(queries, keyval)


def divide_kernel(partial_ref, out_ref):
    rows = partial_ref.shape[1] - TAIL
    summed = jnp.sum(partial_ref[...].astype(F32), axis=0)
    attended = []
    for row, (at, size) in zip(totals_of(summed, rows), row_blocks(rows)):
        square = jnp.broadcast_to(row, (size, HD))
        column = jnp.sum(jnp.where(diagonal(size), square, 0.0), axis=1, keepdims=True)
        attended.append((summed[at : at + size] / column).astype(BF16))
    attended = jnp.concatenate(attended, axis=0)
    along, part = out_ref.shape[0], out_ref.shape[1] // 4
    for y in range(along):
        for far in range(2):
            for other in range(2):
                at = ((far * 2 + other) * along + y) * part
                to = (other * 2 + far) * part
                out_ref[y, to : to + part] = attended[at : at + part]


def divide(partial, along):
    rows = partial.shape[1] - TAIL
    return pl.pallas_call(
        divide_kernel,
        out_shape=jax.ShapeDtypeStruct((along, rows // along, HD), BF16),
        compiler_params=params(8),
    )(partial)


def mix_kernel(y_ref, attended_ref, first_ref, *refs):
    *weight_refs, own_ref, other_ref, first, first_sem = refs
    copy = pltpu.make_async_copy(first_ref, first, first_sem.at[0])
    copy.start()
    mixed = jnp.dot(
        jnp.concatenate([attended_ref[y_ref[0] ^ i] for i in (2, 3)], axis=1),
        jnp.concatenate([ref[...] for ref in weight_refs[1:]], axis=0),
        preferred_element_type=F32,
    )
    copy.wait()
    mixed += jnp.dot(
        jnp.concatenate([attended_ref[y_ref[0] ^ i] for i in (0, 1)], axis=1),
        jnp.concatenate([first[...], weight_refs[0][...]], axis=0),
        preferred_element_type=F32,
    )
    half = own_ref.shape[0]
    own_ref[...] = mixed[:half]
    other_ref[...] = mixed[half:].astype(BF16)


def mix(y, attended, weights):
    rows = attended.shape[1]
    depth, width = weights[0].shape
    vmem = pl.BlockSpec(memory_space=pltpu.VMEM)
    return pl.pallas_call(
        mix_kernel,
        in_specs=[
            pl.BlockSpec(memory_space=pltpu.SMEM),
            vmem,
            pl.BlockSpec(memory_space=pltpu.HBM),
            vmem,
            vmem,
            vmem,
        ],
        out_shape=[
            jax.ShapeDtypeStruct((rows // 2, width), F32),
            jax.ShapeDtypeStruct((rows // 2, width), BF16),
        ],
        scratch_shapes=[pltpu.VMEM((depth, width), BF16), pltpu.SemaphoreType.DMA((1,))],
        compiler_params=params(16),
        cost_estimate=pl.CostEstimate(
            flops=2 * len(weights) * rows * width * depth,
            bytes_accessed=2 * len(weights) * width * depth,
            transcendentals=0,
        ),
    )(y, attended, *weights)


def local(tokens, mod_shift, mod_scale, qkv_weight, q_gain, k_gain, out_weight, out_gate):
    rows, width = tokens.shape

    def along_y(block, distance):
        return lax.ppermute(block, "y", [(i, i ^ distance) for i in range(4)])

    def spread(modulated):
        own = lax.all_gather(modulated, "y", axis=0, tiled=True)
        return [own, swap(own, "core")]

    far = trade_halves(tokens)
    near, pair = modulate_near(tokens, mod_shift, mod_scale)
    parts = spread(near) + spread(modulate_far(far, pair))
    queries, keyval = project(parts, qkv_weight, q_gain, k_gain, 8)
    out_weight, keyval = lax.optimization_barrier((out_weight, keyval))
    weights = [out_weight] + [along_y(out_weight, i) for i in (1, 2, 3)]
    queries = lax.all_to_all(queries, NEAR, 0, 0)
    one, two = swap(keyval, "za"), swap(keyval, "zb")
    three = swap(one, "zb")
    partial = attend(queries, jnp.concatenate([keyval, one, two, three], axis=0))
    partial, weights = lax.optimization_barrier((partial, weights))
    partial = lax.all_to_all(partial, NEAR, 0, 0)
    attended = lax.all_to_all(divide(partial, 4), "y", 0, 0)
    y = lax.axis_index("y").astype(jnp.int32).reshape(1)
    own, other = mix(y, attended, weights)
    summed = own + swap(other, "core").astype(F32)
    arrived = trade_halves(summed[rows:].astype(BF16)).astype(F32)
    return ((summed[:rows] + arrived) * out_gate).astype(BF16)


def solution(mesh):
    fine = Mesh(mesh.devices.reshape(tuple(AXES.values())), ALL)
    heads = ("y", "zh", "core")
    return jax.shard_map(
        local,
        mesh=fine,
        in_specs=(
            P(ALL, None),
            P(),
            P(),
            P(None, None, heads),
            P(),
            P(),
            P(heads, None),
            P(),
        ),
        out_specs=P(ALL, None),
        check_vma=False,
    )
```

time: 185 us -> 163 us (0.88)
  the two profiles are of different devices: /device:TPU:161 before, /device:TPU:1 now
where the time goes in v4:
time: 163 us; the launch traced here: 160 us
  starting transfers between devices  60.5 us (37%)
  waiting for transfers between devices  43.7 us (27%)
  blocking collectives  38.5 us (24%)
  Pallas kernels  14.2 us (9%)
  local copies, waits for them, and re-layouts  2.43 us (1%)
    ppermute x6, starting transfers between devices, swap(): return lax.ppermute(block, axis, [(0, 1), (1, 0)])  27.3 us
    all_gather x2, blocking collectives, spread(): own = lax.all_gather(modulated, 'y', axis=0, tiled=True)  23.6 us
    ppermute x6, waiting for transfers between devices, swap(): return lax.ppermute(block, axis, [(0, 1), (1, 0)])  22.6 us
    ppermute x2, starting transfers between devices, trade_halves(): return lax.ppermute(block, ('zh', 'za'), [(i, i ^ 3) for i in range(4)])  15.3 us
    all_to_all x1, blocking collectives, local(): partial = lax.all_to_all(partial, NEAR, 0, 0)  14.9 us
    ppermute x2, waiting for transfers between devices, trade_halves(): return lax.ppermute(block, ('zh', 'za'), [(i, i ^ 3) for i in range(4)])  13 us
    ppermute x3, starting transfers between devices, along_y(): return lax.ppermute(block, 'y', [(i, i ^ distance) for i in range(4)])  9.89 us
    pallas_call x1, Pallas kernels, attend(): pl.pallas_call(attend_kernel, grid=(blocks // 2,), in_specs=[pl.BlockSpec...  5.58 us
  transfers between devices with their start and end apart: 13, of which 8 were waited for; matrix products, arithmetic and copies ran while one was open for 0% of the time, Pallas kernels for 5%

profile of v4, /device:TPU:1, one launch (start us, length us, event | category | flops | bytes accessed | tf_op | source)
XLA Modules:
  0.0 160.4 jit_solution(11229489246001883406)
XLA Ops:
  0.0 0.0 copy-start.3
  0.0 0.0 copy-start.4
  0.0 13.4 %collective-permute-start.1 = (bf16[24,3072]{1,0:T(8,128)(2,1)}, bf16[24,3072]{1,0:T(8,128)(2,1)S(1)}, u32[]{:S(2)}, u32[]{:S(2)}) collective-permute-start(bf16[24,3072]{1,0:T(8,128)(2,1)} %tokens_ref.1), channel_id=1, source_target_pairs={{0,80},{16,64},{64,16},{80,0},{1,81},{17,65},{65,17},{81,1},{2,82}... | collective-permute-start | bytes 442376 | tf_op jit(solution)/shard_map/ppermute | solution.py:29
  13.4 1.9 %shard_map.82 = (bf16[24,3072]{1,0:T(8,128)(2,1)}, f32[2,1,3072]{2,1,0:T(1,128)}) custom-call(bf16[24,3072]{1,0:T(8,128)(2,1)} %tokens_ref.1, f32[1,3072]{1,0:T(1,128)} %bitcast.7, f32[1,3072]{1,0:T(1,128)} %bitcast.8), custom_call_target="tpu_custom_call" | custom-call | tf_op jit(solution)/shard_map/pallas_call | solution.py:55
  15.3 12.2 %all_gather.6.refs_0_ = bf16[96,3072]{1,0:T(8,128)(2,1)S(1)} all-gather(bf16[24,3072]{1,0:T(8,128)(2,1)} %get-tuple-element.18), channel_id=1, replica_groups=mesh['y'=4,'zh'=2,'core'=2,'za'=2,'zb'=2,'zc'=2,'x'=4] {'y'}, dimensions={0}, use_global_device_ids=true | all-gather | bytes 737280 | tf_op jit(solution)/shard_map/all_gather | solution.py:314
  27.5 4.3 %collective-permute-start = (bf16[96,3072]{1,0:T(8,128)(2,1)S(1)}, bf16[96,3072]{1,0:T(8,128)(2,1)S(1)}, u32[]{:S(2)}, u32[]{:S(2)}) collective-permute-start(bf16[96,3072]{1,0:T(8,128)(2,1)S(1)} %all_gather.6.refs_0_), channel_id=1, source_target_pairs={{0,32},{32,0},{1,33},{33,1},{2,34},{34,2},{3,35},{35,3},{4,36},{36... | collective-permute-start | bytes 1769480 | tf_op jit(solution)/shard_map/ppermute | solution.py:25
  31.8 0.0 collective-permute-done.1.tokens_ref
  31.8 0.0 copy-start.2
  31.8 0.7 copy-done.2
  32.6 0.3 shard_map.83
  32.8 11.4 %all_gather.7.refs_2_ = bf16[96,3072]{1,0:T(8,128)(2,1)S(1)} all-gather(bf16[24,3072]{1,0:T(8,128)(2,1)S(1)} %shard_map.83), channel_id=1, replica_groups=mesh['y'=4,'zh'=2,'core'=2,'za'=2,'zb'=2,'zc'=2,'x'=4] {'y'}, dimensions={0}, use_global_device_ids=true | all-gather | bytes 737280 | tf_op jit(solution)/shard_map/all_gather | solution.py:314
  44.3 3.9 %collective-permute-start.2 = (bf16[96,3072]{1,0:T(8,128)(2,1)S(1)}, bf16[96,3072]{1,0:T(8,128)(2,1)S(1)}, u32[]{:S(2)}, u32[]{:S(2)}) collective-permute-start(bf16[96,3072]{1,0:T(8,128)(2,1)S(1)} %all_gather.7.refs_2_), channel_id=1, source_target_pairs={{0,32},{32,0},{1,33},{33,1},{2,34},{34,2},{3,35},{35,3},{4,36},{36... | collective-permute-start | bytes 1769480 | tf_op jit(solution)/shard_map/ppermute | solution.py:25
  48.1 0.0 collective-permute-done.refs_1_
  48.2 1.6 collective-permute-done.2.refs_3_
  49.8 0.0 copy-done.3
  49.8 0.0 copy-done.4
  49.8 0.0 copy-start
  49.8 1.7 %copy-done = bf16[3,3072,128]{2,1,0:T(8,128)(2,1)S(1)} copy-done((bf16[3,3072,128]{2,1,0:T(8,128)(2,1)S(1)}, bf16[3,3072,128]{2,1,0:T(8,128)(2,1)}, u32[]{:S(2)}) %copy-start) | copy-done | bytes 2359320
  51.4 3.5 %shard_map.84 = (bf16[8,384,128]{2,1,0:T(8,128)(2,1)}, bf16[384,256]{1,0:T(8,128)(2,1)S(1)}) custom-call(bf16[96,3072]{1,0:T(8,128)(2,1)S(1)} %all_gather.6.refs_0_, bf16[96,3072]{1,0:T(8,128)(2,1)S(1)} %collective-permute-done.refs_1_, bf16[96,3072]{1,0:T(8,128)(2,1)S(1)} %all_gather.7.refs_2_, bf16[96,3072]{1,0:T(8,128)(2,1)S(1)} %collective-permute-done.2.refs_3_, ...), custom_call_target="tpu_custom_call" | custom-call | flops 905969664 | bytes 2359296 | tf_op jit(solution)/shard_map/pallas_call | solution.py:132
  54.9 0.0 copy-start.1
  54.9 4.8 %all-to-all-start = ((bf16[8,384,128]{2,1,0:T(8,128)(2,1)}), bf16[8,384,128]{2,1,0:T(8,128)(2,1)S(1)}, u32[]{:S(2)}, u32[]{:S(2)}) async-start(bf16[8,384,128]{2,1,0:T(8,128)(2,1)} %get-tuple-element.20), calls=%async_computation | async-start | bytes 1572864 | tf_op jit(solution)/shard_map/all_to_all | solution.py:323
  59.7 5.2 %collective-permute-start.3 = (bf16[384,256]{1,0:T(8,128)(2,1)S(1)}, bf16[384,256]{1,0:T(8,128)(2,1)S(1)}, u32[]{:S(2)}, u32[]{:S(2)}) collective-permute-start(bf16[384,256]{1,0:T(8,128)(2,1)S(1)} %get-tuple-element.22), channel_id=1, source_target_pairs={{0,16},{16,0},{1,17},{17,1},{2,18},{18,2},{3,19},{19,3},{4,20},{20... | collective-permute-start | bytes 589832 | tf_op jit(solution)/shard_map/ppermute | solution.py:25
  64.9 0.0 copy-done.1
  64.9 3.7 %collective-permute-start.6 = (bf16[128,3072]{1,0:T(8,128)(2,1)S(1)}, bf16[128,3072]{1,0:T(8,128)(2,1)S(1)}, u32[]{:S(2)}, u32[]{:S(2)}) collective-permute-start(bf16[128,3072]{1,0:T(8,128)(2,1)S(1)} %copy-done.1), channel_id=1, source_target_pairs={{0,128},{128,0},{256,384},{384,256},{1,129},{129,1},{257,385},{385... | collective-permute-start | bytes 2359304 | tf_op jit(solution)/shard_map/ppermute | solution.py:311
  68.6 4.3 %collective-permute-start.7 = (bf16[128,3072]{1,0:T(8,128)(2,1)S(1)}, bf16[128,3072]{1,0:T(8,128)(2,1)}, u32[]{:S(2)}, u32[]{:S(2)}) collective-permute-start(bf16[128,3072]{1,0:T(8,128)(2,1)S(1)} %copy-done.1), channel_id=1, source_target_pairs={{0,256},{128,384},{256,0},{384,128},{1,257},{129,385},{257,1},{385... | collective-permute-start | bytes 2359304 | tf_op jit(solution)/shard_map/ppermute | solution.py:311
  72.9 1.9 %collective-permute-start.8 = (bf16[128,3072]{1,0:T(8,128)(2,1)S(1)}, bf16[128,3072]{1,0:T(8,128)(2,1)}, u32[]{:S(2)}, u32[]{:S(2)}) collective-permute-start(bf16[128,3072]{1,0:T(8,128)(2,1)S(1)} %copy-done.1), channel_id=1, source_target_pairs={{0,384},{128,256},{256,128},{384,0},{1,385},{129,257},{257,129},{3... | collective-permute-start | bytes 2359304 | tf_op jit(solution)/shard_map/ppermute | solution.py:311
  74.8 3.1 %collective-permute-start.4 = (bf16[384,256]{1,0:T(8,128)(2,1)S(1)}, bf16[384,256]{1,0:T(8,128)(2,1)S(1)}, u32[]{:S(2)}, u32[]{:S(2)}) collective-permute-start(bf16[384,256]{1,0:T(8,128)(2,1)S(1)} %get-tuple-element.22), channel_id=1, source_target_pairs={{0,8},{8,0},{1,9},{9,1},{2,10},{10,2},{3,11},{11,3},{4,12},{12,4},... | collective-permute-start | bytes 589832 | tf_op jit(solution)/shard_map/ppermute | solution.py:25
  77.9 2.1 %collective-permute-done.3 = bf16[384,256]{1,0:T(8,128)(2,1)S(1)} collective-permute-done((bf16[384,256]{1,0:T(8,128)(2,1)S(1)}, bf16[384,256]{1,0:T(8,128)(2,1)S(1)}, u32[]{:S(2)}, u32[]{:S(2)}) %collective-permute-start.3) | collective-permute-done | bytes 196640 | tf_op jit(solution)/shard_map/ppermute | solution.py:25
  80.0 3.7 %collective-permute-start.5 = (bf16[384,256]{1,0:T(8,128)(2,1)S(1)}, bf16[384,256]{1,0:T(8,128)(2,1)S(1)}, u32[]{:S(2)}, u32[]{:S(2)}) collective-permute-start(bf16[384,256]{1,0:T(8,128)(2,1)S(1)} %collective-permute-done.3), channel_id=1, source_target_pairs={{0,8},{8,0},{1,9},{9,1},{2,10},{10,2},{3,11},{11,3},{4,12},{12,4},... | collective-permute-start | bytes 589832 | tf_op jit(solution)/shard_map/ppermute | solution.py:25
  83.7 11.3 %collective-permute-done.4 = bf16[384,256]{1,0:T(8,128)(2,1)S(1)} collective-permute-done((bf16[384,256]{1,0:T(8,128)(2,1)S(1)}, bf16[384,256]{1,0:T(8,128)(2,1)S(1)}, u32[]{:S(2)}, u32[]{:S(2)}) %collective-permute-start.4) | collective-permute-done | bytes 196640 | tf_op jit(solution)/shard_map/ppermute | solution.py:25
  95.0 6.3 %collective-permute-done.5 = bf16[384,256]{1,0:T(8,128)(2,1)S(1)} collective-permute-done((bf16[384,256]{1,0:T(8,128)(2,1)S(1)}, bf16[384,256]{1,0:T(8,128)(2,1)S(1)}, u32[]{:S(2)}, u32[]{:S(2)}) %collective-permute-start.5) | collective-permute-done | bytes 196640 | tf_op jit(solution)/shard_map/ppermute | solution.py:25
  101.3 0.1 pad_maximum_fusion.kv_ref
  101.4 0.0 all-to-all-done.q_ref
  101.4 5.6 %shard_map.85 = bf16[8,400,128]{2,1,0:T(8,128)(2,1)S(1)} custom-call(bf16[8,384,128]{2,1,0:T(8,128)(2,1)S(1)} %all-to-all-done.q_ref, bf16[1536,256]{1,0:T(8,128)(2,1)S(1)} %pad_maximum_fusion.kv_ref), custom_call_target="tpu_custom_call" | custom-call | flops 3019898880 | bytes 786432 | tf_op jit(solution)/shard_map/pallas_call | solution.py:214
  107.0 0.0 collective-permute-done.6.refs_0_
  107.0 0.0 collective-permute-done.7.refs_1_
  107.0 3.5 %collective-permute-done.8.refs_2_ = bf16[128,3072]{1,0:T(8,128)(2,1)} collective-permute-done((bf16[128,3072]{1,0:T(8,128)(2,1)S(1)}, bf16[128,3072]{1,0:T(8,128)(2,1)}, u32[]{:S(2)}, u32[]{:S(2)}) %collective-permute-start.8) | collective-permute-done | bytes 786464 | tf_op jit(solution)/shard_map/ppermute | solution.py:311
  110.5 14.9 %all_to_all.15.partial_ref = bf16[8,400,128]{2,1,0:T(8,128)(2,1)S(1)} all-to-all(bf16[8,400,128]{2,1,0:T(8,128)(2,1)S(1)} %shard_map.85), channel_id=1, replica_groups=mesh['y'=4,'zh'=2,'core'=2,'za'=2,'zb'=2,'zc'=2,'x'=4] {'zc','x'}, dimensions={0} | all-to-all | bytes 1638400 | tf_op jit(solution)/shard_map/all_to_all | solution.py:328
  125.4 0.8 shard_map.86
  126.2 3.3 %all-to-all-start.2 = ((bf16[4,96,128]{2,1,0:T(8,128)(2,1)}), bf16[4,96,128]{2,1,0:T(8,128)(2,1)S(1)}, u32[]{:S(2)}, u32[]{:S(2)}) async-start(bf16[4,96,128]{2,1,0:T(8,128)(2,1)} %shard_map.86), calls=%async_computation.2 | async-start | bytes 196608 | tf_op jit(solution)/shard_map/all_to_all | solution.py:329
  129.5 4.6 %all-to-all-done.2.attended_ref = bf16[4,96,128]{2,1,0:T(8,128)(2,1)S(1)} async-done(((bf16[4,96,128]{2,1,0:T(8,128)(2,1)}), bf16[4,96,128]{2,1,0:T(8,128)(2,1)S(1)}, u32[]{:S(2)}, u32[]{:S(2)}) %all-to-all-start.2) | async-done | bytes 98336 | tf_op jit(solution)/shard_map/all_to_all | solution.py:329
  134.1 2.2 %shard_map.87 = (f32[48,3072]{1,0:T(8,128)S(1)}, bf16[48,3072]{1,0:T(8,128)(2,1)S(1)}) custom-call(s32[1]{0:T(128)} %bitcast.y_ref, bf16[4,96,128]{2,1,0:T(8,128)(2,1)S(1)} %all-to-all-done.2.attended_ref, bf16[128,3072]{1,0:T(8,128)(2,1)S(1)} %copy-done.1, bf16[128,3072]{1,0:T(8,128)(2,1)S(1)} %collective-permute-done.6.refs_0_, ...), custom_call_target="tpu_custom_call" | custom-call | flops 301989888 | bytes 3145728 | tf_op jit(solution)/shard_map/pallas_call | solution.py:283
  136.3 0.0 copy-start.5
  136.3 7.2 %collective-permute-start.9 = (bf16[48,3072]{1,0:T(8,128)(2,1)S(1)}, bf16[48,3072]{1,0:T(8,128)(2,1)S(1)}, u32[]{:S(2)}, u32[]{:S(2)}) collective-permute-start(bf16[48,3072]{1,0:T(8,128)(2,1)S(1)} %get-tuple-element.30), channel_id=1, source_target_pairs={{0,32},{32,0},{1,33},{33,1},{2,34},{34,2},{3,35},{35,3},{4,36},{36... | collective-permute-start | bytes 884744 | tf_op jit(solution)/shard_map/ppermute | solution.py:25
  143.5 1.2 collective-permute-done.9
  144.7 0.1 convert_add_fusion
  144.8 1.9 %collective-permute-start.10 = (bf16[24,3072]{1,0:T(8,128)(2,1)S(1)}, bf16[24,3072]{1,0:T(8,128)(2,1)S(1)}, u32[]{:S(2)}, u32[]{:S(2)}) collective-permute-start(bf16[24,3072]{1,0:T(8,128)(2,1)S(1)} %slice.17), channel_id=1, source_target_pairs={{0,80},{16,64},{64,16},{80,0},{1,81},{17,65},{65,17},{81,1},{2,82}... | collective-permute-start | bytes 442376 | tf_op jit(solution)/shard_map/ppermute | solution.py:29
  146.7 13.0 %collective-permute-done.10 = bf16[24,3072]{1,0:T(8,128)(2,1)S(1)} collective-permute-done((bf16[24,3072]{1,0:T(8,128)(2,1)S(1)}, bf16[24,3072]{1,0:T(8,128)(2,1)S(1)}, u32[]{:S(2)}, u32[]{:S(2)}) %collective-permute-start.10) | collective-permute-done | bytes 147488 | tf_op jit(solution)/shard_map/ppermute | solution.py:29
  159.7 0.0 copy-done.5
  159.7 0.7 fusion.1
  (1 shorter events, 0.0 us)
Async XLA Ops:
  0.0 49.8 %copy-start.3 = (f32[128]{0:T(128)S(1)}, f32[128]{0:T(128)}, u32[]{:S(2)}) copy-start(f32[128]{0:T(128)} %param.12) | copy-start | bytes 1540
  0.0 49.8 %copy-start.4 = (f32[128]{0:T(128)S(1)}, f32[128]{0:T(128)}, u32[]{:S(2)}) copy-start(f32[128]{0:T(128)} %param.13) | copy-start | bytes 1540
  0.0 31.8 %collective-permute-start.1 = (bf16[24,3072]{1,0:T(8,128)(2,1)}, bf16[24,3072]{1,0:T(8,128)(2,1)S(1)}, u32[]{:S(2)}, u32[]{:S(2)}) collective-permute-start(bf16[24,3072]{1,0:T(8,128)(2,1)} %tokens_ref.1), channel_id=1, source_target_pairs={{0,80},{16,64},{64,16},{80,0},{1,81},{17,65},{65,17},{81,1},{2,82}... | collective-permute-start | bytes 442376 | tf_op jit(solution)/shard_map/ppermute | solution.py:29
  27.5 20.6 %collective-permute-start = (bf16[96,3072]{1,0:T(8,128)(2,1)S(1)}, bf16[96,3072]{1,0:T(8,128)(2,1)S(1)}, u32[]{:S(2)}, u32[]{:S(2)}) collective-permute-start(bf16[96,3072]{1,0:T(8,128)(2,1)S(1)} %all_gather.6.refs_0_), channel_id=1, source_target_pairs={{0,32},{32,0},{1,33},{33,1},{2,34},{34,2},{3,35},{35,3},{4,36},{36... | collective-permute-start | bytes 1769480 | tf_op jit(solution)/shard_map/ppermute | solution.py:25
  31.8 0.7 copy-start.2
  44.3 5.5 %collective-permute-start.2 = (bf16[96,3072]{1,0:T(8,128)(2,1)S(1)}, bf16[96,3072]{1,0:T(8,128)(2,1)S(1)}, u32[]{:S(2)}, u32[]{:S(2)}) collective-permute-start(bf16[96,3072]{1,0:T(8,128)(2,1)S(1)} %all_gather.7.refs_2_), channel_id=1, source_target_pairs={{0,32},{32,0},{1,33},{33,1},{2,34},{34,2},{3,35},{35,3},{4,36},{36... | collective-permute-start | bytes 1769480 | tf_op jit(solution)/shard_map/ppermute | solution.py:25
  49.8 1.7 %copy-start = (bf16[3,3072,128]{2,1,0:T(8,128)(2,1)S(1)}, bf16[3,3072,128]{2,1,0:T(8,128)(2,1)}, u32[]{:S(2)}) copy-start(bf16[3,3072,128]{2,1,0:T(8,128)(2,1)} %refs_4_.1) | copy-start | bytes 7077892
  54.9 9.9 %copy-start.1 = (bf16[128,3072]{1,0:T(8,128)(2,1)S(1)}, bf16[128,3072]{1,0:T(8,128)(2,1)}, u32[]{:S(2)}) copy-start(bf16[128,3072]{1,0:T(8,128)(2,1)} %first_ref) | copy-start | bytes 2359300
  54.9 46.4 %all-to-all-start = ((bf16[8,384,128]{2,1,0:T(8,128)(2,1)}), bf16[8,384,128]{2,1,0:T(8,128)(2,1)S(1)}, u32[]{:S(2)}, u32[]{:S(2)}) async-start(bf16[8,384,128]{2,1,0:T(8,128)(2,1)} %get-tuple-element.20), calls=%async_computation | async-start | bytes 1572864 | tf_op jit(solution)/shard_map/all_to_all | solution.py:323
  59.7 20.3 %collective-permute-start.3 = (bf16[384,256]{1,0:T(8,128)(2,1)S(1)}, bf16[384,256]{1,0:T(8,128)(2,1)S(1)}, u32[]{:S(2)}, u32[]{:S(2)}) collective-permute-start(bf16[384,256]{1,0:T(8,128)(2,1)S(1)} %get-tuple-element.22), channel_id=1, source_target_pairs={{0,16},{16,0},{1,17},{17,1},{2,18},{18,2},{3,19},{19,3},{4,20},{20... | collective-permute-start | bytes 589832 | tf_op jit(solution)/shard_map/ppermute | solution.py:25
  64.9 42.1 %collective-permute-start.6 = (bf16[128,3072]{1,0:T(8,128)(2,1)S(1)}, bf16[128,3072]{1,0:T(8,128)(2,1)S(1)}, u32[]{:S(2)}, u32[]{:S(2)}) collective-permute-start(bf16[128,3072]{1,0:T(8,128)(2,1)S(1)} %copy-done.1), channel_id=1, source_target_pairs={{0,128},{128,0},{256,384},{384,256},{1,129},{129,1},{257,385},{385... | collective-permute-start | bytes 2359304 | tf_op jit(solution)/shard_map/ppermute | solution.py:311
  68.6 38.4 %collective-permute-start.7 = (bf16[128,3072]{1,0:T(8,128)(2,1)S(1)}, bf16[128,3072]{1,0:T(8,128)(2,1)}, u32[]{:S(2)}, u32[]{:S(2)}) collective-permute-start(bf16[128,3072]{1,0:T(8,128)(2,1)S(1)} %copy-done.1), channel_id=1, source_target_pairs={{0,256},{128,384},{256,0},{384,128},{1,257},{129,385},{257,1},{385... | collective-permute-start | bytes 2359304 | tf_op jit(solution)/shard_map/ppermute | solution.py:311
  72.9 37.6 %collective-permute-start.8 = (bf16[128,3072]{1,0:T(8,128)(2,1)S(1)}, bf16[128,3072]{1,0:T(8,128)(2,1)}, u32[]{:S(2)}, u32[]{:S(2)}) collective-permute-start(bf16[128,3072]{1,0:T(8,128)(2,1)S(1)} %copy-done.1), channel_id=1, source_target_pairs={{0,384},{128,256},{256,128},{384,0},{1,385},{129,257},{257,129},{3... | collective-permute-start | bytes 2359304 | tf_op jit(solution)/shard_map/ppermute | solution.py:311
  74.8 20.2 %collective-permute-start.4 = (bf16[384,256]{1,0:T(8,128)(2,1)S(1)}, bf16[384,256]{1,0:T(8,128)(2,1)S(1)}, u32[]{:S(2)}, u32[]{:S(2)}) collective-permute-start(bf16[384,256]{1,0:T(8,128)(2,1)S(1)} %get-tuple-element.22), channel_id=1, source_target_pairs={{0,8},{8,0},{1,9},{9,1},{2,10},{10,2},{3,11},{11,3},{4,12},{12,4},... | collective-permute-start | bytes 589832 | tf_op jit(solution)/shard_map/ppermute | solution.py:25
  80.0 21.3 %collective-permute-start.5 = (bf16[384,256]{1,0:T(8,128)(2,1)S(1)}, bf16[384,256]{1,0:T(8,128)(2,1)S(1)}, u32[]{:S(2)}, u32[]{:S(2)}) collective-permute-start(bf16[384,256]{1,0:T(8,128)(2,1)S(1)} %collective-permute-done.3), channel_id=1, source_target_pairs={{0,8},{8,0},{1,9},{9,1},{2,10},{10,2},{3,11},{11,3},{4,12},{12,4},... | collective-permute-start | bytes 589832 | tf_op jit(solution)/shard_map/ppermute | solution.py:25
  126.2 7.9 %all-to-all-start.2 = ((bf16[4,96,128]{2,1,0:T(8,128)(2,1)}), bf16[4,96,128]{2,1,0:T(8,128)(2,1)S(1)}, u32[]{:S(2)}, u32[]{:S(2)}) async-start(bf16[4,96,128]{2,1,0:T(8,128)(2,1)} %shard_map.86), calls=%async_computation.2 | async-start | bytes 196608 | tf_op jit(solution)/shard_map/all_to_all | solution.py:329
  136.3 23.4 %copy-start.5 = (f32[3072]{0:T(1024)S(1)}, f32[3072]{0:T(1024)}, u32[]{:S(2)}) copy-start(f32[3072]{0:T(1024)} %param.15) | copy-start | bytes 36868
  136.3 8.4 %collective-permute-start.9 = (bf16[48,3072]{1,0:T(8,128)(2,1)S(1)}, bf16[48,3072]{1,0:T(8,128)(2,1)S(1)}, u32[]{:S(2)}, u32[]{:S(2)}) collective-permute-start(bf16[48,3072]{1,0:T(8,128)(2,1)S(1)} %get-tuple-element.30), channel_id=1, source_target_pairs={{0,32},{32,0},{1,33},{33,1},{2,34},{34,2},{3,35},{35,3},{4,36},{36... | collective-permute-start | bytes 884744 | tf_op jit(solution)/shard_map/ppermute | solution.py:25
  144.8 14.9 %collective-permute-start.10 = (bf16[24,3072]{1,0:T(8,128)(2,1)S(1)}, bf16[24,3072]{1,0:T(8,128)(2,1)S(1)}, u32[]{:S(2)}, u32[]{:S(2)}) collective-permute-start(bf16[24,3072]{1,0:T(8,128)(2,1)S(1)} %slice.17), channel_id=1, source_target_pairs={{0,80},{16,64},{64,16},{80,0},{1,81},{17,65},{65,17},{81,1},{2,82}... | collective-permute-start | bytes 442376 | tf_op jit(solution)/shard_map/ppermute | solution.py:29

commit v5 on v4

v5 whole, which is shorter than its diff:
```python
import math

import jax
import jax.numpy as jnp
from jax import lax
from jax.experimental import pallas as pl
from jax.experimental.pallas import tpu as pltpu
from jax.sharding import Mesh, PartitionSpec as P

HD = 128
epsilon = 1e-06
AXES = {"y": 4, "zh": 2, "core": 2, "za": 2, "zb": 2, "zc": 2, "x": 4}
ALL = tuple(AXES)
NEAR = ("zc", "x")
F32 = jnp.float32
BF16 = jnp.bfloat16
MIB = 1 << 20


def params(mib):
    return pltpu.CompilerParams(vmem_limit_bytes=mib * MIB)


def swap(block, axis):
    return lax.ppermute(block, axis, [(0, 1), (1, 0)])


def trade_halves(block):
    return lax.ppermute(block, ("zh", "za"), [(i, i ^ 3) for i in range(4)])


def normalize(tokens, shift, scale):
    widened = tokens.astype(F32)
    center = widened - jnp.mean(widened, axis=-1, keepdims=True)
    spread = jnp.mean(center * center, axis=-1, keepdims=True)
    normed = center * lax.rsqrt(spread + epsilon)
    return (normed * scale + shift).astype(BF16)


def modulate_near_kernel(tokens_ref, *refs):
    *row_refs, out_ref, rows_ref, tokens, sem = refs
    copies = [pltpu.make_async_copy(tokens_ref, tokens, sem.at[0])]
    for i, ref in enumerate(row_refs):
        copies.append(
            pltpu.make_async_copy(ref, rows_ref.at[i, :, pl.ds(0, ref.shape[1])], sem.at[i + 1])
        )
    for copy in copies:
        copy.start()
    for copy in copies:
        copy.wait()
    out_ref[...] = normalize(tokens[...], rows_ref[0], rows_ref[1])


def modulate_near(tokens, rows):
    width = tokens.shape[1]
    return pl.pallas_call(
        modulate_near_kernel,
        in_specs=[pl.BlockSpec(memory_space=pltpu.HBM)] * (1 + len(rows)),
        out_specs=[pl.BlockSpec(memory_space=pltpu.VMEM)] * 2,
        out_shape=[
            jax.ShapeDtypeStruct(tokens.shape, BF16),
            jax.ShapeDtypeStruct((len(rows), 1, width), F32),
        ],
        scratch_shapes=[
            pltpu.VMEM(tokens.shape, BF16),
            pltpu.SemaphoreType.DMA((1 + len(rows),)),
        ],
        compiler_params=params(60),
    )(tokens, *[row[None] for row in rows])


def modulate_far_kernel(tokens_ref, rows_ref, out_ref, gains_ref):
    out_ref[...] = normalize(tokens_ref[...], rows_ref[0], rows_ref[1])
    gains_ref[...] = rows_ref[2:, :, :HD]


def modulate_far(tokens, rows):
    return pl.pallas_call(
        modulate_far_kernel,
        out_shape=[
            jax.ShapeDtypeStruct(tokens.shape, BF16),
            jax.ShapeDtypeStruct((2, 1, HD), F32),
        ],
        compiler_params=params(8),
    )(tokens, rows)


STEPS = 4


def project_kernel(tokens_refs, gains_ref, weight_ref, q_ref, kv_ref, weights, sem):
    depth = weights.shape[2]
    copies = [
        pltpu.make_async_copy(
            weight_ref.at[:, pl.ds(i * depth, depth)], weights.at[i], sem.at[i]
        )
        for i in range(STEPS)
    ]
    for copy in copies:
        copy.start()
    total = 0.0
    for i, copy in enumerate(copies):
        tokens = [ref[:, i * depth : (i + 1) * depth] for ref in tokens_refs]
        tokens = jnp.concatenate(tokens, axis=0)
        copy.wait()
        weight = jnp.concatenate([weights[i, j] for j in range(3)], axis=1)
        total += jnp.dot(tokens, weight, preferred_element_type=F32)

    def normed(i, gain):
        part = total[:, i * HD : (i + 1) * HD]
        meansq = jnp.mean(part * part, axis=-1, keepdims=True)
        return part * lax.rsqrt(meansq + epsilon) * gain

    kv_ref[:, :HD] = normed(1, gains_ref[1]).astype(BF16)
    kv_ref[:, HD:] = total[:, 2 * HD :].astype(BF16)
    queries = normed(0, gains_ref[0] * (math.log2(math.e) / math.sqrt(HD))).astype(BF16)
    for i in range(q_ref.shape[0]):
        q_ref[i] = queries


def project(tokens, gains, weight, copies):
    width = tokens[0].shape[1]
    rows = sum(part.shape[0] for part in tokens)
    count = len(tokens)
    vmem = pl.BlockSpec(memory_space=pltpu.VMEM)
    return pl.pallas_call(
        lambda *refs: project_kernel(refs[:count], *refs[count:]),
        in_specs=[vmem] * (count + 1) + [pl.BlockSpec(memory_space=pltpu.HBM)],
        out_specs=[vmem, vmem],
        out_shape=[
            jax.ShapeDtypeStruct((copies, rows, HD), BF16),
            jax.ShapeDtypeStruct((rows, 2 * HD), BF16),
        ],
        scratch_shapes=[
            pltpu.VMEM((STEPS, 3, width // STEPS, HD), BF16),
            pltpu.SemaphoreType.DMA((STEPS,)),
        ],
        compiler_params=params(50),
        cost_estimate=pl.CostEstimate(
            flops=2 * rows * width * 3 * HD, bytes_accessed=3 * width * HD * 2, transcendentals=0
        ),
    )(*tokens, gains, weight)


TAIL = 16


def diagonal(rows):
    down = lax.broadcasted_iota(jnp.int32, (rows, HD), 0)
    return down == lax.broadcasted_iota(jnp.int32, (rows, HD), 1)


def row_blocks(rows):
    return [(at, min(HD, rows - at)) for at in range(0, rows, HD)]


def tail_of(rows):
    row_of = lax.broadcasted_iota(jnp.int32, (TAIL, HD), 0)
    tail = jnp.zeros((TAIL, HD), F32)
    for j, row in enumerate(rows):
        high = row.astype(BF16).astype(F32)
        tail = jnp.where(row_of == j, high, tail)
        tail = jnp.where(row_of == len(rows) + j, row - high, tail)
    return tail.astype(BF16)


def totals_of(block, rows):
    count = len(row_blocks(rows))
    starts = [rows + j for j in range(count)]
    return [block[at : at + 1] + block[at + count : at + count + 1] for at in starts]


def attend_kernel(q_ref, kv_ref, out_ref):
    blocks, rows, _ = q_ref.shape
    step = kv_ref.shape[0] // 2

    @pl.loop(0, blocks, step=2)
    def _(first):
        totals = [0.0, 0.0]
        for at in range(0, kv_ref.shape[0], step):
            ones = jnp.ones((step, HD), BF16)
            values = jnp.concatenate([kv_ref[at : at + step, HD:], ones], axis=1)
            for i in range(2):
                scores = lax.dot_general(
                    q_ref[first + i],
                    kv_ref[at : at + step, :HD],
                    (((1,), (1,)), ((), ())),
                    preferred_element_type=F32,
                )
                weights = jnp.exp2(scores).astype(BF16)
                totals[i] += jnp.dot(weights, values, preferred_element_type=F32)
        for i, total in enumerate(totals):
            out_ref[first + i, :rows] = total[:, :HD].astype(BF16)
            sums = [
                jnp.where(diagonal(size), total[at : at + size, HD:], 0.0)
                for at, size in row_blocks(rows)
            ]
            out_ref[first + i, rows:] = tail_of(
                [jnp.sum(square, axis=0, keepdims=True) for square in sums]
            )


def attend(queries, keyval):
    blocks, rows, _ = queries.shape
    keys = keyval.shape[0]
    vmem = pl.BlockSpec(memory_space=pltpu.VMEM)
    return pl.pallas_call(
        attend_kernel,
        in_specs=[vmem, vmem],
        out_specs=vmem,
        out_shape=jax.ShapeDtypeStruct((blocks, rows + TAIL, HD), BF16),
        compiler_params=params(16),
        cost_estimate=pl.CostEstimate(
            flops=4 * blocks * rows * keys * HD,
            bytes_accessed=4 * keys * HD,
            transcendentals=blocks * rows * keys,
        ),
    )(queries, keyval)


def divide_kernel(partial_ref, out_ref):
    rows = partial_ref.shape[1] - TAIL
    summed = jnp.sum(partial_ref[...].astype(F32), axis=0)
    attended = []
    for row, (at, size) in zip(totals_of(summed, rows), row_blocks(rows)):
        square = jnp.broadcast_to(row, (size, HD))
        column = jnp.sum(jnp.where(diagonal(size), square, 0.0), axis=1, keepdims=True)
        attended.append((summed[at : at + size] / column).astype(BF16))
    attended = jnp.concatenate(attended, axis=0)
    along, part = out_ref.shape[0], out_ref.shape[1] // 4
    for y in range(along):
        for far in range(2):
            for other in range(2):
                at = ((other * 2 + far) * along + y) * part
                to = (other * 2 + far) * part
                out_ref[y, to : to + part] = attended[at : at + part]


def divide(partial, along):
    rows = partial.shape[1] - TAIL
    return pl.pallas_call(
        divide_kernel,
        out_shape=jax.ShapeDtypeStruct((along, rows // along, HD), BF16),
        compiler_params=params(8),
    )(partial)


def mix_kernel(y_ref, attended_ref, first_ref, *refs):
    *weight_refs, own_ref, other_ref, first, first_sem = refs
    copy = pltpu.make_async_copy(first_ref, first, first_sem.at[0])
    copy.start()
    attended = jnp.concatenate([attended_ref[y_ref[0] ^ i] for i in range(4)], axis=1)
    half, width = own_ref.shape
    step = width // 4
    copy.wait()
    for at in range(0, width, step):
        weight = [ref[:, at : at + step] for ref in (first, *weight_refs)]
        weight = jnp.concatenate(weight, axis=0)
        mixed = jnp.dot(attended, weight, preferred_element_type=F32)
        own_ref[:, at : at + step] = mixed[:half]
        other_ref[:, at : at + step] = mixed[half:].astype(BF16)


def mix(y, attended, weights):
    rows = attended.shape[1]
    depth, width = weights[0].shape
    vmem = pl.BlockSpec(memory_space=pltpu.VMEM)
    return pl.pallas_call(
        mix_kernel,
        in_specs=[
            pl.BlockSpec(memory_space=pltpu.SMEM),
            vmem,
            pl.BlockSpec(memory_space=pltpu.HBM),
            vmem,
            vmem,
            vmem,
        ],
        out_shape=[
            jax.ShapeDtypeStruct((rows // 2, width), F32),
            jax.ShapeDtypeStruct((rows // 2, width), BF16),
        ],
        scratch_shapes=[pltpu.VMEM((depth, width), BF16), pltpu.SemaphoreType.DMA((1,))],
        compiler_params=params(16),
        cost_estimate=pl.CostEstimate(
            flops=2 * len(weights) * rows * width * depth,
            bytes_accessed=2 * len(weights) * width * depth,
            transcendentals=0,
        ),
    )(y, attended, *weights)


def local(tokens, mod_shift, mod_scale, qkv_weight, q_gain, k_gain, out_weight, out_gate):
    rows, width = tokens.shape

    def along_y(block, distance):
        return lax.ppermute(block, "y", [(i, i ^ distance) for i in range(4)])

    def spread(modulated):
        return lax.all_gather(modulated, "y", axis=0, tiled=True)

    far = trade_halves(tokens)
    near, rows_held = modulate_near(tokens, [mod_shift, mod_scale, q_gain, k_gain])
    far, gains = modulate_far(far, rows_held)
    own = jnp.concatenate([spread(near), spread(far)], axis=0)
    queries, keyval = project([own, swap(own, "core")], gains, qkv_weight, 8)
    out_weight, keyval = lax.optimization_barrier((out_weight, keyval))
    weights = [out_weight] + [along_y(out_weight, i) for i in (1, 2, 3)]
    queries = lax.all_to_all(queries, NEAR, 0, 0)
    one, two = swap(keyval, "za"), swap(keyval, "zb")
    three = swap(one, "zb")
    partial = attend(queries, jnp.concatenate([keyval, one, two, three], axis=0))
    partial, weights[1], weights[3] = lax.optimization_barrier((partial, weights[1], weights[3]))
    partial = lax.all_to_all(partial, NEAR, 0, 0)
    attended = lax.all_to_all(divide(partial, 4), "y", 0, 0)
    y = lax.axis_index("y").astype(jnp.int32).reshape(1)
    own, other = mix(y, attended, weights)
    summed = own + swap(other, "core").astype(F32)
    arrived = trade_halves(summed[rows:].astype(BF16)).astype(F32)
    return ((summed[:rows] + arrived) * out_gate).astype(BF16)


def solution(mesh):
    fine = Mesh(mesh.devices.reshape(tuple(AXES.values())), ALL)
    heads = ("y", "zh", "core")
    return jax.shard_map(
        local,
        mesh=fine,
        in_specs=(
            P(ALL, None),
            P(),
            P(),
            P(None, None, heads),
            P(),
            P(),
            P(heads, None),
            P(),
        ),
        out_specs=P(ALL, None),
        check_vma=False,
    )
```

time: 163 us -> 155 us (0.951); the launches traced: 160 us -> 154 us
  blocking collectives: 38.5 us -> 22.4 us
  starting transfers between devices: 60.5 us -> 75.1 us
  waiting for transfers between devices: 43.7 us -> 40.5 us
  local copies, waits for them, and re-layouts: 2.43 us -> 0.11 us
    all_to_all x1 -> x0, blocking collectives: 14.9 us -> none  [local(): partial = lax.all_to_all(partial, NEAR, 0, 0)]
    ppermute x6 -> x5, waiting for transfers between devices: 22.6 us -> 15.7 us  [swap(): return lax.ppermute(block, axis, [(0, 1), (1, 0)])]
    all_to_all x0 -> x1, starting transfers between devices: none -> 6.6 us  [local(): partial = lax.all_to_all(partial, NEAR, 0, 0)]
    all_to_all x0 -> x1, waiting for transfers between devices: none -> 5.38 us  [local(): partial = lax.all_to_all(partial, NEAR, 0, 0)]
    ppermute x2, starting transfers between devices: 15.3 us -> 20 us  [trade_halves(): return lax.ppermute(block, ('zh', 'za'), [(i, i ^ 3) for i in range(4)])]
    all_to_all x1, waiting for transfers between devices: 4.61 us -> 1.05 us  [local(): attended = lax.all_to_all(divide(partial, 4), 'y', 0, 0)]
    ppermute x6 -> x5, starting transfers between devices: 27.3 us -> 30 us  [swap(): return lax.ppermute(block, axis, [(0, 1), (1, 0)])]
    ppermute x3, waiting for transfers between devices: 3.48 us -> 6.16 us  [along_y(): return lax.ppermute(block, 'y', [(i, i ^ distance) for i in range(4)])]
  transfers between devices with their start and end apart: 13 -> 13, of which waited for: 8 -> 8; matrix products, arithmetic and copies ran while one was open for 0% -> 0% of each run, Pallas kernels for 5% -> 6%
where the time goes in v5:
time: 155 us; the launch traced here: 154 us
  starting transfers between devices  75.1 us (48%)
  waiting for transfers between devices  40.5 us (26%)
  blocking collectives  22.4 us (14%)
  Pallas kernels  15.3 us (10%)
    ppermute x5, starting transfers between devices, swap(): return lax.ppermute(block, axis, [(0, 1), (1, 0)])  30 us
    all_gather x2, blocking collectives, spread(): return lax.all_gather(modulated, 'y', axis=0, tiled=True)  22.4 us
    ppermute x2, starting transfers between devices, trade_halves(): return lax.ppermute(block, ('zh', 'za'), [(i, i ^ 3) for i in range(4)])  20 us
    ppermute x5, waiting for transfers between devices, swap(): return lax.ppermute(block, axis, [(0, 1), (1, 0)])  15.7 us
    ppermute x2, waiting for transfers between devices, trade_halves(): return lax.ppermute(block, ('zh', 'za'), [(i, i ^ 3) for i in range(4)])  12.2 us
    ppermute x3, starting transfers between devices, along_y(): return lax.ppermute(block, 'y', [(i, i ^ distance) for i in range(4)])  10.1 us
    all_to_all x1, starting transfers between devices, local(): partial = lax.all_to_all(partial, NEAR, 0, 0)  6.6 us
    pallas_call x1, Pallas kernels, attend(): pl.pallas_call(attend_kernel, in_specs=[vmem, vmem], out_specs=vmem, out_...  6.45 us
  transfers between devices with their start and end apart: 13, of which 8 were waited for; matrix products, arithmetic and copies ran while one was open for 0% of the time, Pallas kernels for 6%

profile of v5, /device:TPU:1, one launch (start us, length us, event | category | flops | bytes accessed | tf_op | source)
XLA Modules:
  0.0 154.4 jit_solution(10611523355782986708)
XLA Ops:
  0.0 13.3 %collective-permute-start = (bf16[24,3072]{1,0:T(8,128)(2,1)}, bf16[24,3072]{1,0:T(8,128)(2,1)S(1)}, u32[]{:S(2)}, u32[]{:S(2)}) collective-permute-start(bf16[24,3072]{1,0:T(8,128)(2,1)} %tokens_ref.1), channel_id=1, source_target_pairs={{0,80},{16,64},{64,16},{80,0},{1,81},{17,65},{65,17},{81,1},{2,82}... | collective-permute-start | bytes 442376 | tf_op jit(solution)/shard_map/ppermute | solution.py:29
  13.3 1.9 %shard_map.82 = (bf16[24,3072]{1,0:T(8,128)(2,1)}, f32[4,1,3072]{2,1,0:T(1,128)}) custom-call(bf16[24,3072]{1,0:T(8,128)(2,1)} %tokens_ref.1, f32[1,3072]{1,0:T(1,128)} %bitcast.5, f32[1,3072]{1,0:T(1,128)} %bitcast.6, f32[1,128]{1,0:T(1,128)} %bitcast.7, f32[1,128]{1,0:T(1,128)} %bitcast.8), custom_call_target="tpu_custom_call" | custom-call | tf_op jit(solution)/shard_map/pallas_call | solution.py:56
  15.2 0.0 copy-start.1
  15.2 12.3 %all_gather.6 = bf16[96,3072]{1,0:T(8,128)(2,1)S(1)} all-gather(bf16[24,3072]{1,0:T(8,128)(2,1)} %get-tuple-element.18), channel_id=1, replica_groups=mesh['y'=4,'zh'=2,'core'=2,'za'=2,'zb'=2,'zc'=2,'x'=4] {'y'}, dimensions={0}, use_global_device_ids=true | all-gather | bytes 737280 | tf_op jit(solution)/shard_map/all_gather | solution.py:299
  27.6 0.0 collective-permute-done.tokens_ref
  27.6 0.0 copy-done.1
  27.6 0.3 shard_map.83
  27.9 10.0 %all_gather.7 = bf16[96,3072]{1,0:T(8,128)(2,1)S(1)} all-gather(bf16[24,3072]{1,0:T(8,128)(2,1)S(1)} %get-tuple-element.20), channel_id=1, replica_groups=mesh['y'=4,'zh'=2,'core'=2,'za'=2,'zb'=2,'zc'=2,'x'=4] {'y'}, dimensions={0}, use_global_device_ids=true | all-gather | bytes 737280 | tf_op jit(solution)/shard_map/all_gather | solution.py:299
  38.0 7.6 %collective-permute-start.1 = (bf16[192,3072]{1,0:T(8,128)(2,1)S(1)}, bf16[192,3072]{1,0:T(8,128)(2,1)S(1)}, u32[]{:S(2)}, u32[]{:S(2)}) collective-permute-start(bf16[192,3072]{1,0:T(8,128)(2,1)S(1)} %constant_dynamic-update-slice_fusion.refs_0_), channel_id=1, source_target_pairs={{0,32},{32,0},{1,33},{33,1},{2,34},{34,2},{3,35},{35,3},{4,36},{36... | collective-permute-start | bytes 3538952 | tf_op jit(solution)/shard_map/ppermute | solution.py:25
  45.5 2.5 %collective-permute-done.1.refs_1_ = bf16[192,3072]{1,0:T(8,128)(2,1)S(1)} collective-permute-done((bf16[192,3072]{1,0:T(8,128)(2,1)S(1)}, bf16[192,3072]{1,0:T(8,128)(2,1)S(1)}, u32[]{:S(2)}, u32[]{:S(2)}) %collective-permute-start.1) | collective-permute-done | bytes 1179680 | tf_op jit(solution)/shard_map/ppermute | solution.py:25
  48.0 3.8 %shard_map.84 = (bf16[8,384,128]{2,1,0:T(8,128)(2,1)}, bf16[384,256]{1,0:T(8,128)(2,1)S(1)}) custom-call(bf16[192,3072]{1,0:T(8,128)(2,1)S(1)} %constant_dynamic-update-slice_fusion.refs_0_, bf16[192,3072]{1,0:T(8,128)(2,1)S(1)} %collective-permute-done.1.refs_1_, f32[2,1,128]{2,1,0:T(1,128)S(1)} %get-tuple-element.21.refs_2_, bf16[3,3072,128]{2,1,0:T(8,128)(2,1)} %refs_3_.1), custom_call_target="tpu_custom_call" | custom-call | flops 905969664 | bytes 2359296 | tf_op jit(solution)/shard_map/pallas_call | solution.py:126
  51.8 0.0 copy-start
  51.8 4.6 %all-to-all-start = ((bf16[8,384,128]{2,1,0:T(8,128)(2,1)}), bf16[8,384,128]{2,1,0:T(8,128)(2,1)S(1)}, u32[]{:S(2)}, u32[]{:S(2)}) async-start(bf16[8,384,128]{2,1,0:T(8,128)(2,1)} %get-tuple-element.22), calls=%async_computation | async-start | bytes 1572864 | tf_op jit(solution)/shard_map/all_to_all | solution.py:308
  56.4 5.1 %collective-permute-start.2 = (bf16[384,256]{1,0:T(8,128)(2,1)S(1)}, bf16[384,256]{1,0:T(8,128)(2,1)S(1)}, u32[]{:S(2)}, u32[]{:S(2)}) collective-permute-start(bf16[384,256]{1,0:T(8,128)(2,1)S(1)} %get-tuple-element.24), channel_id=1, source_target_pairs={{0,16},{16,0},{1,17},{17,1},{2,18},{18,2},{3,19},{19,3},{4,20},{20... | collective-permute-start | bytes 589832 | tf_op jit(solution)/shard_map/ppermute | solution.py:25
  61.5 0.0 copy-done
  61.5 3.9 %collective-permute-start.5 = (bf16[128,3072]{1,0:T(8,128)(2,1)S(1)}, bf16[128,3072]{1,0:T(8,128)(2,1)S(1)}, u32[]{:S(2)}, u32[]{:S(2)}) collective-permute-start(bf16[128,3072]{1,0:T(8,128)(2,1)S(1)} %copy-done), channel_id=1, source_target_pairs={{0,128},{128,0},{256,384},{384,256},{1,129},{129,1},{257,385},{385... | collective-permute-start | bytes 2359304 | tf_op jit(solution)/shard_map/ppermute | solution.py:296
  65.4 3.1 %collective-permute-start.6 = (bf16[128,3072]{1,0:T(8,128)(2,1)S(1)}, bf16[128,3072]{1,0:T(8,128)(2,1)}, u32[]{:S(2)}, u32[]{:S(2)}) collective-permute-start(bf16[128,3072]{1,0:T(8,128)(2,1)S(1)} %copy-done), channel_id=1, source_target_pairs={{0,384},{128,256},{256,128},{384,0},{1,385},{129,257},{257,129},{3... | collective-permute-start | bytes 2359304 | tf_op jit(solution)/shard_map/ppermute | solution.py:296
  68.6 2.7 %collective-permute-start.3 = (bf16[384,256]{1,0:T(8,128)(2,1)S(1)}, bf16[384,256]{1,0:T(8,128)(2,1)S(1)}, u32[]{:S(2)}, u32[]{:S(2)}) collective-permute-start(bf16[384,256]{1,0:T(8,128)(2,1)S(1)} %get-tuple-element.24), channel_id=1, source_target_pairs={{0,8},{8,0},{1,9},{9,1},{2,10},{10,2},{3,11},{11,3},{4,12},{12,4},... | collective-permute-start | bytes 589832 | tf_op jit(solution)/shard_map/ppermute | solution.py:25
  71.3 5.1 %collective-permute-done.2 = bf16[384,256]{1,0:T(8,128)(2,1)S(1)} collective-permute-done((bf16[384,256]{1,0:T(8,128)(2,1)S(1)}, bf16[384,256]{1,0:T(8,128)(2,1)S(1)}, u32[]{:S(2)}, u32[]{:S(2)}) %collective-permute-start.2) | collective-permute-done | bytes 196640 | tf_op jit(solution)/shard_map/ppermute | solution.py:25
  76.4 8.5 %collective-permute-start.4 = (bf16[384,256]{1,0:T(8,128)(2,1)S(1)}, bf16[384,256]{1,0:T(8,128)(2,1)S(1)}, u32[]{:S(2)}, u32[]{:S(2)}) collective-permute-start(bf16[384,256]{1,0:T(8,128)(2,1)S(1)} %collective-permute-done.2), channel_id=1, source_target_pairs={{0,8},{8,0},{1,9},{9,1},{2,10},{10,2},{3,11},{11,3},{4,12},{12,4},... | collective-permute-start | bytes 589832 | tf_op jit(solution)/shard_map/ppermute | solution.py:25
  84.9 0.0 collective-permute-done.3
  84.9 7.0 %collective-permute-done.4 = bf16[384,256]{1,0:T(8,128)(2,1)S(1)} collective-permute-done((bf16[384,256]{1,0:T(8,128)(2,1)S(1)}, bf16[384,256]{1,0:T(8,128)(2,1)S(1)}, u32[]{:S(2)}, u32[]{:S(2)}) %collective-permute-start.4) | collective-permute-done | bytes 196640 | tf_op jit(solution)/shard_map/ppermute | solution.py:25
  91.9 0.1 pad_maximum_fusion.kv_ref
  92.0 0.0 all-to-all-done.q_ref
  92.0 6.5 %shard_map.85 = bf16[8,400,128]{2,1,0:T(8,128)(2,1)} custom-call(bf16[8,384,128]{2,1,0:T(8,128)(2,1)S(1)} %all-to-all-done.q_ref, bf16[1536,256]{1,0:T(8,128)(2,1)S(1)} %pad_maximum_fusion.kv_ref), custom_call_target="tpu_custom_call" | custom-call | flops 2415919104 | bytes 786432 | tf_op jit(solution)/shard_map/pallas_call | solution.py:207
  98.4 0.0 collective-permute-done.5.refs_0_
  98.4 0.0 collective-permute-done.6.refs_2_
  98.4 6.6 %all-to-all-start.1 = ((bf16[8,400,128]{2,1,0:T(8,128)(2,1)}), bf16[8,400,128]{2,1,0:T(8,128)(2,1)S(1)}, u32[]{:S(2)}, u32[]{:S(2)}) async-start(bf16[8,400,128]{2,1,0:T(8,128)(2,1)} %shard_map.85), calls=%async_computation.1 | async-start | bytes 1638400 | tf_op jit(solution)/shard_map/all_to_all | solution.py:313
  105.0 3.1 %collective-permute-start.7 = (bf16[128,3072]{1,0:T(8,128)(2,1)S(1)}, bf16[128,3072]{1,0:T(8,128)(2,1)}, u32[]{:S(2)}, u32[]{:S(2)}) collective-permute-start(bf16[128,3072]{1,0:T(8,128)(2,1)S(1)} %copy-done), channel_id=1, source_target_pairs={{0,256},{128,384},{256,0},{384,128},{1,257},{129,385},{257,1},{385... | collective-permute-start | bytes 2359304 | tf_op jit(solution)/shard_map/ppermute | solution.py:296
  108.1 5.4 %all-to-all-done.1.partial_ref = bf16[8,400,128]{2,1,0:T(8,128)(2,1)S(1)} async-done(((bf16[8,400,128]{2,1,0:T(8,128)(2,1)}), bf16[8,400,128]{2,1,0:T(8,128)(2,1)S(1)}, u32[]{:S(2)}, u32[]{:S(2)}) %all-to-all-start.1) | async-done | bytes 819232 | tf_op jit(solution)/shard_map/all_to_all | solution.py:313
  113.5 0.8 shard_map.86
  114.3 3.7 %all-to-all-start.2 = ((bf16[4,96,128]{2,1,0:T(8,128)(2,1)}), bf16[4,96,128]{2,1,0:T(8,128)(2,1)S(1)}, u32[]{:S(2)}, u32[]{:S(2)}) async-start(bf16[4,96,128]{2,1,0:T(8,128)(2,1)} %shard_map.86), calls=%async_computation.2 | async-start | bytes 196608 | tf_op jit(solution)/shard_map/all_to_all | solution.py:314
  118.0 6.2 %collective-permute-done.7.refs_1_ = bf16[128,3072]{1,0:T(8,128)(2,1)} collective-permute-done((bf16[128,3072]{1,0:T(8,128)(2,1)S(1)}, bf16[128,3072]{1,0:T(8,128)(2,1)}, u32[]{:S(2)}, u32[]{:S(2)}) %collective-permute-start.7) | collective-permute-done | bytes 786464 | tf_op jit(solution)/shard_map/ppermute | solution.py:296
  124.2 1.1 all-to-all-done.2.attended_ref
  125.2 2.1 %shard_map.87 = (f32[48,3072]{1,0:T(8,128)S(1)}, bf16[48,3072]{1,0:T(8,128)(2,1)S(1)}) custom-call(s32[1]{0:T(128)} %bitcast.y_ref, bf16[4,96,128]{2,1,0:T(8,128)(2,1)S(1)} %all-to-all-done.2.attended_ref, bf16[128,3072]{1,0:T(8,128)(2,1)S(1)} %copy-done, bf16[128,3072]{1,0:T(8,128)(2,1)S(1)} %collective-permute-done.5.refs_0_, ...), custom_call_target="tpu_custom_call" | custom-call | flops 301989888 | bytes 3145728 | tf_op jit(solution)/shard_map/pallas_call | solution.py:268
  127.3 0.0 copy-start.2
  127.3 6.2 %collective-permute-start.8 = (bf16[48,3072]{1,0:T(8,128)(2,1)S(1)}, bf16[48,3072]{1,0:T(8,128)(2,1)S(1)}, u32[]{:S(2)}, u32[]{:S(2)}) collective-permute-start(bf16[48,3072]{1,0:T(8,128)(2,1)S(1)} %get-tuple-element.30), channel_id=1, source_target_pairs={{0,32},{32,0},{1,33},{33,1},{2,34},{34,2},{3,35},{35,3},{4,36},{36... | collective-permute-start | bytes 884744 | tf_op jit(solution)/shard_map/ppermute | solution.py:25
  133.5 1.2 collective-permute-done.8
  134.7 0.1 convert_add_fusion
  134.7 6.8 %collective-permute-start.9 = (bf16[24,3072]{1,0:T(8,128)(2,1)S(1)}, bf16[24,3072]{1,0:T(8,128)(2,1)S(1)}, u32[]{:S(2)}, u32[]{:S(2)}) collective-permute-start(bf16[24,3072]{1,0:T(8,128)(2,1)S(1)} %slice.17), channel_id=1, source_target_pairs={{0,80},{16,64},{64,16},{80,0},{1,81},{17,65},{65,17},{81,1},{2,82}... | collective-permute-start | bytes 442376 | tf_op jit(solution)/shard_map/ppermute | solution.py:29
  141.5 12.2 %collective-permute-done.9 = bf16[24,3072]{1,0:T(8,128)(2,1)S(1)} collective-permute-done((bf16[24,3072]{1,0:T(8,128)(2,1)S(1)}, bf16[24,3072]{1,0:T(8,128)(2,1)S(1)}, u32[]{:S(2)}, u32[]{:S(2)}) %collective-permute-start.9) | collective-permute-done | bytes 147488 | tf_op jit(solution)/shard_map/ppermute | solution.py:29
  153.7 0.0 copy-done.2
  153.7 0.7 fusion.1
  (3 shorter events, 0.1 us)
Async XLA Ops:
  0.0 27.6 %collective-permute-start = (bf16[24,3072]{1,0:T(8,128)(2,1)}, bf16[24,3072]{1,0:T(8,128)(2,1)S(1)}, u32[]{:S(2)}, u32[]{:S(2)}) collective-permute-start(bf16[24,3072]{1,0:T(8,128)(2,1)} %tokens_ref.1), channel_id=1, source_target_pairs={{0,80},{16,64},{64,16},{80,0},{1,81},{17,65},{65,17},{81,1},{2,82}... | collective-permute-start | bytes 442376 | tf_op jit(solution)/shard_map/ppermute | solution.py:29
  15.2 12.4 %copy-start.1 = (f32[4,1,3072]{2,1,0:T(1,128)S(1)}, f32[4,1,3072]{2,1,0:T(1,128)}, u32[]{:S(2)}) copy-start(f32[4,1,3072]{2,1,0:T(1,128)} %get-tuple-element.19.rows_ref) | copy-start | bytes 147460
  38.0 10.0 %collective-permute-start.1 = (bf16[192,3072]{1,0:T(8,128)(2,1)S(1)}, bf16[192,3072]{1,0:T(8,128)(2,1)S(1)}, u32[]{:S(2)}, u32[]{:S(2)}) collective-permute-start(bf16[192,3072]{1,0:T(8,128)(2,1)S(1)} %constant_dynamic-update-slice_fusion.refs_0_), channel_id=1, source_target_pairs={{0,32},{32,0},{1,33},{33,1},{2,34},{34,2},{3,35},{35,3},{4,36},{36... | collective-permute-start | bytes 3538952 | tf_op jit(solution)/shard_map/ppermute | solution.py:25
  51.8 9.7 %copy-start = (bf16[128,3072]{1,0:T(8,128)(2,1)S(1)}, bf16[128,3072]{1,0:T(8,128)(2,1)}, u32[]{:S(2)}) copy-start(bf16[128,3072]{1,0:T(8,128)(2,1)} %first_ref) | copy-start | bytes 2359300
  51.8 40.1 %all-to-all-start = ((bf16[8,384,128]{2,1,0:T(8,128)(2,1)}), bf16[8,384,128]{2,1,0:T(8,128)(2,1)S(1)}, u32[]{:S(2)}, u32[]{:S(2)}) async-start(bf16[8,384,128]{2,1,0:T(8,128)(2,1)} %get-tuple-element.22), calls=%async_computation | async-start | bytes 1572864 | tf_op jit(solution)/shard_map/all_to_all | solution.py:308
  56.4 20.1 %collective-permute-start.2 = (bf16[384,256]{1,0:T(8,128)(2,1)S(1)}, bf16[384,256]{1,0:T(8,128)(2,1)S(1)}, u32[]{:S(2)}, u32[]{:S(2)}) collective-permute-start(bf16[384,256]{1,0:T(8,128)(2,1)S(1)} %get-tuple-element.24), channel_id=1, source_target_pairs={{0,16},{16,0},{1,17},{17,1},{2,18},{18,2},{3,19},{19,3},{4,20},{20... | collective-permute-start | bytes 589832 | tf_op jit(solution)/shard_map/ppermute | solution.py:25
  61.5 36.9 %collective-permute-start.5 = (bf16[128,3072]{1,0:T(8,128)(2,1)S(1)}, bf16[128,3072]{1,0:T(8,128)(2,1)S(1)}, u32[]{:S(2)}, u32[]{:S(2)}) collective-permute-start(bf16[128,3072]{1,0:T(8,128)(2,1)S(1)} %copy-done), channel_id=1, source_target_pairs={{0,128},{128,0},{256,384},{384,256},{1,129},{129,1},{257,385},{385... | collective-permute-start | bytes 2359304 | tf_op jit(solution)/shard_map/ppermute | solution.py:296
  65.4 33.0 %collective-permute-start.6 = (bf16[128,3072]{1,0:T(8,128)(2,1)S(1)}, bf16[128,3072]{1,0:T(8,128)(2,1)}, u32[]{:S(2)}, u32[]{:S(2)}) collective-permute-start(bf16[128,3072]{1,0:T(8,128)(2,1)S(1)} %copy-done), channel_id=1, source_target_pairs={{0,384},{128,256},{256,128},{384,0},{1,385},{129,257},{257,129},{3... | collective-permute-start | bytes 2359304 | tf_op jit(solution)/shard_map/ppermute | solution.py:296
  68.6 16.4 %collective-permute-start.3 = (bf16[384,256]{1,0:T(8,128)(2,1)S(1)}, bf16[384,256]{1,0:T(8,128)(2,1)S(1)}, u32[]{:S(2)}, u32[]{:S(2)}) collective-permute-start(bf16[384,256]{1,0:T(8,128)(2,1)S(1)} %get-tuple-element.24), channel_id=1, source_target_pairs={{0,8},{8,0},{1,9},{9,1},{2,10},{10,2},{3,11},{11,3},{4,12},{12,4},... | collective-permute-start | bytes 589832 | tf_op jit(solution)/shard_map/ppermute | solution.py:25
  76.4 15.5 %collective-permute-start.4 = (bf16[384,256]{1,0:T(8,128)(2,1)S(1)}, bf16[384,256]{1,0:T(8,128)(2,1)S(1)}, u32[]{:S(2)}, u32[]{:S(2)}) collective-permute-start(bf16[384,256]{1,0:T(8,128)(2,1)S(1)} %collective-permute-done.2), channel_id=1, source_target_pairs={{0,8},{8,0},{1,9},{9,1},{2,10},{10,2},{3,11},{11,3},{4,12},{12,4},... | collective-permute-start | bytes 589832 | tf_op jit(solution)/shard_map/ppermute | solution.py:25
  98.4 15.1 %all-to-all-start.1 = ((bf16[8,400,128]{2,1,0:T(8,128)(2,1)}), bf16[8,400,128]{2,1,0:T(8,128)(2,1)S(1)}, u32[]{:S(2)}, u32[]{:S(2)}) async-start(bf16[8,400,128]{2,1,0:T(8,128)(2,1)} %shard_map.85), calls=%async_computation.1 | async-start | bytes 1638400 | tf_op jit(solution)/shard_map/all_to_all | solution.py:313
  105.0 19.1 %collective-permute-start.7 = (bf16[128,3072]{1,0:T(8,128)(2,1)S(1)}, bf16[128,3072]{1,0:T(8,128)(2,1)}, u32[]{:S(2)}, u32[]{:S(2)}) collective-permute-start(bf16[128,3072]{1,0:T(8,128)(2,1)S(1)} %copy-done), channel_id=1, source_target_pairs={{0,256},{128,384},{256,0},{384,128},{1,257},{129,385},{257,1},{385... | collective-permute-start | bytes 2359304 | tf_op jit(solution)/shard_map/ppermute | solution.py:296
  114.3 10.9 %all-to-all-start.2 = ((bf16[4,96,128]{2,1,0:T(8,128)(2,1)}), bf16[4,96,128]{2,1,0:T(8,128)(2,1)S(1)}, u32[]{:S(2)}, u32[]{:S(2)}) async-start(bf16[4,96,128]{2,1,0:T(8,128)(2,1)} %shard_map.86), calls=%async_computation.2 | async-start | bytes 196608 | tf_op jit(solution)/shard_map/all_to_all | solution.py:314
  127.3 26.4 %copy-start.2 = (f32[3072]{0:T(1024)S(1)}, f32[3072]{0:T(1024)}, u32[]{:S(2)}) copy-start(f32[3072]{0:T(1024)} %param.15) | copy-start | bytes 36868
  127.3 7.4 %collective-permute-start.8 = (bf16[48,3072]{1,0:T(8,128)(2,1)S(1)}, bf16[48,3072]{1,0:T(8,128)(2,1)S(1)}, u32[]{:S(2)}, u32[]{:S(2)}) collective-permute-start(bf16[48,3072]{1,0:T(8,128)(2,1)S(1)} %get-tuple-element.30), channel_id=1, source_target_pairs={{0,32},{32,0},{1,33},{33,1},{2,34},{34,2},{3,35},{35,3},{4,36},{36... | collective-permute-start | bytes 884744 | tf_op jit(solution)/shard_map/ppermute | solution.py:25
  134.7 18.9 %collective-permute-start.9 = (bf16[24,3072]{1,0:T(8,128)(2,1)S(1)}, bf16[24,3072]{1,0:T(8,128)(2,1)S(1)}, u32[]{:S(2)}, u32[]{:S(2)}) collective-permute-start(bf16[24,3072]{1,0:T(8,128)(2,1)S(1)} %slice.17), channel_id=1, source_target_pairs={{0,80},{16,64},{64,16},{80,0},{1,81},{17,65},{65,17},{81,1},{2,82}... | collective-permute-start | bytes 442376 | tf_op jit(solution)/shard_map/ppermute | solution.py:29

commit v6 on v5

--- a/solution.py
+++ b/solution.py
@@ -249,7 +249,7 @@
     *weight_refs, own_ref, other_ref, first, first_sem = refs
     copy = pltpu.make_async_copy(first_ref, first, first_sem.at[0])
     copy.start()
-    attended = jnp.concatenate([attended_ref[y_ref[0] ^ i] for i in range(4)], axis=1)
+    attended = jnp.concatenate([attended_ref[y_ref[0] ^ i] for i in (0, 1, 3, 2)], axis=1)
     half, width = own_ref.shape
     step = width // 4
     copy.wait()
@@ -271,10 +271,8 @@
             pl.BlockSpec(memory_space=pltpu.SMEM),
             vmem,
             pl.BlockSpec(memory_space=pltpu.HBM),
-            vmem,
-            vmem,
-            vmem,
-        ],
+        ]
+        + [vmem] * (len(weights) - 1),
         out_shape=[
             jax.ShapeDtypeStruct((rows // 2, width), F32),
             jax.ShapeDtypeStruct((rows // 2, width), BF16),
@@ -282,8 +280,8 @@
         scratch_shapes=[pltpu.VMEM((depth, width), BF16), pltpu.SemaphoreType.DMA((1,))],
         compiler_params=params(16),
         cost_estimate=pl.CostEstimate(
-            flops=2 * len(weights) * rows * width * depth,
-            bytes_accessed=2 * len(weights) * width * depth,
+            flops=8 * rows * width * depth,
+            bytes_accessed=8 * width * depth,
             transcendentals=0,
         ),
     )(y, attended, *weights)
@@ -304,16 +302,18 @@
     own = jnp.concatenate([spread(near), spread(far)], axis=0)
     queries, keyval = project([own, swap(own, "core")], gains, qkv_weight, 8)
     out_weight, keyval = lax.optimization_barrier((out_weight, keyval))
-    weights = [out_weight] + [along_y(out_weight, i) for i in (1, 2, 3)]
+    half = out_weight.shape[0] // 2
+    weights = [along_y(out_weight, i) for i in (1, 3)]
+    weights += [along_y(out_weight[:half], 2), along_y(out_weight[half:], 2)]
     queries = lax.all_to_all(queries, NEAR, 0, 0)
     one, two = swap(keyval, "za"), swap(keyval, "zb")
     three = swap(one, "zb")
     partial = attend(queries, jnp.concatenate([keyval, one, two, three], axis=0))
-    partial, weights[1], weights[3] = lax.optimization_barrier((partial, weights[1], weights[3]))
+    partial, *weights[:3] = lax.optimization_barrier((partial, *weights[:3]))
     partial = lax.all_to_all(partial, NEAR, 0, 0)
     attended = lax.all_to_all(divide(partial, 4), "y", 0, 0)
     y = lax.axis_index("y").astype(jnp.int32).reshape(1)
-    own, other = mix(y, attended, weights)
+    own, other = mix(y, attended, [out_weight, *weights])
     summed = own + swap(other, "core").astype(F32)
     arrived = trade_halves(summed[rows:].astype(BF16)).astype(F32)
     return ((summed[:rows] + arrived) * out_gate).astype(BF16)

time: 155 us -> 156 us (level)
  waiting for transfers between devices: 40.5 us -> 33.8 us
  starting transfers between devices: 75.1 us -> 81.2 us
    ppermute x3 -> x4, waiting for transfers between devices: 6.16 us -> 0.76 us  [along_y(): return lax.ppermute(block, 'y', [(i, i ^ distance) for i in range(4)])]
    ppermute x5, waiting for transfers between devices: 15.7 us -> 10.5 us  [swap(): return lax.ppermute(block, axis, [(0, 1), (1, 0)])]
    ppermute x5, starting transfers between devices: 30 us -> 33.7 us  [swap(): return lax.ppermute(block, axis, [(0, 1), (1, 0)])]
    all_to_all x1, waiting for transfers between devices: 1.05 us -> 4.65 us  [local(): attended = lax.all_to_all(divide(partial, 4), 'y', 0, 0)]
    ppermute x3 -> x4, starting transfers between devices: 10.1 us -> 12.7 us  [along_y(): return lax.ppermute(block, 'y', [(i, i ^ distance) for i in range(4)])]
  transfers between devices with their start and end apart: 13 -> 14, of which waited for: 8 -> 8; matrix products, arithmetic and copies ran while one was open for 0% -> 1% of each run, Pallas kernels for 6% -> 6%
where the time goes in v6:
time: 156 us; the launch traced here: 155 us
  starting transfers between devices  81.2 us (52%)
  waiting for transfers between devices  33.8 us (22%)
  blocking collectives  22.4 us (14%)
  Pallas kernels  15.2 us (10%)
    ppermute x5, starting transfers between devices, swap(): return lax.ppermute(block, axis, [(0, 1), (1, 0)])  33.7 us
    all_gather x2, blocking collectives, spread(): return lax.all_gather(modulated, 'y', axis=0, tiled=True)  22.4 us
    ppermute x2, starting transfers between devices, trade_halves(): return lax.ppermute(block, ('zh', 'za'), [(i, i ^ 3) for i in range(4)])  18.6 us
    ppermute x4, starting transfers between devices, along_y(): return lax.ppermute(block, 'y', [(i, i ^ distance) for i in range(4)])  12.7 us
    ppermute x2, waiting for transfers between devices, trade_halves(): return lax.ppermute(block, ('zh', 'za'), [(i, i ^ 3) for i in range(4)])  12.5 us
    ppermute x5, waiting for transfers between devices, swap(): return lax.ppermute(block, axis, [(0, 1), (1, 0)])  10.5 us
    all_to_all x1, starting transfers between devices, local(): partial = lax.all_to_all(partial, NEAR, 0, 0)  7.16 us
    pallas_call x1, Pallas kernels, attend(): pl.pallas_call(attend_kernel, in_specs=[vmem, vmem], out_specs=vmem, out_...  6.46 us
  transfers between devices with their start and end apart: 14, of which 8 were waited for; matrix products, arithmetic and copies ran while one was open for 1% of the time, Pallas kernels for 6%

profile of v6, /device:TPU:1, one launch (start us, length us, event | category | flops | bytes accessed | tf_op | source)
XLA Modules:
  0.0 154.7 jit_solution(4530183674698080510)
XLA Ops:
  0.0 13.3 %collective-permute-start = (bf16[24,3072]{1,0:T(8,128)(2,1)}, bf16[24,3072]{1,0:T(8,128)(2,1)S(1)}, u32[]{:S(2)}, u32[]{:S(2)}) collective-permute-start(bf16[24,3072]{1,0:T(8,128)(2,1)} %tokens_ref.1), channel_id=1, source_target_pairs={{0,80},{16,64},{64,16},{80,0},{1,81},{17,65},{65,17},{81,1},{2,82}... | collective-permute-start | bytes 442376 | tf_op jit(solution)/shard_map/ppermute | solution.py:29
  13.3 1.9 %shard_map.82 = (bf16[24,3072]{1,0:T(8,128)(2,1)}, f32[4,1,3072]{2,1,0:T(1,128)}) custom-call(bf16[24,3072]{1,0:T(8,128)(2,1)} %tokens_ref.1, f32[1,3072]{1,0:T(1,128)} %bitcast.5, f32[1,3072]{1,0:T(1,128)} %bitcast.6, f32[1,128]{1,0:T(1,128)} %bitcast.7, f32[1,128]{1,0:T(1,128)} %bitcast.8), custom_call_target="tpu_custom_call" | custom-call | tf_op jit(solution)/shard_map/pallas_call | solution.py:56
  15.2 0.0 copy-start.1
  15.2 12.3 %all_gather.6 = bf16[96,3072]{1,0:T(8,128)(2,1)S(1)} all-gather(bf16[24,3072]{1,0:T(8,128)(2,1)} %get-tuple-element.19), channel_id=1, replica_groups=mesh['y'=4,'zh'=2,'core'=2,'za'=2,'zb'=2,'zc'=2,'x'=4] {'y'}, dimensions={0}, use_global_device_ids=true | all-gather | bytes 737280 | tf_op jit(solution)/shard_map/all_gather | solution.py:297
  27.6 0.0 collective-permute-done.tokens_ref
  27.6 0.0 copy-done.1
  27.6 0.3 shard_map.83
  27.9 10.0 %all_gather.7 = bf16[96,3072]{1,0:T(8,128)(2,1)S(1)} all-gather(bf16[24,3072]{1,0:T(8,128)(2,1)S(1)} %get-tuple-element.21), channel_id=1, replica_groups=mesh['y'=4,'zh'=2,'core'=2,'za'=2,'zb'=2,'zc'=2,'x'=4] {'y'}, dimensions={0}, use_global_device_ids=true | all-gather | bytes 737280 | tf_op jit(solution)/shard_map/all_gather | solution.py:297
  38.0 7.6 %collective-permute-start.1 = (bf16[192,3072]{1,0:T(8,128)(2,1)S(1)}, bf16[192,3072]{1,0:T(8,128)(2,1)S(1)}, u32[]{:S(2)}, u32[]{:S(2)}) collective-permute-start(bf16[192,3072]{1,0:T(8,128)(2,1)S(1)} %constant_dynamic-update-slice_fusion.refs_0_), channel_id=1, source_target_pairs={{0,32},{32,0},{1,33},{33,1},{2,34},{34,2},{3,35},{35,3},{4,36},{36... | collective-permute-start | bytes 3538952 | tf_op jit(solution)/shard_map/ppermute | solution.py:25
  45.5 2.5 %collective-permute-done.1.refs_1_ = bf16[192,3072]{1,0:T(8,128)(2,1)S(1)} collective-permute-done((bf16[192,3072]{1,0:T(8,128)(2,1)S(1)}, bf16[192,3072]{1,0:T(8,128)(2,1)S(1)}, u32[]{:S(2)}, u32[]{:S(2)}) %collective-permute-start.1) | collective-permute-done | bytes 1179680 | tf_op jit(solution)/shard_map/ppermute | solution.py:25
  48.0 3.8 %shard_map.84 = (bf16[8,384,128]{2,1,0:T(8,128)(2,1)}, bf16[384,256]{1,0:T(8,128)(2,1)S(1)}) custom-call(bf16[192,3072]{1,0:T(8,128)(2,1)S(1)} %constant_dynamic-update-slice_fusion.refs_0_, bf16[192,3072]{1,0:T(8,128)(2,1)S(1)} %collective-permute-done.1.refs_1_, f32[2,1,128]{2,1,0:T(1,128)S(1)} %get-tuple-element.22.refs_2_, bf16[3,3072,128]{2,1,0:T(8,128)(2,1)} %refs_3_.1), custom_call_target="tpu_custom_call" | custom-call | flops 905969664 | bytes 2359296 | tf_op jit(solution)/shard_map/pallas_call | solution.py:126
  51.8 0.0 copy-start
  51.8 4.6 %all-to-all-start = ((bf16[8,384,128]{2,1,0:T(8,128)(2,1)}), bf16[8,384,128]{2,1,0:T(8,128)(2,1)S(1)}, u32[]{:S(2)}, u32[]{:S(2)}) async-start(bf16[8,384,128]{2,1,0:T(8,128)(2,1)} %get-tuple-element.23), calls=%async_computation | async-start | bytes 1572864 | tf_op jit(solution)/shard_map/all_to_all | solution.py:308
  56.4 5.1 %collective-permute-start.2 = (bf16[384,256]{1,0:T(8,128)(2,1)S(1)}, bf16[384,256]{1,0:T(8,128)(2,1)S(1)}, u32[]{:S(2)}, u32[]{:S(2)}) collective-permute-start(bf16[384,256]{1,0:T(8,128)(2,1)S(1)} %get-tuple-element.25), channel_id=1, source_target_pairs={{0,16},{16,0},{1,17},{17,1},{2,18},{18,2},{3,19},{19,3},{4,20},{20... | collective-permute-start | bytes 589832 | tf_op jit(solution)/shard_map/ppermute | solution.py:25
  61.5 3.2 %collective-permute-start.3 = (bf16[384,256]{1,0:T(8,128)(2,1)S(1)}, bf16[384,256]{1,0:T(8,128)(2,1)S(1)}, u32[]{:S(2)}, u32[]{:S(2)}) collective-permute-start(bf16[384,256]{1,0:T(8,128)(2,1)S(1)} %get-tuple-element.25), channel_id=1, source_target_pairs={{0,8},{8,0},{1,9},{9,1},{2,10},{10,2},{3,11},{11,3},{4,12},{12,4},... | collective-permute-start | bytes 589832 | tf_op jit(solution)/shard_map/ppermute | solution.py:25
  64.7 0.0 copy-done
  64.7 3.4 %collective-permute-start.5 = (bf16[128,3072]{1,0:T(8,128)(2,1)S(1)}, bf16[128,3072]{1,0:T(8,128)(2,1)S(1)}, u32[]{:S(2)}, u32[]{:S(2)}) collective-permute-start(bf16[128,3072]{1,0:T(8,128)(2,1)S(1)} %copy-done), channel_id=1, source_target_pairs={{0,128},{128,0},{256,384},{384,256},{1,129},{129,1},{257,385},{385... | collective-permute-start | bytes 2359304 | tf_op jit(solution)/shard_map/ppermute | solution.py:294
  68.1 3.1 %collective-permute-start.6 = (bf16[128,3072]{1,0:T(8,128)(2,1)S(1)}, bf16[128,3072]{1,0:T(8,128)(2,1)}, u32[]{:S(2)}, u32[]{:S(2)}) collective-permute-start(bf16[128,3072]{1,0:T(8,128)(2,1)S(1)} %copy-done), channel_id=1, source_target_pairs={{0,384},{128,256},{256,128},{384,0},{1,385},{129,257},{257,129},{3... | collective-permute-start | bytes 2359304 | tf_op jit(solution)/shard_map/ppermute | solution.py:294
  71.3 4.4 %collective-permute-done.2 = bf16[384,256]{1,0:T(8,128)(2,1)S(1)} collective-permute-done((bf16[384,256]{1,0:T(8,128)(2,1)S(1)}, bf16[384,256]{1,0:T(8,128)(2,1)S(1)}, u32[]{:S(2)}, u32[]{:S(2)}) %collective-permute-start.2) | collective-permute-done | bytes 196640 | tf_op jit(solution)/shard_map/ppermute | solution.py:25
  75.7 9.4 %collective-permute-start.4 = (bf16[384,256]{1,0:T(8,128)(2,1)S(1)}, bf16[384,256]{1,0:T(8,128)(2,1)S(1)}, u32[]{:S(2)}, u32[]{:S(2)}) collective-permute-start(bf16[384,256]{1,0:T(8,128)(2,1)S(1)} %collective-permute-done.2), channel_id=1, source_target_pairs={{0,8},{8,0},{1,9},{9,1},{2,10},{10,2},{3,11},{11,3},{4,12},{12,4},... | collective-permute-start | bytes 589832 | tf_op jit(solution)/shard_map/ppermute | solution.py:25
  85.1 0.9 fusion.2
  86.0 3.1 %collective-permute-start.7 = (bf16[64,3072]{1,0:T(8,128)(2,1)}, bf16[64,3072]{1,0:T(8,128)(2,1)}, u32[]{:S(2)}, u32[]{:S(2)}) collective-permute-start(bf16[64,3072]{1,0:T(8,128)(2,1)} %get-tuple-element.34), channel_id=1, source_target_pairs={{0,256},{128,384},{256,0},{384,128},{1,257},{129,385},{257,1},{385... | collective-permute-start | bytes 1179656 | tf_op jit(solution)/shard_map/ppermute | solution.py:294
  89.1 0.0 collective-permute-done.3
  89.1 2.4 %collective-permute-done.4 = bf16[384,256]{1,0:T(8,128)(2,1)S(1)} collective-permute-done((bf16[384,256]{1,0:T(8,128)(2,1)S(1)}, bf16[384,256]{1,0:T(8,128)(2,1)S(1)}, u32[]{:S(2)}, u32[]{:S(2)}) %collective-permute-start.4) | collective-permute-done | bytes 196640 | tf_op jit(solution)/shard_map/ppermute | solution.py:25
  91.6 0.1 pad_maximum_fusion.kv_ref
  91.6 0.0 all-to-all-done.q_ref
  91.6 6.5 %shard_map.85 = bf16[8,400,128]{2,1,0:T(8,128)(2,1)} custom-call(bf16[8,384,128]{2,1,0:T(8,128)(2,1)S(1)} %all-to-all-done.q_ref, bf16[1536,256]{1,0:T(8,128)(2,1)S(1)} %pad_maximum_fusion.kv_ref), custom_call_target="tpu_custom_call" | custom-call | flops 2415919104 | bytes 786432 | tf_op jit(solution)/shard_map/pallas_call | solution.py:207
  98.1 0.0 copy-start.2
  98.1 0.8 collective-permute-done.7.refs_2_
  98.8 0.0 collective-permute-done.5.refs_0_
  98.8 0.0 collective-permute-done.6.refs_1_
  98.8 7.2 %all-to-all-start.1 = ((bf16[8,400,128]{2,1,0:T(8,128)(2,1)}), bf16[8,400,128]{2,1,0:T(8,128)(2,1)S(1)}, u32[]{:S(2)}, u32[]{:S(2)}) async-start(bf16[8,400,128]{2,1,0:T(8,128)(2,1)} %shard_map.85), calls=%async_computation.1 | async-start | bytes 1638400 | tf_op jit(solution)/shard_map/all_to_all | solution.py:313
  106.0 0.0 copy-done.2
  106.0 3.1 %collective-permute-start.8 = (bf16[64,3072]{1,0:T(8,128)(2,1)S(1)}, bf16[64,3072]{1,0:T(8,128)(2,1)S(1)}, u32[]{:S(2)}, u32[]{:S(2)}) collective-permute-start(bf16[64,3072]{1,0:T(8,128)(2,1)S(1)} %copy-done.2), channel_id=1, source_target_pairs={{0,256},{128,384},{256,0},{384,128},{1,257},{129,385},{257,1},{385... | collective-permute-start | bytes 1179656 | tf_op jit(solution)/shard_map/ppermute | solution.py:294
  109.1 5.4 %all-to-all-done.1.partial_ref = bf16[8,400,128]{2,1,0:T(8,128)(2,1)S(1)} async-done(((bf16[8,400,128]{2,1,0:T(8,128)(2,1)}), bf16[8,400,128]{2,1,0:T(8,128)(2,1)S(1)}, u32[]{:S(2)}, u32[]{:S(2)}) %all-to-all-start.1) | async-done | bytes 819232 | tf_op jit(solution)/shard_map/all_to_all | solution.py:313
  114.5 0.8 shard_map.86
  115.3 4.5 %all-to-all-start.2 = ((bf16[4,96,128]{2,1,0:T(8,128)(2,1)}), bf16[4,96,128]{2,1,0:T(8,128)(2,1)S(1)}, u32[]{:S(2)}, u32[]{:S(2)}) async-start(bf16[4,96,128]{2,1,0:T(8,128)(2,1)} %shard_map.86), calls=%async_computation.2 | async-start | bytes 196608 | tf_op jit(solution)/shard_map/all_to_all | solution.py:314
  119.8 0.0 collective-permute-done.8.refs_3_
  119.8 4.6 %all-to-all-done.2.attended_ref = bf16[4,96,128]{2,1,0:T(8,128)(2,1)S(1)} async-done(((bf16[4,96,128]{2,1,0:T(8,128)(2,1)}), bf16[4,96,128]{2,1,0:T(8,128)(2,1)S(1)}, u32[]{:S(2)}, u32[]{:S(2)}) %all-to-all-start.2) | async-done | bytes 98336 | tf_op jit(solution)/shard_map/all_to_all | solution.py:314
  124.4 1.9 %shard_map.87 = (f32[48,3072]{1,0:T(8,128)S(1)}, bf16[48,3072]{1,0:T(8,128)(2,1)S(1)}) custom-call(s32[1]{0:T(128)} %bitcast.y_ref, bf16[4,96,128]{2,1,0:T(8,128)(2,1)S(1)} %all-to-all-done.2.attended_ref, bf16[128,3072]{1,0:T(8,128)(2,1)S(1)} %copy-done, bf16[128,3072]{1,0:T(8,128)(2,1)S(1)} %collective-permute-done.5.refs_0_, ...), custom_call_target="tpu_custom_call" | custom-call | flops 301989888 | bytes 3145728 | tf_op jit(solution)/shard_map/pallas_call | solution.py:268
  126.4 0.0 copy-start.3
  126.4 8.5 %collective-permute-start.9 = (bf16[48,3072]{1,0:T(8,128)(2,1)S(1)}, bf16[48,3072]{1,0:T(8,128)(2,1)S(1)}, u32[]{:S(2)}, u32[]{:S(2)}) collective-permute-start(bf16[48,3072]{1,0:T(8,128)(2,1)S(1)} %get-tuple-element.32), channel_id=1, source_target_pairs={{0,32},{32,0},{1,33},{33,1},{2,34},{34,2},{3,35},{35,3},{4,36},{36... | collective-permute-start | bytes 884744 | tf_op jit(solution)/shard_map/ppermute | solution.py:25
  134.8 1.2 collective-permute-done.9
  136.0 0.1 convert_add_fusion
  136.1 5.3 %collective-permute-start.10 = (bf16[24,3072]{1,0:T(8,128)(2,1)S(1)}, bf16[24,3072]{1,0:T(8,128)(2,1)S(1)}, u32[]{:S(2)}, u32[]{:S(2)}) collective-permute-start(bf16[24,3072]{1,0:T(8,128)(2,1)S(1)} %slice.25), channel_id=1, source_target_pairs={{0,80},{16,64},{64,16},{80,0},{1,81},{17,65},{65,17},{81,1},{2,82}... | collective-permute-start | bytes 442376 | tf_op jit(solution)/shard_map/ppermute | solution.py:29
  141.5 12.5 %collective-permute-done.10 = bf16[24,3072]{1,0:T(8,128)(2,1)S(1)} collective-permute-done((bf16[24,3072]{1,0:T(8,128)(2,1)S(1)}, bf16[24,3072]{1,0:T(8,128)(2,1)S(1)}, u32[]{:S(2)}, u32[]{:S(2)}) %collective-permute-start.10) | collective-permute-done | bytes 147488 | tf_op jit(solution)/shard_map/ppermute | solution.py:29
  153.9 0.0 copy-done.3
  153.9 0.7 fusion.1
  (3 shorter events, 0.1 us)
Async XLA Ops:
  0.0 27.6 %collective-permute-start = (bf16[24,3072]{1,0:T(8,128)(2,1)}, bf16[24,3072]{1,0:T(8,128)(2,1)S(1)}, u32[]{:S(2)}, u32[]{:S(2)}) collective-permute-start(bf16[24,3072]{1,0:T(8,128)(2,1)} %tokens_ref.1), channel_id=1, source_target_pairs={{0,80},{16,64},{64,16},{80,0},{1,81},{17,65},{65,17},{81,1},{2,82}... | collective-permute-start | bytes 442376 | tf_op jit(solution)/shard_map/ppermute | solution.py:29
  15.2 12.4 %copy-start.1 = (f32[4,1,3072]{2,1,0:T(1,128)S(1)}, f32[4,1,3072]{2,1,0:T(1,128)}, u32[]{:S(2)}) copy-start(f32[4,1,3072]{2,1,0:T(1,128)} %get-tuple-element.20.rows_ref) | copy-start | bytes 147460
  38.0 10.0 %collective-permute-start.1 = (bf16[192,3072]{1,0:T(8,128)(2,1)S(1)}, bf16[192,3072]{1,0:T(8,128)(2,1)S(1)}, u32[]{:S(2)}, u32[]{:S(2)}) collective-permute-start(bf16[192,3072]{1,0:T(8,128)(2,1)S(1)} %constant_dynamic-update-slice_fusion.refs_0_), channel_id=1, source_target_pairs={{0,32},{32,0},{1,33},{33,1},{2,34},{34,2},{3,35},{35,3},{4,36},{36... | collective-permute-start | bytes 3538952 | tf_op jit(solution)/shard_map/ppermute | solution.py:25
  51.8 12.9 %copy-start = (bf16[128,3072]{1,0:T(8,128)(2,1)S(1)}, bf16[128,3072]{1,0:T(8,128)(2,1)}, u32[]{:S(2)}) copy-start(bf16[128,3072]{1,0:T(8,128)(2,1)} %first_ref) | copy-start | bytes 2359300
  51.8 39.8 %all-to-all-start = ((bf16[8,384,128]{2,1,0:T(8,128)(2,1)}), bf16[8,384,128]{2,1,0:T(8,128)(2,1)S(1)}, u32[]{:S(2)}, u32[]{:S(2)}) async-start(bf16[8,384,128]{2,1,0:T(8,128)(2,1)} %get-tuple-element.23), calls=%async_computation | async-start | bytes 1572864 | tf_op jit(solution)/shard_map/all_to_all | solution.py:308
  56.4 19.3 %collective-permute-start.2 = (bf16[384,256]{1,0:T(8,128)(2,1)S(1)}, bf16[384,256]{1,0:T(8,128)(2,1)S(1)}, u32[]{:S(2)}, u32[]{:S(2)}) collective-permute-start(bf16[384,256]{1,0:T(8,128)(2,1)S(1)} %get-tuple-element.25), channel_id=1, source_target_pairs={{0,16},{16,0},{1,17},{17,1},{2,18},{18,2},{3,19},{19,3},{4,20},{20... | collective-permute-start | bytes 589832 | tf_op jit(solution)/shard_map/ppermute | solution.py:25
  61.5 27.6 %collective-permute-start.3 = (bf16[384,256]{1,0:T(8,128)(2,1)S(1)}, bf16[384,256]{1,0:T(8,128)(2,1)S(1)}, u32[]{:S(2)}, u32[]{:S(2)}) collective-permute-start(bf16[384,256]{1,0:T(8,128)(2,1)S(1)} %get-tuple-element.25), channel_id=1, source_target_pairs={{0,8},{8,0},{1,9},{9,1},{2,10},{10,2},{3,11},{11,3},{4,12},{12,4},... | collective-permute-start | bytes 589832 | tf_op jit(solution)/shard_map/ppermute | solution.py:25
  64.7 34.1 %collective-permute-start.5 = (bf16[128,3072]{1,0:T(8,128)(2,1)S(1)}, bf16[128,3072]{1,0:T(8,128)(2,1)S(1)}, u32[]{:S(2)}, u32[]{:S(2)}) collective-permute-start(bf16[128,3072]{1,0:T(8,128)(2,1)S(1)} %copy-done), channel_id=1, source_target_pairs={{0,128},{128,0},{256,384},{384,256},{1,129},{129,1},{257,385},{385... | collective-permute-start | bytes 2359304 | tf_op jit(solution)/shard_map/ppermute | solution.py:294
  68.1 30.7 %collective-permute-start.6 = (bf16[128,3072]{1,0:T(8,128)(2,1)S(1)}, bf16[128,3072]{1,0:T(8,128)(2,1)}, u32[]{:S(2)}, u32[]{:S(2)}) collective-permute-start(bf16[128,3072]{1,0:T(8,128)(2,1)S(1)} %copy-done), channel_id=1, source_target_pairs={{0,384},{128,256},{256,128},{384,0},{1,385},{129,257},{257,129},{3... | collective-permute-start | bytes 2359304 | tf_op jit(solution)/shard_map/ppermute | solution.py:294
  75.7 15.8 %collective-permute-start.4 = (bf16[384,256]{1,0:T(8,128)(2,1)S(1)}, bf16[384,256]{1,0:T(8,128)(2,1)S(1)}, u32[]{:S(2)}, u32[]{:S(2)}) collective-permute-start(bf16[384,256]{1,0:T(8,128)(2,1)S(1)} %collective-permute-done.2), channel_id=1, source_target_pairs={{0,8},{8,0},{1,9},{9,1},{2,10},{10,2},{3,11},{11,3},{4,12},{12,4},... | collective-permute-start | bytes 589832 | tf_op jit(solution)/shard_map/ppermute | solution.py:25
  86.0 12.8 %collective-permute-start.7 = (bf16[64,3072]{1,0:T(8,128)(2,1)}, bf16[64,3072]{1,0:T(8,128)(2,1)}, u32[]{:S(2)}, u32[]{:S(2)}) collective-permute-start(bf16[64,3072]{1,0:T(8,128)(2,1)} %get-tuple-element.34), channel_id=1, source_target_pairs={{0,256},{128,384},{256,0},{384,128},{1,257},{129,385},{257,1},{385... | collective-permute-start | bytes 1179656 | tf_op jit(solution)/shard_map/ppermute | solution.py:294
  98.1 7.9 %copy-start.2 = (bf16[64,3072]{1,0:T(8,128)(2,1)S(1)}, bf16[64,3072]{1,0:T(8,128)(2,1)}, u32[]{:S(2)}) copy-start(bf16[64,3072]{1,0:T(8,128)(2,1)} %get-tuple-element.33) | copy-start | bytes 1179652
  98.8 15.6 %all-to-all-start.1 = ((bf16[8,400,128]{2,1,0:T(8,128)(2,1)}), bf16[8,400,128]{2,1,0:T(8,128)(2,1)S(1)}, u32[]{:S(2)}, u32[]{:S(2)}) async-start(bf16[8,400,128]{2,1,0:T(8,128)(2,1)} %shard_map.85), calls=%async_computation.1 | async-start | bytes 1638400 | tf_op jit(solution)/shard_map/all_to_all | solution.py:313
  106.0 13.8 %collective-permute-start.8 = (bf16[64,3072]{1,0:T(8,128)(2,1)S(1)}, bf16[64,3072]{1,0:T(8,128)(2,1)S(1)}, u32[]{:S(2)}, u32[]{:S(2)}) collective-permute-start(bf16[64,3072]{1,0:T(8,128)(2,1)S(1)} %copy-done.2), channel_id=1, source_target_pairs={{0,256},{128,384},{256,0},{384,128},{1,257},{129,385},{257,1},{385... | collective-permute-start | bytes 1179656 | tf_op jit(solution)/shard_map/ppermute | solution.py:294
  115.3 9.1 %all-to-all-start.2 = ((bf16[4,96,128]{2,1,0:T(8,128)(2,1)}), bf16[4,96,128]{2,1,0:T(8,128)(2,1)S(1)}, u32[]{:S(2)}, u32[]{:S(2)}) async-start(bf16[4,96,128]{2,1,0:T(8,128)(2,1)} %shard_map.86), calls=%async_computation.2 | async-start | bytes 196608 | tf_op jit(solution)/shard_map/all_to_all | solution.py:314
  126.4 27.6 %copy-start.3 = (f32[3072]{0:T(1024)S(1)}, f32[3072]{0:T(1024)}, u32[]{:S(2)}) copy-start(f32[3072]{0:T(1024)} %param.15) | copy-start | bytes 36868
  126.4 9.6 %collective-permute-start.9 = (bf16[48,3072]{1,0:T(8,128)(2,1)S(1)}, bf16[48,3072]{1,0:T(8,128)(2,1)S(1)}, u32[]{:S(2)}, u32[]{:S(2)}) collective-permute-start(bf16[48,3072]{1,0:T(8,128)(2,1)S(1)} %get-tuple-element.32), channel_id=1, source_target_pairs={{0,32},{32,0},{1,33},{33,1},{2,34},{34,2},{3,35},{35,3},{4,36},{36... | collective-permute-start | bytes 884744 | tf_op jit(solution)/shard_map/ppermute | solution.py:25
  136.1 17.8 %collective-permute-start.10 = (bf16[24,3072]{1,0:T(8,128)(2,1)S(1)}, bf16[24,3072]{1,0:T(8,128)(2,1)S(1)}, u32[]{:S(2)}, u32[]{:S(2)}) collective-permute-start(bf16[24,3072]{1,0:T(8,128)(2,1)S(1)} %slice.25), channel_id=1, source_target_pairs={{0,80},{16,64},{64,16},{80,0},{1,81},{17,65},{65,17},{81,1},{2,82}... | collective-permute-start | bytes 442376 | tf_op jit(solution)/shard_map/ppermute | solution.py:29

commit v7 on v6

--- a/solution.py
+++ b/solution.py
@@ -173,41 +173,38 @@
 def attend_kernel(q_ref, kv_ref, out_ref):
     blocks, rows, _ = q_ref.shape
     step = kv_ref.shape[0] // 2
-
-    @pl.loop(0, blocks, step=2)
-    def _(first):
-        totals = [0.0, 0.0]
-        for at in range(0, kv_ref.shape[0], step):
-            ones = jnp.ones((step, HD), BF16)
-            values = jnp.concatenate([kv_ref[at : at + step, HD:], ones], axis=1)
-            for i in range(2):
-                scores = lax.dot_general(
-                    q_ref[first + i],
-                    kv_ref[at : at + step, :HD],
-                    (((1,), (1,)), ((), ())),
-                    preferred_element_type=F32,
-                )
-                weights = jnp.exp2(scores).astype(BF16)
-                totals[i] += jnp.dot(weights, values, preferred_element_type=F32)
-        for i, total in enumerate(totals):
-            out_ref[first + i, :rows] = total[:, :HD].astype(BF16)
-            sums = [
-                jnp.where(diagonal(size), total[at : at + size, HD:], 0.0)
-                for at, size in row_blocks(rows)
-            ]
-            out_ref[first + i, rows:] = tail_of(
-                [jnp.sum(square, axis=0, keepdims=True) for square in sums]
+    totals = [0.0] * blocks
+    for at in range(0, kv_ref.shape[0], step):
+        values = jnp.concatenate([kv_ref[at : at + step, HD:], jnp.ones((step, HD), BF16)], axis=1)
+        for i in range(blocks):
+            scores = lax.dot_general(
+                q_ref[i],
+                kv_ref[at : at + step, :HD],
+                (((1,), (1,)), ((), ())),
+                preferred_element_type=F32,
             )
+            weights = jnp.exp2(scores).astype(BF16)
+            totals[i] += jnp.dot(weights, values, preferred_element_type=F32)
+    for i, total in enumerate(totals):
+        out_ref[i, :rows] = total[:, :HD].astype(BF16)
+        sums = [
+            jnp.where(diagonal(size), total[at : at + size, HD:], 0.0)
+            for at, size in row_blocks(rows)
+        ]
+        out_ref[i, rows:] = tail_of([jnp.sum(square, axis=0, keepdims=True) for square in sums])
 
 
 def attend(queries, keyval):
     blocks, rows, _ = queries.shape
     keys = keyval.shape[0]
-    vmem = pl.BlockSpec(memory_space=pltpu.VMEM)
     return pl.pallas_call(
         attend_kernel,
-        in_specs=[vmem, vmem],
-        out_specs=vmem,
+        grid=(blocks // 2,),
+        in_specs=[
+            pl.BlockSpec((2, rows, HD), lambda i: (i, 0, 0)),
+            pl.BlockSpec(keyval.shape, lambda i: (0, 0)),
+        ],
+        out_specs=pl.BlockSpec((2, rows + TAIL, HD), lambda i: (i, 0, 0)),
         out_shape=jax.ShapeDtypeStruct((blocks, rows + TAIL, HD), BF16),
         compiler_params=params(16),
         cost_estimate=pl.CostEstimate(
@@ -246,19 +243,21 @@
 
 
 def mix_kernel(y_ref, attended_ref, first_ref, *refs):
-    *weight_refs, own_ref, other_ref, first, first_sem = refs
+    *weight_refs, near_ref, far_ref, near_out_ref, far_out_ref, first, first_sem = refs
     copy = pltpu.make_async_copy(first_ref, first, first_sem.at[0])
     copy.start()
     attended = jnp.concatenate([attended_ref[y_ref[0] ^ i] for i in (0, 1, 3, 2)], axis=1)
-    half, width = own_ref.shape
+    part, width = near_ref.shape
     step = width // 4
     copy.wait()
     for at in range(0, width, step):
         weight = [ref[:, at : at + step] for ref in (first, *weight_refs)]
         weight = jnp.concatenate(weight, axis=0)
         mixed = jnp.dot(attended, weight, preferred_element_type=F32)
-        own_ref[:, at : at + step] = mixed[:half]
-        other_ref[:, at : at + step] = mixed[half:].astype(BF16)
+        near_ref[:, at : at + step] = mixed[:part]
+        far_ref[:, at : at + step] = mixed[part : 2 * part]
+        near_out_ref[:, at : at + step] = mixed[2 * part : 3 * part].astype(BF16)
+        far_out_ref[:, at : at + step] = mixed[3 * part :].astype(BF16)
 
 
 def mix(y, attended, weights):
@@ -274,8 +273,7 @@
         ]
         + [vmem] * (len(weights) - 1),
         out_shape=[
-            jax.ShapeDtypeStruct((rows // 2, width), F32),
-            jax.ShapeDtypeStruct((rows // 2, width), BF16),
+            jax.ShapeDtypeStruct((rows // 4, width), kind) for kind in (F32, F32, BF16, BF16)
         ],
         scratch_shapes=[pltpu.VMEM((depth, width), BF16), pltpu.SemaphoreType.DMA((1,))],
         compiler_params=params(16),
@@ -288,7 +286,7 @@
 
 
 def local(tokens, mod_shift, mod_scale, qkv_weight, q_gain, k_gain, out_weight, out_gate):
-    rows, width = tokens.shape
+    width = tokens.shape[1]
 
     def along_y(block, distance):
         return lax.ppermute(block, "y", [(i, i ^ distance) for i in range(4)])
@@ -313,10 +311,11 @@
     partial = lax.all_to_all(partial, NEAR, 0, 0)
     attended = lax.all_to_all(divide(partial, 4), "y", 0, 0)
     y = lax.axis_index("y").astype(jnp.int32).reshape(1)
-    own, other = mix(y, attended, [out_weight, *weights])
-    summed = own + swap(other, "core").astype(F32)
-    arrived = trade_halves(summed[rows:].astype(BF16)).astype(F32)
-    return ((summed[:rows] + arrived) * out_gate).astype(BF16)
+    near, far, near_out, far_out = mix(y, attended, [out_weight, *weights])
+    far = (far + swap(far_out, "core").astype(F32)).astype(BF16)
+    near_out, far = lax.optimization_barrier((near_out, far))
+    arrived = trade_halves(far).astype(F32)
+    return ((near + swap(near_out, "core").astype(F32) + arrived) * out_gate).astype(BF16)
 
 
 def solution(mesh):

time: 156 us -> 158 us (1.013)
  starting transfers between devices: 81.2 us -> 83.3 us
    ppermute x5 -> x6, starting transfers between devices: 33.7 us -> 36 us  [swap(): return lax.ppermute(block, axis, [(0, 1), (1, 0)])]
    ppermute x5 -> x6, waiting for transfers between devices: 10.5 us -> 10.3 us  [swap(): return lax.ppermute(block, axis, [(0, 1), (1, 0)])]
  transfers between devices with their start and end apart: 14 -> 15, of which waited for: 8 -> 8; matrix products, arithmetic and copies ran while one was open for 1% -> 1% of each run, Pallas kernels for 6% -> 6%
where the time goes in v7:
time: 158 us; the launch traced here: 157 us
  starting transfers between devices  83.3 us (53%)
  waiting for transfers between devices  33.9 us (21%)
  blocking collectives  22.4 us (14%)
  Pallas kernels  15 us (9%)
    ppermute x6, starting transfers between devices, swap(): return lax.ppermute(block, axis, [(0, 1), (1, 0)])  36 us
    all_gather x2, blocking collectives, spread(): return lax.all_gather(modulated, 'y', axis=0, tiled=True)  22.4 us
    ppermute x2, starting transfers between devices, trade_halves(): return lax.ppermute(block, ('zh', 'za'), [(i, i ^ 3) for i in range(4)])  18.4 us
    ppermute x4, starting transfers between devices, along_y(): return lax.ppermute(block, 'y', [(i, i ^ distance) for i in range(4)])  12.7 us
    ppermute x2, waiting for transfers between devices, trade_halves(): return lax.ppermute(block, ('zh', 'za'), [(i, i ^ 3) for i in range(4)])  12.7 us
    ppermute x6, waiting for transfers between devices, swap(): return lax.ppermute(block, axis, [(0, 1), (1, 0)])  10.3 us
    all_to_all x1, starting transfers between devices, local(): partial = lax.all_to_all(partial, NEAR, 0, 0)  7.16 us
    pallas_call x1, Pallas kernels, attend(): pl.pallas_call(attend_kernel, grid=(blocks // 2,), in_specs=[pl.BlockSpec...  6.29 us
  transfers between devices with their start and end apart: 15, of which 8 were waited for; matrix products, arithmetic and copies ran while one was open for 1% of the time, Pallas kernels for 6%

profile of v7, /device:TPU:1, one launch (start us, length us, event | category | flops | bytes accessed | tf_op | source)
XLA Modules:
  0.0 156.7 jit_solution(3457532553067834828)
XLA Ops:
  0.0 13.3 %collective-permute-start = (bf16[24,3072]{1,0:T(8,128)(2,1)}, bf16[24,3072]{1,0:T(8,128)(2,1)S(1)}, u32[]{:S(2)}, u32[]{:S(2)}) collective-permute-start(bf16[24,3072]{1,0:T(8,128)(2,1)} %tokens_ref.1), channel_id=1, source_target_pairs={{0,80},{16,64},{64,16},{80,0},{1,81},{17,65},{65,17},{81,1},{2,82}... | collective-permute-start | bytes 442376 | tf_op jit(solution)/shard_map/ppermute | solution.py:29
  13.3 1.9 %shard_map.82 = (bf16[24,3072]{1,0:T(8,128)(2,1)}, f32[4,1,3072]{2,1,0:T(1,128)}) custom-call(bf16[24,3072]{1,0:T(8,128)(2,1)} %tokens_ref.1, f32[1,3072]{1,0:T(1,128)} %bitcast.5, f32[1,3072]{1,0:T(1,128)} %bitcast.6, f32[1,128]{1,0:T(1,128)} %bitcast.7, f32[1,128]{1,0:T(1,128)} %bitcast.8), custom_call_target="tpu_custom_call" | custom-call | tf_op jit(solution)/shard_map/pallas_call | solution.py:56
  15.2 0.0 copy-start.1
  15.2 12.3 %all_gather.6 = bf16[96,3072]{1,0:T(8,128)(2,1)S(1)} all-gather(bf16[24,3072]{1,0:T(8,128)(2,1)} %get-tuple-element.23), channel_id=1, replica_groups=mesh['y'=4,'zh'=2,'core'=2,'za'=2,'zb'=2,'zc'=2,'x'=4] {'y'}, dimensions={0}, use_global_device_ids=true | all-gather | bytes 737280 | tf_op jit(solution)/shard_map/all_gather | solution.py:295
  27.6 0.0 collective-permute-done.tokens_ref
  27.6 0.0 copy-done.1
  27.6 0.3 shard_map.83
  27.9 10.0 %all_gather.7 = bf16[96,3072]{1,0:T(8,128)(2,1)S(1)} all-gather(bf16[24,3072]{1,0:T(8,128)(2,1)S(1)} %get-tuple-element.25), channel_id=1, replica_groups=mesh['y'=4,'zh'=2,'core'=2,'za'=2,'zb'=2,'zc'=2,'x'=4] {'y'}, dimensions={0}, use_global_device_ids=true | all-gather | bytes 737280 | tf_op jit(solution)/shard_map/all_gather | solution.py:295
  38.0 7.6 %collective-permute-start.1 = (bf16[192,3072]{1,0:T(8,128)(2,1)S(1)}, bf16[192,3072]{1,0:T(8,128)(2,1)S(1)}, u32[]{:S(2)}, u32[]{:S(2)}) collective-permute-start(bf16[192,3072]{1,0:T(8,128)(2,1)S(1)} %constant_dynamic-update-slice_fusion.refs_0_), channel_id=1, source_target_pairs={{0,32},{32,0},{1,33},{33,1},{2,34},{34,2},{3,35},{35,3},{4,36},{36... | collective-permute-start | bytes 3538952 | tf_op jit(solution)/shard_map/ppermute | solution.py:25
  45.5 2.5 %collective-permute-done.1.refs_1_ = bf16[192,3072]{1,0:T(8,128)(2,1)S(1)} collective-permute-done((bf16[192,3072]{1,0:T(8,128)(2,1)S(1)}, bf16[192,3072]{1,0:T(8,128)(2,1)S(1)}, u32[]{:S(2)}, u32[]{:S(2)}) %collective-permute-start.1) | collective-permute-done | bytes 1179680 | tf_op jit(solution)/shard_map/ppermute | solution.py:25
  48.0 3.8 %shard_map.84 = (bf16[8,384,128]{2,1,0:T(8,128)(2,1)}, bf16[384,256]{1,0:T(8,128)(2,1)S(1)}) custom-call(bf16[192,3072]{1,0:T(8,128)(2,1)S(1)} %constant_dynamic-update-slice_fusion.refs_0_, bf16[192,3072]{1,0:T(8,128)(2,1)S(1)} %collective-permute-done.1.refs_1_, f32[2,1,128]{2,1,0:T(1,128)S(1)} %get-tuple-element.26.refs_2_, bf16[3,3072,128]{2,1,0:T(8,128)(2,1)} %refs_3_.1), custom_call_target="tpu_custom_call" | custom-call | flops 905969664 | bytes 2359296 | tf_op jit(solution)/shard_map/pallas_call | solution.py:126
  51.8 0.0 copy-start
  51.8 4.6 %all-to-all-start = ((bf16[8,384,128]{2,1,0:T(8,128)(2,1)}), bf16[8,384,128]{2,1,0:T(8,128)(2,1)S(1)}, u32[]{:S(2)}, u32[]{:S(2)}) async-start(bf16[8,384,128]{2,1,0:T(8,128)(2,1)} %get-tuple-element.27), calls=%async_computation | async-start | bytes 1572864 | tf_op jit(solution)/shard_map/all_to_all | solution.py:306
  56.4 5.1 %collective-permute-start.2 = (bf16[384,256]{1,0:T(8,128)(2,1)S(1)}, bf16[384,256]{1,0:T(8,128)(2,1)S(1)}, u32[]{:S(2)}, u32[]{:S(2)}) collective-permute-start(bf16[384,256]{1,0:T(8,128)(2,1)S(1)} %get-tuple-element.29), channel_id=1, source_target_pairs={{0,16},{16,0},{1,17},{17,1},{2,18},{18,2},{3,19},{19,3},{4,20},{20... | collective-permute-start | bytes 589832 | tf_op jit(solution)/shard_map/ppermute | solution.py:25
  61.5 3.2 %collective-permute-start.3 = (bf16[384,256]{1,0:T(8,128)(2,1)S(1)}, bf16[384,256]{1,0:T(8,128)(2,1)S(1)}, u32[]{:S(2)}, u32[]{:S(2)}) collective-permute-start(bf16[384,256]{1,0:T(8,128)(2,1)S(1)} %get-tuple-element.29), channel_id=1, source_target_pairs={{0,8},{8,0},{1,9},{9,1},{2,10},{10,2},{3,11},{11,3},{4,12},{12,4},... | collective-permute-start | bytes 589832 | tf_op jit(solution)/shard_map/ppermute | solution.py:25
  64.7 0.0 copy-done
  64.7 3.4 %collective-permute-start.5 = (bf16[128,3072]{1,0:T(8,128)(2,1)S(1)}, bf16[128,3072]{1,0:T(8,128)(2,1)S(1)}, u32[]{:S(2)}, u32[]{:S(2)}) collective-permute-start(bf16[128,3072]{1,0:T(8,128)(2,1)S(1)} %copy-done), channel_id=1, source_target_pairs={{0,128},{128,0},{256,384},{384,256},{1,129},{129,1},{257,385},{385... | collective-permute-start | bytes 2359304 | tf_op jit(solution)/shard_map/ppermute | solution.py:292
  68.1 3.1 %collective-permute-start.6 = (bf16[128,3072]{1,0:T(8,128)(2,1)S(1)}, bf16[128,3072]{1,0:T(8,128)(2,1)}, u32[]{:S(2)}, u32[]{:S(2)}) collective-permute-start(bf16[128,3072]{1,0:T(8,128)(2,1)S(1)} %copy-done), channel_id=1, source_target_pairs={{0,384},{128,256},{256,128},{384,0},{1,385},{129,257},{257,129},{3... | collective-permute-start | bytes 2359304 | tf_op jit(solution)/shard_map/ppermute | solution.py:292
  71.3 4.4 %collective-permute-done.2 = bf16[384,256]{1,0:T(8,128)(2,1)S(1)} collective-permute-done((bf16[384,256]{1,0:T(8,128)(2,1)S(1)}, bf16[384,256]{1,0:T(8,128)(2,1)S(1)}, u32[]{:S(2)}, u32[]{:S(2)}) %collective-permute-start.2) | collective-permute-done | bytes 196640 | tf_op jit(solution)/shard_map/ppermute | solution.py:25
  75.7 9.4 %collective-permute-start.4 = (bf16[384,256]{1,0:T(8,128)(2,1)S(1)}, bf16[384,256]{1,0:T(8,128)(2,1)S(1)}, u32[]{:S(2)}, u32[]{:S(2)}) collective-permute-start(bf16[384,256]{1,0:T(8,128)(2,1)S(1)} %collective-permute-done.2), channel_id=1, source_target_pairs={{0,8},{8,0},{1,9},{9,1},{2,10},{10,2},{3,11},{11,3},{4,12},{12,4},... | collective-permute-start | bytes 589832 | tf_op jit(solution)/shard_map/ppermute | solution.py:25
  85.1 0.9 fusion
  86.0 3.1 %collective-permute-start.7 = (bf16[64,3072]{1,0:T(8,128)(2,1)}, bf16[64,3072]{1,0:T(8,128)(2,1)}, u32[]{:S(2)}, u32[]{:S(2)}) collective-permute-start(bf16[64,3072]{1,0:T(8,128)(2,1)} %get-tuple-element.42), channel_id=1, source_target_pairs={{0,256},{128,384},{256,0},{384,128},{1,257},{129,385},{257,1},{385... | collective-permute-start | bytes 1179656 | tf_op jit(solution)/shard_map/ppermute | solution.py:292
  89.1 0.0 collective-permute-done.3
  89.1 2.5 %collective-permute-done.4 = bf16[384,256]{1,0:T(8,128)(2,1)S(1)} collective-permute-done((bf16[384,256]{1,0:T(8,128)(2,1)S(1)}, bf16[384,256]{1,0:T(8,128)(2,1)S(1)}, u32[]{:S(2)}, u32[]{:S(2)}) %collective-permute-start.4) | collective-permute-done | bytes 196640 | tf_op jit(solution)/shard_map/ppermute | solution.py:25
  91.6 0.1 pad_maximum_fusion.kv_ref
  91.6 0.0 all-to-all-done.q_ref
  91.6 6.3 %shard_map.85 = bf16[8,400,128]{2,1,0:T(8,128)(2,1)} custom-call(bf16[8,384,128]{2,1,0:T(8,128)(2,1)S(1)} %all-to-all-done.q_ref, bf16[1536,256]{1,0:T(8,128)(2,1)S(1)} %pad_maximum_fusion.kv_ref), custom_call_target="tpu_custom_call" | custom-call | flops 2415919104 | bytes 786432 | tf_op jit(solution)/shard_map/pallas_call | solution.py:200
  97.9 0.0 copy-start.2
  97.9 0.9 collective-permute-done.7.refs_2_
  98.8 0.0 collective-permute-done.5.refs_0_
  98.9 0.0 collective-permute-done.6.refs_1_
  98.9 7.2 %all-to-all-start.1 = ((bf16[8,400,128]{2,1,0:T(8,128)(2,1)}), bf16[8,400,128]{2,1,0:T(8,128)(2,1)S(1)}, u32[]{:S(2)}, u32[]{:S(2)}) async-start(bf16[8,400,128]{2,1,0:T(8,128)(2,1)} %shard_map.85), calls=%async_computation.1 | async-start | bytes 1638400 | tf_op jit(solution)/shard_map/all_to_all | solution.py:311
  106.0 0.0 copy-done.2
  106.0 3.1 %collective-permute-start.8 = (bf16[64,3072]{1,0:T(8,128)(2,1)S(1)}, bf16[64,3072]{1,0:T(8,128)(2,1)S(1)}, u32[]{:S(2)}, u32[]{:S(2)}) collective-permute-start(bf16[64,3072]{1,0:T(8,128)(2,1)S(1)} %copy-done.2), channel_id=1, source_target_pairs={{0,256},{128,384},{256,0},{384,128},{1,257},{129,385},{257,1},{385... | collective-permute-start | bytes 1179656 | tf_op jit(solution)/shard_map/ppermute | solution.py:292
  109.1 5.4 %all-to-all-done.1.partial_ref = bf16[8,400,128]{2,1,0:T(8,128)(2,1)S(1)} async-done(((bf16[8,400,128]{2,1,0:T(8,128)(2,1)}), bf16[8,400,128]{2,1,0:T(8,128)(2,1)S(1)}, u32[]{:S(2)}, u32[]{:S(2)}) %all-to-all-start.1) | async-done | bytes 819232 | tf_op jit(solution)/shard_map/all_to_all | solution.py:311
  114.5 0.8 shard_map.86
  115.3 4.5 %all-to-all-start.2 = ((bf16[4,96,128]{2,1,0:T(8,128)(2,1)}), bf16[4,96,128]{2,1,0:T(8,128)(2,1)S(1)}, u32[]{:S(2)}, u32[]{:S(2)}) async-start(bf16[4,96,128]{2,1,0:T(8,128)(2,1)} %shard_map.86), calls=%async_computation.2 | async-start | bytes 196608 | tf_op jit(solution)/shard_map/all_to_all | solution.py:312
  119.8 0.0 collective-permute-done.8.refs_3_
  119.8 4.6 %all-to-all-done.2.attended_ref = bf16[4,96,128]{2,1,0:T(8,128)(2,1)S(1)} async-done(((bf16[4,96,128]{2,1,0:T(8,128)(2,1)}), bf16[4,96,128]{2,1,0:T(8,128)(2,1)S(1)}, u32[]{:S(2)}, u32[]{:S(2)}) %all-to-all-start.2) | async-done | bytes 98336 | tf_op jit(solution)/shard_map/all_to_all | solution.py:312
  124.4 0.0 copy-start.3
  124.4 1.9 %shard_map.87 = (f32[24,3072]{1,0:T(8,128)S(1)}, f32[24,3072]{1,0:T(8,128)S(1)}, bf16[24,3072]{1,0:T(8,128)(2,1)S(1)}, bf16[24,3072]{1,0:T(8,128)(2,1)S(1)}) custom-call(s32[1]{0:T(128)} %bitcast.y_ref, bf16[4,96,128]{2,1,0:T(8,128)(2,1)S(1)} %all-to-all-done.2.attended_ref, bf16[128,3072]{1,0:T(8,128)(2,1)S(1)} %copy-done, ...), custom_call_target="tpu_custom_call" | custom-call | flops 301989888 | bytes 3145728 | tf_op jit(solution)/shard_map/pallas_call | solution.py:267
  126.4 8.5 %collective-permute-start.9 = (bf16[24,3072]{1,0:T(8,128)(2,1)S(1)}, bf16[24,3072]{1,0:T(8,128)(2,1)S(1)}, u32[]{:S(2)}, u32[]{:S(2)}) collective-permute-start(bf16[24,3072]{1,0:T(8,128)(2,1)S(1)} %get-tuple-element.38), channel_id=1, source_target_pairs={{0,32},{32,0},{1,33},{33,1},{2,34},{34,2},{3,35},{35,3},{4,36},{36... | collective-permute-start | bytes 442376 | tf_op jit(solution)/shard_map/ppermute | solution.py:25
  134.8 1.0 collective-permute-done.9
  135.9 2.3 %collective-permute-start.10 = (bf16[24,3072]{1,0:T(8,128)(2,1)S(1)}, bf16[24,3072]{1,0:T(8,128)(2,1)S(1)}, u32[]{:S(2)}, u32[]{:S(2)}) collective-permute-start(bf16[24,3072]{1,0:T(8,128)(2,1)S(1)} %get-tuple-element.39), channel_id=1, source_target_pairs={{0,32},{32,0},{1,33},{33,1},{2,34},{34,2},{3,35},{35,3},{4,36},{36... | collective-permute-start | bytes 442376 | tf_op jit(solution)/shard_map/ppermute | solution.py:25
  138.1 5.2 %collective-permute-start.11 = (bf16[24,3072]{1,0:T(8,128)(2,1)S(1)}, bf16[24,3072]{1,0:T(8,128)(2,1)S(1)}, u32[]{:S(2)}, u32[]{:S(2)}) collective-permute-start(bf16[24,3072]{1,0:T(8,128)(2,1)S(1)} %add_convert_fusion), channel_id=1, source_target_pairs={{0,80},{16,64},{64,16},{80,0},{1,81},{17,65},{65,17},{81,1},{2,82}... | collective-permute-start | bytes 442376 | tf_op jit(solution)/shard_map/ppermute | solution.py:29
  143.3 0.0 collective-permute-done.10
  143.3 12.7 %collective-permute-done.11 = bf16[24,3072]{1,0:T(8,128)(2,1)S(1)} collective-permute-done((bf16[24,3072]{1,0:T(8,128)(2,1)S(1)}, bf16[24,3072]{1,0:T(8,128)(2,1)S(1)}, u32[]{:S(2)}, u32[]{:S(2)}) %collective-permute-start.11) | collective-permute-done | bytes 147488 | tf_op jit(solution)/shard_map/ppermute | solution.py:29
  156.0 0.0 copy-done.3
  156.0 0.7 multiply_convert_fusion
  (3 shorter events, 0.1 us)
Async XLA Ops:
  0.0 27.6 %collective-permute-start = (bf16[24,3072]{1,0:T(8,128)(2,1)}, bf16[24,3072]{1,0:T(8,128)(2,1)S(1)}, u32[]{:S(2)}, u32[]{:S(2)}) collective-permute-start(bf16[24,3072]{1,0:T(8,128)(2,1)} %tokens_ref.1), channel_id=1, source_target_pairs={{0,80},{16,64},{64,16},{80,0},{1,81},{17,65},{65,17},{81,1},{2,82}... | collective-permute-start | bytes 442376 | tf_op jit(solution)/shard_map/ppermute | solution.py:29
  15.2 12.4 %copy-start.1 = (f32[4,1,3072]{2,1,0:T(1,128)S(1)}, f32[4,1,3072]{2,1,0:T(1,128)}, u32[]{:S(2)}) copy-start(f32[4,1,3072]{2,1,0:T(1,128)} %get-tuple-element.24.rows_ref) | copy-start | bytes 147460
  38.0 10.0 %collective-permute-start.1 = (bf16[192,3072]{1,0:T(8,128)(2,1)S(1)}, bf16[192,3072]{1,0:T(8,128)(2,1)S(1)}, u32[]{:S(2)}, u32[]{:S(2)}) collective-permute-start(bf16[192,3072]{1,0:T(8,128)(2,1)S(1)} %constant_dynamic-update-slice_fusion.refs_0_), channel_id=1, source_target_pairs={{0,32},{32,0},{1,33},{33,1},{2,34},{34,2},{3,35},{35,3},{4,36},{36... | collective-permute-start | bytes 3538952 | tf_op jit(solution)/shard_map/ppermute | solution.py:25
  51.8 12.9 %copy-start = (bf16[128,3072]{1,0:T(8,128)(2,1)S(1)}, bf16[128,3072]{1,0:T(8,128)(2,1)}, u32[]{:S(2)}) copy-start(bf16[128,3072]{1,0:T(8,128)(2,1)} %first_ref) | copy-start | bytes 2359300
  51.8 39.8 %all-to-all-start = ((bf16[8,384,128]{2,1,0:T(8,128)(2,1)}), bf16[8,384,128]{2,1,0:T(8,128)(2,1)S(1)}, u32[]{:S(2)}, u32[]{:S(2)}) async-start(bf16[8,384,128]{2,1,0:T(8,128)(2,1)} %get-tuple-element.27), calls=%async_computation | async-start | bytes 1572864 | tf_op jit(solution)/shard_map/all_to_all | solution.py:306
  56.4 19.3 %collective-permute-start.2 = (bf16[384,256]{1,0:T(8,128)(2,1)S(1)}, bf16[384,256]{1,0:T(8,128)(2,1)S(1)}, u32[]{:S(2)}, u32[]{:S(2)}) collective-permute-start(bf16[384,256]{1,0:T(8,128)(2,1)S(1)} %get-tuple-element.29), channel_id=1, source_target_pairs={{0,16},{16,0},{1,17},{17,1},{2,18},{18,2},{3,19},{19,3},{4,20},{20... | collective-permute-start | bytes 589832 | tf_op jit(solution)/shard_map/ppermute | solution.py:25
  61.5 27.6 %collective-permute-start.3 = (bf16[384,256]{1,0:T(8,128)(2,1)S(1)}, bf16[384,256]{1,0:T(8,128)(2,1)S(1)}, u32[]{:S(2)}, u32[]{:S(2)}) collective-permute-start(bf16[384,256]{1,0:T(8,128)(2,1)S(1)} %get-tuple-element.29), channel_id=1, source_target_pairs={{0,8},{8,0},{1,9},{9,1},{2,10},{10,2},{3,11},{11,3},{4,12},{12,4},... | collective-permute-start | bytes 589832 | tf_op jit(solution)/shard_map/ppermute | solution.py:25
  64.7 34.1 %collective-permute-start.5 = (bf16[128,3072]{1,0:T(8,128)(2,1)S(1)}, bf16[128,3072]{1,0:T(8,128)(2,1)S(1)}, u32[]{:S(2)}, u32[]{:S(2)}) collective-permute-start(bf16[128,3072]{1,0:T(8,128)(2,1)S(1)} %copy-done), channel_id=1, source_target_pairs={{0,128},{128,0},{256,384},{384,256},{1,129},{129,1},{257,385},{385... | collective-permute-start | bytes 2359304 | tf_op jit(solution)/shard_map/ppermute | solution.py:292
  68.1 30.7 %collective-permute-start.6 = (bf16[128,3072]{1,0:T(8,128)(2,1)S(1)}, bf16[128,3072]{1,0:T(8,128)(2,1)}, u32[]{:S(2)}, u32[]{:S(2)}) collective-permute-start(bf16[128,3072]{1,0:T(8,128)(2,1)S(1)} %copy-done), channel_id=1, source_target_pairs={{0,384},{128,256},{256,128},{384,0},{1,385},{129,257},{257,129},{3... | collective-permute-start | bytes 2359304 | tf_op jit(solution)/shard_map/ppermute | solution.py:292
  75.7 15.8 %collective-permute-start.4 = (bf16[384,256]{1,0:T(8,128)(2,1)S(1)}, bf16[384,256]{1,0:T(8,128)(2,1)S(1)}, u32[]{:S(2)}, u32[]{:S(2)}) collective-permute-start(bf16[384,256]{1,0:T(8,128)(2,1)S(1)} %collective-permute-done.2), channel_id=1, source_target_pairs={{0,8},{8,0},{1,9},{9,1},{2,10},{10,2},{3,11},{11,3},{4,12},{12,4},... | collective-permute-start | bytes 589832 | tf_op jit(solution)/shard_map/ppermute | solution.py:25
  86.0 12.8 %collective-permute-start.7 = (bf16[64,3072]{1,0:T(8,128)(2,1)}, bf16[64,3072]{1,0:T(8,128)(2,1)}, u32[]{:S(2)}, u32[]{:S(2)}) collective-permute-start(bf16[64,3072]{1,0:T(8,128)(2,1)} %get-tuple-element.42), channel_id=1, source_target_pairs={{0,256},{128,384},{256,0},{384,128},{1,257},{129,385},{257,1},{385... | collective-permute-start | bytes 1179656 | tf_op jit(solution)/shard_map/ppermute | solution.py:292
  97.9 8.1 %copy-start.2 = (bf16[64,3072]{1,0:T(8,128)(2,1)S(1)}, bf16[64,3072]{1,0:T(8,128)(2,1)}, u32[]{:S(2)}) copy-start(bf16[64,3072]{1,0:T(8,128)(2,1)} %get-tuple-element.41) | copy-start | bytes 1179652
  98.9 15.6 %all-to-all-start.1 = ((bf16[8,400,128]{2,1,0:T(8,128)(2,1)}), bf16[8,400,128]{2,1,0:T(8,128)(2,1)S(1)}, u32[]{:S(2)}, u32[]{:S(2)}) async-start(bf16[8,400,128]{2,1,0:T(8,128)(2,1)} %shard_map.85), calls=%async_computation.1 | async-start | bytes 1638400 | tf_op jit(solution)/shard_map/all_to_all | solution.py:311
  106.0 13.8 %collective-permute-start.8 = (bf16[64,3072]{1,0:T(8,128)(2,1)S(1)}, bf16[64,3072]{1,0:T(8,128)(2,1)S(1)}, u32[]{:S(2)}, u32[]{:S(2)}) collective-permute-start(bf16[64,3072]{1,0:T(8,128)(2,1)S(1)} %copy-done.2), channel_id=1, source_target_pairs={{0,256},{128,384},{256,0},{384,128},{1,257},{129,385},{257,1},{385... | collective-permute-start | bytes 1179656 | tf_op jit(solution)/shard_map/ppermute | solution.py:292
  115.3 9.1 %all-to-all-start.2 = ((bf16[4,96,128]{2,1,0:T(8,128)(2,1)}), bf16[4,96,128]{2,1,0:T(8,128)(2,1)S(1)}, u32[]{:S(2)}, u32[]{:S(2)}) async-start(bf16[4,96,128]{2,1,0:T(8,128)(2,1)} %shard_map.86), calls=%async_computation.2 | async-start | bytes 196608 | tf_op jit(solution)/shard_map/all_to_all | solution.py:312
  124.4 31.6 %copy-start.3 = (f32[3072]{0:T(1024)S(1)}, f32[3072]{0:T(1024)}, u32[]{:S(2)}) copy-start(f32[3072]{0:T(1024)} %param.15) | copy-start | bytes 36868
  126.4 9.5 %collective-permute-start.9 = (bf16[24,3072]{1,0:T(8,128)(2,1)S(1)}, bf16[24,3072]{1,0:T(8,128)(2,1)S(1)}, u32[]{:S(2)}, u32[]{:S(2)}) collective-permute-start(bf16[24,3072]{1,0:T(8,128)(2,1)S(1)} %get-tuple-element.38), channel_id=1, source_target_pairs={{0,32},{32,0},{1,33},{33,1},{2,34},{34,2},{3,35},{35,3},{4,36},{36... | collective-permute-start | bytes 442376 | tf_op jit(solution)/shard_map/ppermute | solution.py:25
  135.9 7.5 %collective-permute-start.10 = (bf16[24,3072]{1,0:T(8,128)(2,1)S(1)}, bf16[24,3072]{1,0:T(8,128)(2,1)S(1)}, u32[]{:S(2)}, u32[]{:S(2)}) collective-permute-start(bf16[24,3072]{1,0:T(8,128)(2,1)S(1)} %get-tuple-element.39), channel_id=1, source_target_pairs={{0,32},{32,0},{1,33},{33,1},{2,34},{34,2},{3,35},{35,3},{4,36},{36... | collective-permute-start | bytes 442376 | tf_op jit(solution)/shard_map/ppermute | solution.py:25
  138.1 17.9 %collective-permute-start.11 = (bf16[24,3072]{1,0:T(8,128)(2,1)S(1)}, bf16[24,3072]{1,0:T(8,128)(2,1)S(1)}, u32[]{:S(2)}, u32[]{:S(2)}) collective-permute-start(bf16[24,3072]{1,0:T(8,128)(2,1)S(1)} %add_convert_fusion), channel_id=1, source_target_pairs={{0,80},{16,64},{64,16},{80,0},{1,81},{17,65},{65,17},{81,1},{2,82}... | collective-permute-start | bytes 442376 | tf_op jit(solution)/shard_map/ppermute | solution.py:29

commit v8 on v7

--- a/solution.py
+++ b/solution.py
@@ -243,21 +243,19 @@
 
 
 def mix_kernel(y_ref, attended_ref, first_ref, *refs):
-    *weight_refs, near_ref, far_ref, near_out_ref, far_out_ref, first, first_sem = refs
+    *weight_refs, own_ref, other_ref, first, first_sem = refs
     copy = pltpu.make_async_copy(first_ref, first, first_sem.at[0])
     copy.start()
     attended = jnp.concatenate([attended_ref[y_ref[0] ^ i] for i in (0, 1, 3, 2)], axis=1)
-    part, width = near_ref.shape
+    half, width = own_ref.shape
     step = width // 4
     copy.wait()
     for at in range(0, width, step):
         weight = [ref[:, at : at + step] for ref in (first, *weight_refs)]
         weight = jnp.concatenate(weight, axis=0)
         mixed = jnp.dot(attended, weight, preferred_element_type=F32)
-        near_ref[:, at : at + step] = mixed[:part]
-        far_ref[:, at : at + step] = mixed[part : 2 * part]
-        near_out_ref[:, at : at + step] = mixed[2 * part : 3 * part].astype(BF16)
-        far_out_ref[:, at : at + step] = mixed[3 * part :].astype(BF16)
+        own_ref[:, at : at + step] = mixed[:half]
+        other_ref[:, at : at + step] = mixed[half:].astype(BF16)
 
 
 def mix(y, attended, weights):
@@ -273,7 +271,8 @@
         ]
         + [vmem] * (len(weights) - 1),
         out_shape=[
-            jax.ShapeDtypeStruct((rows // 4, width), kind) for kind in (F32, F32, BF16, BF16)
+            jax.ShapeDtypeStruct((rows // 2, width), F32),
+            jax.ShapeDtypeStruct((rows // 2, width), BF16),
         ],
         scratch_shapes=[pltpu.VMEM((depth, width), BF16), pltpu.SemaphoreType.DMA((1,))],
         compiler_params=params(16),
@@ -286,7 +285,7 @@
 
 
 def local(tokens, mod_shift, mod_scale, qkv_weight, q_gain, k_gain, out_weight, out_gate):
-    width = tokens.shape[1]
+    rows, width = tokens.shape
 
     def along_y(block, distance):
         return lax.ppermute(block, "y", [(i, i ^ distance) for i in range(4)])
@@ -311,11 +310,10 @@
     partial = lax.all_to_all(partial, NEAR, 0, 0)
     attended = lax.all_to_all(divide(partial, 4), "y", 0, 0)
     y = lax.axis_index("y").astype(jnp.int32).reshape(1)
-    near, far, near_out, far_out = mix(y, attended, [out_weight, *weights])
-    far = (far + swap(far_out, "core").astype(F32)).astype(BF16)
-    near_out, far = lax.optimization_barrier((near_out, far))
-    arrived = trade_halves(far).astype(F32)
-    return ((near + swap(near_out, "core").astype(F32) + arrived) * out_gate).astype(BF16)
+    own, other = mix(y, attended, [out_weight, *weights])
+    summed = own + swap(other, "core").astype(F32)
+    arrived = trade_halves(summed[rows:].astype(BF16)).astype(F32)
+    return ((summed[:rows] + arrived) * out_gate).astype(BF16)
 
 
 def solution(mesh):

time: 158 us -> 156 us (0.987)
  starting transfers between devices: 83.3 us -> 81.1 us
    ppermute x6 -> x5, starting transfers between devices: 36 us -> 33.7 us  [swap(): return lax.ppermute(block, axis, [(0, 1), (1, 0)])]
    ppermute x6 -> x5, waiting for transfers between devices: 10.3 us -> 10.5 us  [swap(): return lax.ppermute(block, axis, [(0, 1), (1, 0)])]
  transfers between devices with their start and end apart: 15 -> 14, of which waited for: 8 -> 8; matrix products, arithmetic and copies ran while one was open for 1% -> 1% of each run, Pallas kernels for 6% -> 6%
where the time goes in v8:
time: 156 us; the launch traced here: 155 us
  starting transfers between devices  81.1 us (52%)
  waiting for transfers between devices  34.1 us (22%)
  blocking collectives  22.4 us (14%)
  Pallas kernels  15 us (10%)
    ppermute x5, starting transfers between devices, swap(): return lax.ppermute(block, axis, [(0, 1), (1, 0)])  33.7 us
    all_gather x2, blocking collectives, spread(): return lax.all_gather(modulated, 'y', axis=0, tiled=True)  22.4 us
    ppermute x2, starting transfers between devices, trade_halves(): return lax.ppermute(block, ('zh', 'za'), [(i, i ^ 3) for i in range(4)])  18.4 us
    ppermute x4, starting transfers between devices, along_y(): return lax.ppermute(block, 'y', [(i, i ^ distance) for i in range(4)])  12.7 us
    ppermute x2, waiting for transfers between devices, trade_halves(): return lax.ppermute(block, ('zh', 'za'), [(i, i ^ 3) for i in range(4)])  12.6 us
    ppermute x5, waiting for transfers between devices, swap(): return lax.ppermute(block, axis, [(0, 1), (1, 0)])  10.5 us
    all_to_all x1, starting transfers between devices, local(): partial = lax.all_to_all(partial, NEAR, 0, 0)  7.16 us
    pallas_call x1, Pallas kernels, attend(): pl.pallas_call(attend_kernel, grid=(blocks // 2,), in_specs=[pl.BlockSpec...  6.28 us
  transfers between devices with their start and end apart: 14, of which 8 were waited for; matrix products, arithmetic and copies ran while one was open for 1% of the time, Pallas kernels for 6%

profile of v8, /device:TPU:1, one launch (start us, length us, event | category | flops | bytes accessed | tf_op | source)
XLA Modules:
  0.0 154.7 jit_solution(8114319399356177228)
XLA Ops:
  0.0 13.3 %collective-permute-start = (bf16[24,3072]{1,0:T(8,128)(2,1)}, bf16[24,3072]{1,0:T(8,128)(2,1)S(1)}, u32[]{:S(2)}, u32[]{:S(2)}) collective-permute-start(bf16[24,3072]{1,0:T(8,128)(2,1)} %tokens_ref.1), channel_id=1, source_target_pairs={{0,80},{16,64},{64,16},{80,0},{1,81},{17,65},{65,17},{81,1},{2,82}... | collective-permute-start | bytes 442376 | tf_op jit(solution)/shard_map/ppermute | solution.py:29
  13.3 1.9 %shard_map.82 = (bf16[24,3072]{1,0:T(8,128)(2,1)}, f32[4,1,3072]{2,1,0:T(1,128)}) custom-call(bf16[24,3072]{1,0:T(8,128)(2,1)} %tokens_ref.1, f32[1,3072]{1,0:T(1,128)} %bitcast.5, f32[1,3072]{1,0:T(1,128)} %bitcast.6, f32[1,128]{1,0:T(1,128)} %bitcast.7, f32[1,128]{1,0:T(1,128)} %bitcast.8), custom_call_target="tpu_custom_call" | custom-call | tf_op jit(solution)/shard_map/pallas_call | solution.py:56
  15.2 0.0 copy-start.1
  15.2 12.3 %all_gather.6 = bf16[96,3072]{1,0:T(8,128)(2,1)S(1)} all-gather(bf16[24,3072]{1,0:T(8,128)(2,1)} %get-tuple-element.19), channel_id=1, replica_groups=mesh['y'=4,'zh'=2,'core'=2,'za'=2,'zb'=2,'zc'=2,'x'=4] {'y'}, dimensions={0}, use_global_device_ids=true | all-gather | bytes 737280 | tf_op jit(solution)/shard_map/all_gather | solution.py:294
  27.6 0.0 collective-permute-done.tokens_ref
  27.6 0.0 copy-done.1
  27.6 0.3 shard_map.83
  27.9 10.0 %all_gather.7 = bf16[96,3072]{1,0:T(8,128)(2,1)S(1)} all-gather(bf16[24,3072]{1,0:T(8,128)(2,1)S(1)} %get-tuple-element.21), channel_id=1, replica_groups=mesh['y'=4,'zh'=2,'core'=2,'za'=2,'zb'=2,'zc'=2,'x'=4] {'y'}, dimensions={0}, use_global_device_ids=true | all-gather | bytes 737280 | tf_op jit(solution)/shard_map/all_gather | solution.py:294
  38.0 7.6 %collective-permute-start.1 = (bf16[192,3072]{1,0:T(8,128)(2,1)S(1)}, bf16[192,3072]{1,0:T(8,128)(2,1)S(1)}, u32[]{:S(2)}, u32[]{:S(2)}) collective-permute-start(bf16[192,3072]{1,0:T(8,128)(2,1)S(1)} %constant_dynamic-update-slice_fusion.refs_0_), channel_id=1, source_target_pairs={{0,32},{32,0},{1,33},{33,1},{2,34},{34,2},{3,35},{35,3},{4,36},{36... | collective-permute-start | bytes 3538952 | tf_op jit(solution)/shard_map/ppermute | solution.py:25
  45.5 2.5 %collective-permute-done.1.refs_1_ = bf16[192,3072]{1,0:T(8,128)(2,1)S(1)} collective-permute-done((bf16[192,3072]{1,0:T(8,128)(2,1)S(1)}, bf16[192,3072]{1,0:T(8,128)(2,1)S(1)}, u32[]{:S(2)}, u32[]{:S(2)}) %collective-permute-start.1) | collective-permute-done | bytes 1179680 | tf_op jit(solution)/shard_map/ppermute | solution.py:25
  48.0 3.8 %shard_map.84 = (bf16[8,384,128]{2,1,0:T(8,128)(2,1)}, bf16[384,256]{1,0:T(8,128)(2,1)S(1)}) custom-call(bf16[192,3072]{1,0:T(8,128)(2,1)S(1)} %constant_dynamic-update-slice_fusion.refs_0_, bf16[192,3072]{1,0:T(8,128)(2,1)S(1)} %collective-permute-done.1.refs_1_, f32[2,1,128]{2,1,0:T(1,128)S(1)} %get-tuple-element.22.refs_2_, bf16[3,3072,128]{2,1,0:T(8,128)(2,1)} %refs_3_.1), custom_call_target="tpu_custom_call" | custom-call | flops 905969664 | bytes 2359296 | tf_op jit(solution)/shard_map/pallas_call | solution.py:126
  51.8 0.0 copy-start
  51.8 4.6 %all-to-all-start = ((bf16[8,384,128]{2,1,0:T(8,128)(2,1)}), bf16[8,384,128]{2,1,0:T(8,128)(2,1)S(1)}, u32[]{:S(2)}, u32[]{:S(2)}) async-start(bf16[8,384,128]{2,1,0:T(8,128)(2,1)} %get-tuple-element.23), calls=%async_computation | async-start | bytes 1572864 | tf_op jit(solution)/shard_map/all_to_all | solution.py:305
  56.4 5.1 %collective-permute-start.2 = (bf16[384,256]{1,0:T(8,128)(2,1)S(1)}, bf16[384,256]{1,0:T(8,128)(2,1)S(1)}, u32[]{:S(2)}, u32[]{:S(2)}) collective-permute-start(bf16[384,256]{1,0:T(8,128)(2,1)S(1)} %get-tuple-element.25), channel_id=1, source_target_pairs={{0,16},{16,0},{1,17},{17,1},{2,18},{18,2},{3,19},{19,3},{4,20},{20... | collective-permute-start | bytes 589832 | tf_op jit(solution)/shard_map/ppermute | solution.py:25
  61.5 3.2 %collective-permute-start.3 = (bf16[384,256]{1,0:T(8,128)(2,1)S(1)}, bf16[384,256]{1,0:T(8,128)(2,1)S(1)}, u32[]{:S(2)}, u32[]{:S(2)}) collective-permute-start(bf16[384,256]{1,0:T(8,128)(2,1)S(1)} %get-tuple-element.25), channel_id=1, source_target_pairs={{0,8},{8,0},{1,9},{9,1},{2,10},{10,2},{3,11},{11,3},{4,12},{12,4},... | collective-permute-start | bytes 589832 | tf_op jit(solution)/shard_map/ppermute | solution.py:25
  64.7 0.0 copy-done
  64.7 3.4 %collective-permute-start.5 = (bf16[128,3072]{1,0:T(8,128)(2,1)S(1)}, bf16[128,3072]{1,0:T(8,128)(2,1)S(1)}, u32[]{:S(2)}, u32[]{:S(2)}) collective-permute-start(bf16[128,3072]{1,0:T(8,128)(2,1)S(1)} %copy-done), channel_id=1, source_target_pairs={{0,128},{128,0},{256,384},{384,256},{1,129},{129,1},{257,385},{385... | collective-permute-start | bytes 2359304 | tf_op jit(solution)/shard_map/ppermute | solution.py:291
  68.1 3.1 %collective-permute-start.6 = (bf16[128,3072]{1,0:T(8,128)(2,1)S(1)}, bf16[128,3072]{1,0:T(8,128)(2,1)}, u32[]{:S(2)}, u32[]{:S(2)}) collective-permute-start(bf16[128,3072]{1,0:T(8,128)(2,1)S(1)} %copy-done), channel_id=1, source_target_pairs={{0,384},{128,256},{256,128},{384,0},{1,385},{129,257},{257,129},{3... | collective-permute-start | bytes 2359304 | tf_op jit(solution)/shard_map/ppermute | solution.py:291
  71.3 4.4 %collective-permute-done.2 = bf16[384,256]{1,0:T(8,128)(2,1)S(1)} collective-permute-done((bf16[384,256]{1,0:T(8,128)(2,1)S(1)}, bf16[384,256]{1,0:T(8,128)(2,1)S(1)}, u32[]{:S(2)}, u32[]{:S(2)}) %collective-permute-start.2) | collective-permute-done | bytes 196640 | tf_op jit(solution)/shard_map/ppermute | solution.py:25
  75.7 9.4 %collective-permute-start.4 = (bf16[384,256]{1,0:T(8,128)(2,1)S(1)}, bf16[384,256]{1,0:T(8,128)(2,1)S(1)}, u32[]{:S(2)}, u32[]{:S(2)}) collective-permute-start(bf16[384,256]{1,0:T(8,128)(2,1)S(1)} %collective-permute-done.2), channel_id=1, source_target_pairs={{0,8},{8,0},{1,9},{9,1},{2,10},{10,2},{3,11},{11,3},{4,12},{12,4},... | collective-permute-start | bytes 589832 | tf_op jit(solution)/shard_map/ppermute | solution.py:25
  85.1 0.9 fusion.2
  86.0 3.1 %collective-permute-start.7 = (bf16[64,3072]{1,0:T(8,128)(2,1)}, bf16[64,3072]{1,0:T(8,128)(2,1)}, u32[]{:S(2)}, u32[]{:S(2)}) collective-permute-start(bf16[64,3072]{1,0:T(8,128)(2,1)} %get-tuple-element.34), channel_id=1, source_target_pairs={{0,256},{128,384},{256,0},{384,128},{1,257},{129,385},{257,1},{385... | collective-permute-start | bytes 1179656 | tf_op jit(solution)/shard_map/ppermute | solution.py:291
  89.1 0.0 collective-permute-done.3
  89.1 2.4 %collective-permute-done.4 = bf16[384,256]{1,0:T(8,128)(2,1)S(1)} collective-permute-done((bf16[384,256]{1,0:T(8,128)(2,1)S(1)}, bf16[384,256]{1,0:T(8,128)(2,1)S(1)}, u32[]{:S(2)}, u32[]{:S(2)}) %collective-permute-start.4) | collective-permute-done | bytes 196640 | tf_op jit(solution)/shard_map/ppermute | solution.py:25
  91.6 0.1 pad_maximum_fusion.kv_ref
  91.6 0.0 all-to-all-done.q_ref
  91.6 6.3 %shard_map.85 = bf16[8,400,128]{2,1,0:T(8,128)(2,1)} custom-call(bf16[8,384,128]{2,1,0:T(8,128)(2,1)S(1)} %all-to-all-done.q_ref, bf16[1536,256]{1,0:T(8,128)(2,1)S(1)} %pad_maximum_fusion.kv_ref), custom_call_target="tpu_custom_call" | custom-call | flops 2415919104 | bytes 786432 | tf_op jit(solution)/shard_map/pallas_call | solution.py:200
  97.9 0.0 copy-start.2
  97.9 0.9 collective-permute-done.7.refs_2_
  98.8 0.0 collective-permute-done.5.refs_0_
  98.8 0.0 collective-permute-done.6.refs_1_
  98.8 7.2 %all-to-all-start.1 = ((bf16[8,400,128]{2,1,0:T(8,128)(2,1)}), bf16[8,400,128]{2,1,0:T(8,128)(2,1)S(1)}, u32[]{:S(2)}, u32[]{:S(2)}) async-start(bf16[8,400,128]{2,1,0:T(8,128)(2,1)} %shard_map.85), calls=%async_computation.1 | async-start | bytes 1638400 | tf_op jit(solution)/shard_map/all_to_all | solution.py:310
  106.0 0.0 copy-done.2
  106.0 3.1 %collective-permute-start.8 = (bf16[64,3072]{1,0:T(8,128)(2,1)S(1)}, bf16[64,3072]{1,0:T(8,128)(2,1)S(1)}, u32[]{:S(2)}, u32[]{:S(2)}) collective-permute-start(bf16[64,3072]{1,0:T(8,128)(2,1)S(1)} %copy-done.2), channel_id=1, source_target_pairs={{0,256},{128,384},{256,0},{384,128},{1,257},{129,385},{257,1},{385... | collective-permute-start | bytes 1179656 | tf_op jit(solution)/shard_map/ppermute | solution.py:291
  109.1 5.4 %all-to-all-done.1.partial_ref = bf16[8,400,128]{2,1,0:T(8,128)(2,1)S(1)} async-done(((bf16[8,400,128]{2,1,0:T(8,128)(2,1)}), bf16[8,400,128]{2,1,0:T(8,128)(2,1)S(1)}, u32[]{:S(2)}, u32[]{:S(2)}) %all-to-all-start.1) | async-done | bytes 819232 | tf_op jit(solution)/shard_map/all_to_all | solution.py:310
  114.5 0.8 shard_map.86
  115.3 4.5 %all-to-all-start.2 = ((bf16[4,96,128]{2,1,0:T(8,128)(2,1)}), bf16[4,96,128]{2,1,0:T(8,128)(2,1)S(1)}, u32[]{:S(2)}, u32[]{:S(2)}) async-start(bf16[4,96,128]{2,1,0:T(8,128)(2,1)} %shard_map.86), calls=%async_computation.2 | async-start | bytes 196608 | tf_op jit(solution)/shard_map/all_to_all | solution.py:311
  119.8 0.0 collective-permute-done.8.refs_3_
  119.8 4.6 %all-to-all-done.2.attended_ref = bf16[4,96,128]{2,1,0:T(8,128)(2,1)S(1)} async-done(((bf16[4,96,128]{2,1,0:T(8,128)(2,1)}), bf16[4,96,128]{2,1,0:T(8,128)(2,1)S(1)}, u32[]{:S(2)}, u32[]{:S(2)}) %all-to-all-start.2) | async-done | bytes 98336 | tf_op jit(solution)/shard_map/all_to_all | solution.py:311
  124.4 1.9 %shard_map.87 = (f32[48,3072]{1,0:T(8,128)S(1)}, bf16[48,3072]{1,0:T(8,128)(2,1)S(1)}) custom-call(s32[1]{0:T(128)} %bitcast.y_ref, bf16[4,96,128]{2,1,0:T(8,128)(2,1)S(1)} %all-to-all-done.2.attended_ref, bf16[128,3072]{1,0:T(8,128)(2,1)S(1)} %copy-done, bf16[128,3072]{1,0:T(8,128)(2,1)S(1)} %collective-permute-done.5.refs_0_, ...), custom_call_target="tpu_custom_call" | custom-call | flops 301989888 | bytes 3145728 | tf_op jit(solution)/shard_map/pallas_call | solution.py:265
  126.4 0.0 copy-start.3
  126.4 8.5 %collective-permute-start.9 = (bf16[48,3072]{1,0:T(8,128)(2,1)S(1)}, bf16[48,3072]{1,0:T(8,128)(2,1)S(1)}, u32[]{:S(2)}, u32[]{:S(2)}) collective-permute-start(bf16[48,3072]{1,0:T(8,128)(2,1)S(1)} %get-tuple-element.32), channel_id=1, source_target_pairs={{0,32},{32,0},{1,33},{33,1},{2,34},{34,2},{3,35},{35,3},{4,36},{36... | collective-permute-start | bytes 884744 | tf_op jit(solution)/shard_map/ppermute | solution.py:25
  134.8 1.2 collective-permute-done.9
  136.0 0.1 convert_add_fusion
  136.1 5.2 %collective-permute-start.10 = (bf16[24,3072]{1,0:T(8,128)(2,1)S(1)}, bf16[24,3072]{1,0:T(8,128)(2,1)S(1)}, u32[]{:S(2)}, u32[]{:S(2)}) collective-permute-start(bf16[24,3072]{1,0:T(8,128)(2,1)S(1)} %slice.25), channel_id=1, source_target_pairs={{0,80},{16,64},{64,16},{80,0},{1,81},{17,65},{65,17},{81,1},{2,82}... | collective-permute-start | bytes 442376 | tf_op jit(solution)/shard_map/ppermute | solution.py:29
  141.3 12.6 %collective-permute-done.10 = bf16[24,3072]{1,0:T(8,128)(2,1)S(1)} collective-permute-done((bf16[24,3072]{1,0:T(8,128)(2,1)S(1)}, bf16[24,3072]{1,0:T(8,128)(2,1)S(1)}, u32[]{:S(2)}, u32[]{:S(2)}) %collective-permute-start.10) | collective-permute-done | bytes 147488 | tf_op jit(solution)/shard_map/ppermute | solution.py:29
  153.9 0.0 copy-done.3
  153.9 0.7 fusion.1
  (3 shorter events, 0.1 us)
Async XLA Ops:
  0.0 27.6 %collective-permute-start = (bf16[24,3072]{1,0:T(8,128)(2,1)}, bf16[24,3072]{1,0:T(8,128)(2,1)S(1)}, u32[]{:S(2)}, u32[]{:S(2)}) collective-permute-start(bf16[24,3072]{1,0:T(8,128)(2,1)} %tokens_ref.1), channel_id=1, source_target_pairs={{0,80},{16,64},{64,16},{80,0},{1,81},{17,65},{65,17},{81,1},{2,82}... | collective-permute-start | bytes 442376 | tf_op jit(solution)/shard_map/ppermute | solution.py:29
  15.2 12.4 %copy-start.1 = (f32[4,1,3072]{2,1,0:T(1,128)S(1)}, f32[4,1,3072]{2,1,0:T(1,128)}, u32[]{:S(2)}) copy-start(f32[4,1,3072]{2,1,0:T(1,128)} %get-tuple-element.20.rows_ref) | copy-start | bytes 147460
  38.0 10.0 %collective-permute-start.1 = (bf16[192,3072]{1,0:T(8,128)(2,1)S(1)}, bf16[192,3072]{1,0:T(8,128)(2,1)S(1)}, u32[]{:S(2)}, u32[]{:S(2)}) collective-permute-start(bf16[192,3072]{1,0:T(8,128)(2,1)S(1)} %constant_dynamic-update-slice_fusion.refs_0_), channel_id=1, source_target_pairs={{0,32},{32,0},{1,33},{33,1},{2,34},{34,2},{3,35},{35,3},{4,36},{36... | collective-permute-start | bytes 3538952 | tf_op jit(solution)/shard_map/ppermute | solution.py:25
  51.8 12.9 %copy-start = (bf16[128,3072]{1,0:T(8,128)(2,1)S(1)}, bf16[128,3072]{1,0:T(8,128)(2,1)}, u32[]{:S(2)}) copy-start(bf16[128,3072]{1,0:T(8,128)(2,1)} %first_ref) | copy-start | bytes 2359300
  51.8 39.8 %all-to-all-start = ((bf16[8,384,128]{2,1,0:T(8,128)(2,1)}), bf16[8,384,128]{2,1,0:T(8,128)(2,1)S(1)}, u32[]{:S(2)}, u32[]{:S(2)}) async-start(bf16[8,384,128]{2,1,0:T(8,128)(2,1)} %get-tuple-element.23), calls=%async_computation | async-start | bytes 1572864 | tf_op jit(solution)/shard_map/all_to_all | solution.py:305
  56.4 19.3 %collective-permute-start.2 = (bf16[384,256]{1,0:T(8,128)(2,1)S(1)}, bf16[384,256]{1,0:T(8,128)(2,1)S(1)}, u32[]{:S(2)}, u32[]{:S(2)}) collective-permute-start(bf16[384,256]{1,0:T(8,128)(2,1)S(1)} %get-tuple-element.25), channel_id=1, source_target_pairs={{0,16},{16,0},{1,17},{17,1},{2,18},{18,2},{3,19},{19,3},{4,20},{20... | collective-permute-start | bytes 589832 | tf_op jit(solution)/shard_map/ppermute | solution.py:25
  61.5 27.6 %collective-permute-start.3 = (bf16[384,256]{1,0:T(8,128)(2,1)S(1)}, bf16[384,256]{1,0:T(8,128)(2,1)S(1)}, u32[]{:S(2)}, u32[]{:S(2)}) collective-permute-start(bf16[384,256]{1,0:T(8,128)(2,1)S(1)} %get-tuple-element.25), channel_id=1, source_target_pairs={{0,8},{8,0},{1,9},{9,1},{2,10},{10,2},{3,11},{11,3},{4,12},{12,4},... | collective-permute-start | bytes 589832 | tf_op jit(solution)/shard_map/ppermute | solution.py:25
  64.7 34.1 %collective-permute-start.5 = (bf16[128,3072]{1,0:T(8,128)(2,1)S(1)}, bf16[128,3072]{1,0:T(8,128)(2,1)S(1)}, u32[]{:S(2)}, u32[]{:S(2)}) collective-permute-start(bf16[128,3072]{1,0:T(8,128)(2,1)S(1)} %copy-done), channel_id=1, source_target_pairs={{0,128},{128,0},{256,384},{384,256},{1,129},{129,1},{257,385},{385... | collective-permute-start | bytes 2359304 | tf_op jit(solution)/shard_map/ppermute | solution.py:291
  68.1 30.7 %collective-permute-start.6 = (bf16[128,3072]{1,0:T(8,128)(2,1)S(1)}, bf16[128,3072]{1,0:T(8,128)(2,1)}, u32[]{:S(2)}, u32[]{:S(2)}) collective-permute-start(bf16[128,3072]{1,0:T(8,128)(2,1)S(1)} %copy-done), channel_id=1, source_target_pairs={{0,384},{128,256},{256,128},{384,0},{1,385},{129,257},{257,129},{3... | collective-permute-start | bytes 2359304 | tf_op jit(solution)/shard_map/ppermute | solution.py:291
  75.7 15.8 %collective-permute-start.4 = (bf16[384,256]{1,0:T(8,128)(2,1)S(1)}, bf16[384,256]{1,0:T(8,128)(2,1)S(1)}, u32[]{:S(2)}, u32[]{:S(2)}) collective-permute-start(bf16[384,256]{1,0:T(8,128)(2,1)S(1)} %collective-permute-done.2), channel_id=1, source_target_pairs={{0,8},{8,0},{1,9},{9,1},{2,10},{10,2},{3,11},{11,3},{4,12},{12,4},... | collective-permute-start | bytes 589832 | tf_op jit(solution)/shard_map/ppermute | solution.py:25
  86.0 12.8 %collective-permute-start.7 = (bf16[64,3072]{1,0:T(8,128)(2,1)}, bf16[64,3072]{1,0:T(8,128)(2,1)}, u32[]{:S(2)}, u32[]{:S(2)}) collective-permute-start(bf16[64,3072]{1,0:T(8,128)(2,1)} %get-tuple-element.34), channel_id=1, source_target_pairs={{0,256},{128,384},{256,0},{384,128},{1,257},{129,385},{257,1},{385... | collective-permute-start | bytes 1179656 | tf_op jit(solution)/shard_map/ppermute | solution.py:291
  97.9 8.1 %copy-start.2 = (bf16[64,3072]{1,0:T(8,128)(2,1)S(1)}, bf16[64,3072]{1,0:T(8,128)(2,1)}, u32[]{:S(2)}) copy-start(bf16[64,3072]{1,0:T(8,128)(2,1)} %get-tuple-element.33) | copy-start | bytes 1179652
  98.8 15.6 %all-to-all-start.1 = ((bf16[8,400,128]{2,1,0:T(8,128)(2,1)}), bf16[8,400,128]{2,1,0:T(8,128)(2,1)S(1)}, u32[]{:S(2)}, u32[]{:S(2)}) async-start(bf16[8,400,128]{2,1,0:T(8,128)(2,1)} %shard_map.85), calls=%async_computation.1 | async-start | bytes 1638400 | tf_op jit(solution)/shard_map/all_to_all | solution.py:310
  106.0 13.8 %collective-permute-start.8 = (bf16[64,3072]{1,0:T(8,128)(2,1)S(1)}, bf16[64,3072]{1,0:T(8,128)(2,1)S(1)}, u32[]{:S(2)}, u32[]{:S(2)}) collective-permute-start(bf16[64,3072]{1,0:T(8,128)(2,1)S(1)} %copy-done.2), channel_id=1, source_target_pairs={{0,256},{128,384},{256,0},{384,128},{1,257},{129,385},{257,1},{385... | collective-permute-start | bytes 1179656 | tf_op jit(solution)/shard_map/ppermute | solution.py:291
  115.3 9.1 %all-to-all-start.2 = ((bf16[4,96,128]{2,1,0:T(8,128)(2,1)}), bf16[4,96,128]{2,1,0:T(8,128)(2,1)S(1)}, u32[]{:S(2)}, u32[]{:S(2)}) async-start(bf16[4,96,128]{2,1,0:T(8,128)(2,1)} %shard_map.86), calls=%async_computation.2 | async-start | bytes 196608 | tf_op jit(solution)/shard_map/all_to_all | solution.py:311
  126.4 27.6 %copy-start.3 = (f32[3072]{0:T(1024)S(1)}, f32[3072]{0:T(1024)}, u32[]{:S(2)}) copy-start(f32[3072]{0:T(1024)} %param.15) | copy-start | bytes 36868
  126.4 9.6 %collective-permute-start.9 = (bf16[48,3072]{1,0:T(8,128)(2,1)S(1)}, bf16[48,3072]{1,0:T(8,128)(2,1)S(1)}, u32[]{:S(2)}, u32[]{:S(2)}) collective-permute-start(bf16[48,3072]{1,0:T(8,128)(2,1)S(1)} %get-tuple-element.32), channel_id=1, source_target_pairs={{0,32},{32,0},{1,33},{33,1},{2,34},{34,2},{3,35},{35,3},{4,36},{36... | collective-permute-start | bytes 884744 | tf_op jit(solution)/shard_map/ppermute | solution.py:25
  136.1 17.8 %collective-permute-start.10 = (bf16[24,3072]{1,0:T(8,128)(2,1)S(1)}, bf16[24,3072]{1,0:T(8,128)(2,1)S(1)}, u32[]{:S(2)}, u32[]{:S(2)}) collective-permute-start(bf16[24,3072]{1,0:T(8,128)(2,1)S(1)} %slice.25), channel_id=1, source_target_pairs={{0,80},{16,64},{64,16},{80,0},{1,81},{17,65},{65,17},{81,1},{2,82}... | collective-permute-start | bytes 442376 | tf_op jit(solution)/shard_map/ppermute | solution.py:29
